TPU v7x, 32 devices: a whole 2x2x4 slice. The times are simulated.
32 devices in a mesh: dp: 8 (over z, y), tensor: 4 (over x, core).
Axes of the slice: x: 2, y: 2, z: 4, core: 2. Of those that a mesh axis runs over, the one named last changes fastest.
Arguments:
- tokens: bfloat16 [8, 2048, 768], P('dp', 'tensor'), may hold values from -6 to 6
- picture_ids: int32 [8, 2048], P('dp'), may hold values from -1 to 19, as said below
- ln1_gain: float32 [768], replicated, may hold values from 0.1 to 1.9
- ln1_bias: float32 [768], replicated, may hold values from -3 to 3
- w_qkv: bfloat16 [768, 3, 768], P('dp', None, 'tensor'), may hold values from -0.21875 to 0.21875
- q_gain: float32 [64], replicated, may hold values from 0.1 to 1.9
- k_gain: float32 [64], replicated, may hold values from 0.1 to 1.9
- w_out: bfloat16 [768, 768], P('tensor', 'dp'), may hold values from -1.75 to 1.75
- ln2_gain: float32 [768], replicated, may hold values from 0.1 to 1.9
- ln2_bias: float32 [768], replicated, may hold values from -3 to 3
- w_up: bfloat16 [768, 3072], P('dp', 'tensor'), may hold values from -0.21875 to 0.21875
- w_down: bfloat16 [3072, 768], P('tensor', 'dp'), may hold values from -0.109375 to 0.109375
- cotangent: bfloat16 [8, 2048, 768], P('dp', 'tensor'), may hold values from -6 to 6
Outputs:
- result: bfloat16 [8, 2048, 768], P('dp', 'tensor')
- grad_tokens: bfloat16 [8, 2048, 768], P('dp', 'tensor')
- grad_ln1_gain: float32 [768], replicated
- grad_ln1_bias: float32 [768], replicated
- grad_w_qkv: float32 [768, 3, 768], P('dp', None, 'tensor')
- grad_q_gain: float32 [64], replicated
- grad_k_gain: float32 [64], replicated
- grad_w_out: float32 [768, 768], P('tensor', 'dp')
- grad_ln2_gain: float32 [768], replicated
- grad_ln2_bias: float32 [768], replicated
- grad_w_up: float32 [768, 3072], P('dp', 'tensor')
- grad_w_down: float32 [3072, 768], P('tensor', 'dp')
Inputs may be any that keep to these rules, and one draw needn't show every extreme that they name: `picture_ids`: each row holds whole pictures of 100 to 1024 consecutive slots numbered 0, 1, 2, ... from the row's start, then padding slots marked -1; some picture of every draw has exactly 1024 slots, and some row of every draw holds only pictures of 100 slots, as many as fit.
All inputs are finite; a program needn't handle non-finite values.
Results may differ from a plain program's by a relative error of at most 0.018.
Values may be sent and summed in bfloat16 or wider, within the bound.
No kernel may reach another device: no remote copies, remote signals or barrier semaphores. Data moves between devices by JAX's collectives and lax.ppermute only.
A program may use at most 128 MiB of HBM per device.

v0:
```python
import jax
import jax.numpy as jnp
from jax import lax
from jax.sharding import PartitionSpec as P

HD = 64


EPSILON = 1e-06


def layer_norm(values, gain_vec, bias_vec):
    center = values - jnp.mean(values, axis=-1, keepdims=True)
    spread = jnp.mean(center * center, axis=-1, keepdims=True)
    return center * lax.rsqrt(spread + EPSILON) * gain_vec + bias_vec


def head_norm(values, gain_vec):
    center = values - jnp.mean(values, axis=-1, keepdims=True)
    spread = jnp.mean(center * center, axis=-1, keepdims=True)
    return center * lax.rsqrt(spread + EPSILON) * gain_vec


def both_heads(query_raw, key_raw, q_gain, k_gain):
    return (head_norm(query_raw, q_gain), head_norm(key_raw, k_gain))


def gelu_exact(values):
    return jax.nn.gelu(values, approximate=False)


def split_blocks(values, block_rows):
    heads_here, slot_count = (values.shape[0], values.shape[1])
    shaped = values.reshape((heads_here, slot_count // block_rows, block_rows) + values.shape[2:])
    return jnp.moveaxis(shaped, 1, 0)


def join_blocks(values):
    joined = jnp.moveaxis(values, 0, 1)
    return joined.reshape((joined.shape[0], joined.shape[1] * joined.shape[2]) + joined.shape[3:])


def masked_scores(query_block, key_row, id_block, ids_row):
    score_scale = query_block.shape[-1] ** (-0.5)
    scores = (
        jnp.einsum("hqe,hke->hqk", query_block, key_row, preferred_element_type=jnp.float32)
        * score_scale
    )
    allowed = id_block[:, None] == ids_row[None, :]
    return jnp.where(allowed[None], scores, -1e30)


def attend_forward(query_row, key_row, value_row, ids_row):
    slot_count = query_row.shape[1]
    block_rows = min(512, slot_count)
    id_blocks = ids_row.reshape(slot_count // block_rows, block_rows)

    def one_block(block_pair):
        query_block, id_block = block_pair
        scores = masked_scores(query_block, key_row, id_block, ids_row)
        top_score = jnp.max(scores, axis=-1, keepdims=True)
        exponent = jnp.exp(scores - top_score)
        totals = jnp.sum(exponent, axis=-1, keepdims=True)
        soft_weights = (exponent / totals).astype(jnp.bfloat16)
        attended = jnp.einsum(
            "hqk,hke->hqe", soft_weights, value_row, preferred_element_type=jnp.float32
        )
        return (attended, (top_score + jnp.log(totals))[..., 0])

    attended, log_total = lax.map(one_block, (split_blocks(query_row, block_rows), id_blocks))
    return (join_blocks(attended), join_blocks(log_total))


def attend_backward(query_row, key_row, value_row, ids_row, log_total, grad_row):
    slot_count = query_row.shape[1]
    block_rows = min(512, slot_count)
    score_scale = query_row.shape[-1] ** (-0.5)
    id_blocks = ids_row.reshape(slot_count // block_rows, block_rows)

    def one_block(carry, block_items):
        key_grad, value_grad = carry
        query_block, grad_block, id_block, lse_block = block_items
        scores = masked_scores(query_block, key_row, id_block, ids_row)
        soft_weights = jnp.exp(scores - lse_block[..., None])
        grad_weights = jnp.einsum(
            "hqe,hke->hqk", grad_block, value_row, preferred_element_type=jnp.float32
        )
        inner_sum = jnp.sum(soft_weights * grad_weights, axis=-1, keepdims=True)
        grad_scores = (soft_weights * (grad_weights - inner_sum)).astype(jnp.bfloat16)
        query_grad = (
            jnp.einsum("hqk,hke->hqe", grad_scores, key_row, preferred_element_type=jnp.float32)
            * score_scale
        )
        key_grad = (
            key_grad
            + jnp.einsum(
                "hqk,hqe->hke", grad_scores, query_block, preferred_element_type=jnp.float32
            )
            * score_scale
        )
        value_grad = value_grad + jnp.einsum(
            "hqk,hqe->hke",
            soft_weights.astype(jnp.bfloat16),
            grad_block,
            preferred_element_type=jnp.float32,
        )
        return ((key_grad, value_grad), query_grad)

    zero_grads = jnp.zeros(query_row.shape, jnp.float32)
    block_items = (
        split_blocks(query_row, block_rows),
        split_blocks(grad_row, block_rows),
        id_blocks,
        split_blocks(log_total, block_rows),
    )
    (key_grad, value_grad), query_grad = lax.scan(one_block, (zero_grads, zero_grads), block_items)
    return (join_blocks(query_grad), key_grad, value_grad)


def per_device(
    tokens,
    picture_ids,
    ln1_gain,
    ln1_bias,
    w_qkv,
    q_gain,
    k_gain,
    w_out,
    ln2_gain,
    ln2_bias,
    w_up,
    w_down,
    cotangent,
):
    row_count, local_slots, model_width = tokens.shape
    full_slots = picture_ids.shape[1]
    local_cols = w_qkv.shape[2]
    heads_here = local_cols // HD
    qkv_all, out_all, up_all, down_all = (
        lax.all_gather(w_qkv, "dp", axis=0, tiled=True),
        lax.all_gather(w_out, "dp", axis=1, tiled=True),
        lax.all_gather(w_up, "dp", axis=0, tiled=True),
        lax.all_gather(w_down, "dp", axis=1, tiled=True),
    )
    qkv_matrix = qkv_all.reshape(model_width, 3 * local_cols)
    tokens_float = tokens.astype(jnp.float32)
    normed_one, norm_one_pull = jax.vjp(layer_norm, tokens_float, ln1_gain, ln1_bias)
    normed_full = lax.all_gather(normed_one.astype(jnp.bfloat16), "tensor", axis=1, tiled=True)
    project = jnp.einsum("rsd,dc->rsc", normed_full, qkv_matrix, preferred_element_type=jnp.float32)
    project = project.reshape(row_count, full_slots, 3, heads_here, HD)
    (query_norm, key_norm), head_pull = jax.vjp(
        both_heads, project[:, :, 0], project[:, :, 1], q_gain, k_gain
    )
    query_rows = jnp.moveaxis(query_norm.astype(jnp.bfloat16), 2, 1)
    key_rows = jnp.moveaxis(key_norm.astype(jnp.bfloat16), 2, 1)
    value_rows = jnp.moveaxis(project[:, :, 2].astype(jnp.bfloat16), 2, 1)
    attended, log_total = lax.map(
        lambda row_items: attend_forward(row_items[0], row_items[1], row_items[2], row_items[3]),
        (query_rows, key_rows, value_rows, picture_ids),
    )
    attended_bf = (
        jnp.moveaxis(attended, 1, 2).reshape(row_count, full_slots, local_cols).astype(jnp.bfloat16)
    )
    branch_part = jnp.einsum(
        "rsc,cd->rsd", attended_bf, out_all, preferred_element_type=jnp.float32
    )
    middle = tokens_float + lax.psum_scatter(
        branch_part.astype(jnp.bfloat16), "tensor", scatter_dimension=1, tiled=True
    ).astype(jnp.float32)
    normed_float, norm_two_pull = jax.vjp(layer_norm, middle, ln2_gain, ln2_bias)
    normed_two = normed_float.astype(jnp.bfloat16)
    mlp_input = lax.all_gather(normed_two, "tensor", axis=1, tiled=True)
    up_proj = jnp.einsum("rsd,df->rsf", mlp_input, up_all, preferred_element_type=jnp.float32)
    hidden_float, gelu_pull = jax.vjp(gelu_exact, up_proj)
    hidden = hidden_float.astype(jnp.bfloat16)
    mlp_part = jnp.einsum("rsf,fd->rsd", hidden, down_all, preferred_element_type=jnp.float32)
    mlp_branch = lax.psum_scatter(
        mlp_part.astype(jnp.bfloat16), "tensor", scatter_dimension=1, tiled=True
    ).astype(jnp.float32)
    result = (middle + mlp_branch).astype(jnp.bfloat16)
    grad_input = lax.all_gather(cotangent, "tensor", axis=1, tiled=True)
    grad_hidden = jnp.einsum(
        "rsd,fd->rsf", grad_input, down_all, preferred_element_type=jnp.float32
    )
    grad_down = jnp.einsum("rsf,rsd->fd", hidden, grad_input, preferred_element_type=jnp.float32)
    grad_up_proj = gelu_pull(grad_hidden)[0].astype(jnp.bfloat16)
    grad_up = jnp.einsum("rsd,rsf->df", mlp_input, grad_up_proj, preferred_element_type=jnp.float32)
    grad_normed_two = jnp.einsum(
        "rsf,df->rsd", grad_up_proj, up_all, preferred_element_type=jnp.float32
    )
    grad_normed_two = lax.psum_scatter(
        grad_normed_two.astype(jnp.bfloat16), "tensor", scatter_dimension=1, tiled=True
    ).astype(jnp.float32)
    grad_middle, grad_ln2_gain, grad_ln2_bias = norm_two_pull(grad_normed_two)
    grad_middle = grad_middle + cotangent.astype(jnp.float32)
    grad_branch = lax.all_gather(grad_middle.astype(jnp.bfloat16), "tensor", axis=1, tiled=True)
    grad_out = jnp.einsum(
        "rsc,rsd->cd", attended_bf, grad_branch, preferred_element_type=jnp.float32
    )
    grad_attended = jnp.einsum(
        "rsd,cd->rsc", grad_branch, out_all, preferred_element_type=jnp.float32
    ).astype(jnp.bfloat16)
    grad_heads = jnp.moveaxis(grad_attended.reshape(row_count, full_slots, heads_here, HD), 2, 1)
    query_grad, key_grad, value_grad = lax.map(
        lambda row_items: attend_backward(
            row_items[0], row_items[1], row_items[2], row_items[3], row_items[4], row_items[5]
        ),
        (query_rows, key_rows, value_rows, picture_ids, log_total, grad_heads),
    )
    query_grad = jnp.moveaxis(query_grad, 1, 2)
    key_grad = jnp.moveaxis(key_grad, 1, 2)
    value_grad = jnp.moveaxis(value_grad, 1, 2)
    grad_query_raw, grad_key_raw, grad_q_gain, grad_k_gain = head_pull((query_grad, key_grad))
    grad_project = jnp.stack([grad_query_raw, grad_key_raw, value_grad], axis=2).astype(
        jnp.bfloat16
    )
    grad_project = grad_project.reshape(row_count, full_slots, 3 * local_cols)
    grad_qkv = jnp.einsum(
        "rsd,rsc->dc", normed_full, grad_project, preferred_element_type=jnp.float32
    )
    grad_qkv = grad_qkv.reshape(model_width, 3, local_cols)
    grad_normed_one = jnp.einsum(
        "rsc,dc->rsd", grad_project, qkv_matrix, preferred_element_type=jnp.float32
    )
    grad_normed_one = lax.psum_scatter(
        grad_normed_one.astype(jnp.bfloat16), "tensor", scatter_dimension=1, tiled=True
    ).astype(jnp.float32)
    grad_from_norm, grad_ln1_gain, grad_ln1_bias = norm_one_pull(grad_normed_one)
    grad_tokens = (grad_middle + grad_from_norm).astype(jnp.bfloat16)
    grad_qkv, grad_out, grad_up, grad_down = (
        lax.psum_scatter(grad_qkv, "dp", scatter_dimension=0, tiled=True),
        lax.psum_scatter(grad_out, "dp", scatter_dimension=1, tiled=True),
        lax.psum_scatter(grad_up, "dp", scatter_dimension=0, tiled=True),
        lax.psum_scatter(grad_down, "dp", scatter_dimension=1, tiled=True),
    )
    small_sums = lax.psum(
        (grad_ln1_gain, grad_ln1_bias, grad_q_gain, grad_k_gain, grad_ln2_gain, grad_ln2_bias),
        ("dp", "tensor"),
    )
    return (
        result,
        grad_tokens,
        small_sums[0],
        small_sums[1],
        grad_qkv,
        small_sums[2],
        small_sums[3],
        grad_out,
        small_sums[4],
        small_sums[5],
        grad_up,
        grad_down,
    )


def solution(mesh):
    in_specs = (
        P("dp", "tensor", None),
        P("dp", None),
        P(),
        P(),
        P("dp", None, "tensor"),
        P(),
        P(),
        P("tensor", "dp"),
        P(),
        P(),
        P("dp", "tensor"),
        P("tensor", "dp"),
        P("dp", "tensor", None),
    )
    out_specs = (
        P("dp", "tensor", None),
        P("dp", "tensor", None),
        P(),
        P(),
        P("dp", None, "tensor"),
        P(),
        P(),
        P("tensor", "dp"),
        P(),
        P(),
        P("dp", "tensor"),
        P("tensor", "dp"),
    )
    return jax.shard_map(
        per_device, mesh=mesh, in_specs=in_specs, out_specs=out_specs, check_vma=False
    )
```

profile of v0, /device:TPU:0, one launch (start us, length us, event | category | flops | bytes accessed | tf_op | source)
XLA Modules:
  0.0 924.2 jit_solution(6301381956992522163)
XLA Ops:
  14.9 38.6 %all_gather.25 = bf16[768,3,192]{2,1,0:T(4,128)(2,1)S(1)} all-gather(bf16[96,3,192]{2,1,0:T(4,128)(2,1)S(1)} %copy.34), channel_id=1, replica_groups=mesh['dp'=8,'tensor'=4] {'dp'}, dimensions={0}, use_global_device_ids=true | all-gather | bytes 995328 | tf_op jit(solution)/shard_map/all_gather | solution.py:140
  55.6 31.0 %all_gather.26 = bf16[192,768]{0,1:T(8,128)(2,1)S(1)} all-gather(bf16[192,96]{0,1:T(8,128)(2,1)S(1)} %copy.38), channel_id=1, replica_groups=mesh['dp'=8,'tensor'=4] {'dp'}, dimensions={1}, use_global_device_ids=true | all-gather | bytes 331776 | tf_op jit(solution)/shard_map/all_gather | solution.py:141
  86.6 4.1 convolution_bitcast_fusion
  96.3 83.0 %while.49 = (s32[]{:T(128)}, bf16[4,3,512,64]{2,3,1,0:T(8,128)(2,1)S(1)}, f32[4,3,512]{2,1,0:T(4,128)}, s32[4,512]{1,0:T(4,128)S(1)}, s32[2048]{0:T(1024)S(1)}, ...) while((s32[]{:T(128)}, ...), condition=%wide.region_9.10_spmd.clone, body=%wide.region_6.9_spmd.sunk.clone | while | flops 844102144 | bytes 44175468 | solution.py:70
  97.0 6.0 fusion.163
  103.0 6.8 fusion.164
  109.7 6.7 fusion.165
  117.7 6.0 fusion.163
  123.7 6.8 fusion.164
  130.5 6.7 fusion.165
  138.5 6.0 fusion.163
  144.4 6.8 fusion.164
  151.2 6.7 fusion.165
  159.2 6.0 fusion.163
  165.2 6.8 fusion.164
  171.9 6.7 fusion.165
  182.9 2.7 fusion.58
  186.6 36.7 %reduce-scatter.11.cloned.1.call-done = bf16[1,512,768]{2,1,0:T(8,128)(2,1)} async-done(((bf16[1,2048,768]{2,1,0:T(8,128)(2,1)}), bf16[1,512,768]{2,1,0:T(8,128)(2,1)}) %reduce-scatter.11.cloned.1.call-update) | async-done | bytes 786448 | tf_op jit(solution)/shard_map/reduce_scatter | solution.py:167
  230.3 28.3 %all-gather.9.cloned.1.call-done = bf16[1,2048,768]{2,1,0:T(8,128)(2,1)} async-done(((bf16[1,512,768]{2,1,0:T(8,128)(2,1)}), bf16[1,2048,768]{2,1,0:T(8,128)(2,1)}) %all-gather.9.cloned.1.call-update) | async-done | bytes 3145744 | tf_op jit(solution)/shard_map/all_gather | solution.py:172
  258.6 18.8 %multiply_convert_fusion.1 = (bf16[2048,768]{1,0:T(8,128)(2,1)}, f32[2048,768]{1,0:T(8,128)}, f32[2048,768]{1,0:T(8,128)}) fusion(bf16[768,768]{1,0:T(8,128)(2,1)} %all-gather.11.cloned.1.call-done, bf16[1,2048,768]{2,1,0:T(8,128)(2,1)} %all-gather.9.cloned.1.call-done), kind=kOutput, calls=%fused_computation.51 | convolution fusion | flops 2518155264 | bytes 20054016 | tf_op jit(solution)/shard_map/rsd,df->rsf/dot_general | solution.py:173
  277.4 25.1 %all-gather.13.cloned.1.call-done = bf16[768,768]{0,1:T(8,128)(2,1)} async-done(((bf16[768,96]{0,1:T(8,128)(2,1)}), bf16[768,768]{0,1:T(8,128)(2,1)}) %all-gather.13.cloned.1.call-update) | async-done | bytes 1179664 | tf_op jit(solution)/shard_map/all_gather | solution.py:143
  302.5 28.5 %all-gather.15.cloned.1.call-done = bf16[1,2048,768]{2,1,0:T(8,128)(2,1)} async-done(((bf16[1,512,768]{2,1,0:T(8,128)(2,1)}), bf16[1,2048,768]{2,1,0:T(8,128)(2,1)}) %all-gather.15.cloned.1.call-update) | async-done | bytes 3145744 | tf_op jit(solution)/shard_map/all_gather | solution.py:181
  331.0 10.1 %add_convert_fusion = bf16[2048,768]{1,0:T(8,128)(2,1)S(1)} fusion(f32[2048,768]{1,0:T(8,128)} %get-tuple-element.291, f32[2048,768]{1,0:T(8,128)} %get-tuple-element.301, bf16[768,768]{0,1:T(8,128)(2,1)} %all-gather.13.cloned.1.call-done, bf16[1,2048,768]{2,1,0:T(8,128)(2,1)} %all-gather.15.cloned.1.call-done), kind=kOutput, calls=%fused_computation.50 | convolution fusion | flops 2437939200 | bytes 20054016 | tf_op jit(solution)/shard_map/rsd,fd->rsf/dot_general | solution.py:182
  342.8 4.0 fusion.60
  346.9 6.5 fusion.59
  353.5 31.5 %reduce-scatter.15.cloned.1.call-done = bf16[1,512,768]{2,1,0:T(8,128)(2,1)} async-done(((bf16[1,2048,768]{2,1,0:T(8,128)(2,1)}), bf16[1,512,768]{2,1,0:T(8,128)(2,1)}) %reduce-scatter.15.cloned.1.call-update) | async-done | bytes 786448 | tf_op jit(solution)/shard_map/reduce_scatter | solution.py:191
  388.1 37.3 %reduce-scatter.13.cloned.1.call-done = bf16[1,512,768]{2,1,0:T(8,128)(2,1)} async-done(((bf16[1,2048,768]{2,1,0:T(8,128)(2,1)}), bf16[1,512,768]{2,1,0:T(8,128)(2,1)}) %reduce-scatter.13.cloned.1.call-update) | async-done | bytes 786448 | tf_op jit(solution)/shard_map/reduce_scatter | solution.py:177
  425.4 3.2 fusion.100
  430.9 28.4 %all-gather.17.cloned.1.call-done = bf16[1,2048,768]{2,1,0:T(8,128)(2,1)} async-done(((bf16[1,512,768]{2,1,0:T(8,128)(2,1)}), bf16[1,2048,768]{2,1,0:T(8,128)(2,1)}) %all-gather.17.cloned.1.call-update) | async-done | bytes 3145744 | tf_op jit(solution)/shard_map/all_gather | solution.py:196
  459.3 3.1 fusion.62
  463.2 124.9 %while.50 = (s32[]{:T(128)}, f32[3,2048,64]{1,2,0:T(8,128)}, f32[3,2048,64]{1,2,0:T(8,128)}, f32[4,3,512,64]{2,3,1,0:T(8,128)}, s32[4,512]{1,0:T(4,128)S(1)}, /*...) while((s32[]{:T(128)}, f32[3,2048,64]{1,2,0:T(8,128)}, ...), condition=%wide.region_19.20_spmd.clone.clone, body=%wide.region_17.19_spmd.clone.sunk.clone | while | flops 2063563264 | bytes 169273808 | solution.py:116
  466.7 4.7 fusion.177
  471.4 5.8 multiply_reduce_fusion.8
  477.2 4.9 multiply_convert_fusion.6
  482.1 2.6 copy-done
  487.2 6.2 fusion.178
  496.8 6.1 fusion.177
  502.9 5.8 multiply_reduce_fusion.8
  508.7 4.9 multiply_convert_fusion.6
  513.6 2.6 copy-done
  518.7 6.2 fusion.178
  528.2 6.1 fusion.177
  534.4 5.8 multiply_reduce_fusion.8
  540.1 4.9 multiply_convert_fusion.6
  545.1 2.6 copy-done
  550.2 6.2 fusion.178
  559.7 6.1 fusion.177
  565.9 5.8 multiply_reduce_fusion.8
  571.6 4.9 multiply_convert_fusion.6
  576.6 2.6 copy-done
  581.7 6.2 fusion.178
  591.6 4.5 fusion.86
  598.1 3.0 fusion.82
  606.1 4.0 fusion.61
  610.3 7.0 fusion.54
  617.6 7.0 fusion.50
  624.7 6.0 fusion.43
  630.7 28.1 %reduce-scatter.25.cloned.1.call-done = f32[96,192]{1,0:T(8,128)} async-done(((f32[768,192]{1,0:T(8,128)}), f32[96,192]{1,0:T(8,128)}) %reduce-scatter.25.cloned.1.call-update) | async-done | bytes 73744
  660.4 37.7 %reduce-scatter.17.cloned.1.call-done = bf16[1,512,768]{2,1,0:T(8,128)(2,1)} async-done(((bf16[1,2048,768]{2,1,0:T(8,128)(2,1)}), bf16[1,512,768]{2,1,0:T(8,128)(2,1)}) %reduce-scatter.17.cloned.1.call-update) | async-done | bytes 786448 | tf_op jit(solution)/shard_map/reduce_scatter | solution.py:225
  701.9 40.9 %all-reduce = (f32[768]{0:T(1024)}, f32[768]{0:T(1024)}, f32[64]{0:T(128)}, f32[64]{0:T(128)}, f32[768]{0:T(1024)}, /*index=5*/f32[768]{0:T(1024)}) all-reduce(f32[768]{0:T(1024)S(1)} %get-tuple-element.239, f32[768]{0:T(1024)S(1)} %get-tuple-element.242, ...), channel_id=1, replica_groups=mesh['dp'=8,'tensor'=4] {'dp','tensor'}, use_global_device_ids=true, to_apply=%region_28.29 | all-reduce | flops 3200 | bytes 25600 | tf_op jit(solution)/shard_map/psum | solution.py:236
  742.8 2.8 add_convert_fusion.1
  745.6 26.4 %reduce-scatter.21.cloned.1.call-done = f32[96,768]{1,0:T(8,128)} async-done(((f32[768,768]{1,0:T(8,128)}), f32[96,768]{1,0:T(8,128)}) %reduce-scatter.21.cloned.1.call-update) | async-done | bytes 294928 | tf_op jit(solution)/shard_map/reduce_scatter | solution.py:233
  772.0 72.3 %reduce-scatter.23.cloned.1.call-done = f32[768,96]{0,1:T(8,128)} async-done(((f32[768,768]{0,1:T(8,128)}), f32[768,96]{0,1:T(8,128)}) %reduce-scatter.23.cloned.1.call-update) | async-done | bytes 294928 | tf_op jit(solution)/shard_map/reduce_scatter | solution.py:234
  844.3 72.4 %reduce-scatter.19.cloned.1.call-done = f32[96,3,192]{2,0,1:T(8,128)} async-done(((f32[768,3,192]{2,0,1:T(8,128)}), f32[96,3,192]{2,0,1:T(8,128)}) %reduce-scatter.19.cloned.1.call-update) | async-done | bytes 221200 | tf_op jit(solution)/shard_map/reduce_scatter | solution.py:231
  (296 shorter events, 77.8 us)
Async XLA Ops:
  8.0 6.0 copy-start.25
  8.0 6.6 copy-start.40
  8.0 6.8 copy-start.35
  8.0 78.6 %all-gather.7.cloned.1.call-start = ((), (), s32[]{:S(2)}) async-start(), calls=%async_computation.8 | async-start | bytes 3932160 | tf_op jit(solution)/shard_map/all_gather | solution.py:148
  9.4 5.3 copy-start.36
  11.0 3.8 copy-start.42
  13.4 210.0 %reduce-scatter.11.cloned.1.call-start = ((), (), s32[]{:S(2)}) async-start(), calls=%async_computation.9 | async-start | bytes 3932160 | tf_op jit(solution)/shard_map/reduce_scatter | solution.py:167
  179.3 3.6 copy-start.10
  185.6 37.8 %copy-start.7 = (bf16[1,512,768]{2,1,0:T(8,128)(2,1)S(1)}, bf16[1,512,768]{2,1,0:T(8,128)(2,1)}, u32[]{:S(2)}) copy-start(bf16[1,512,768]{2,1,0:T(8,128)(2,1)} %param.17) | copy-start | bytes 2359300
  185.6 44.7 %all-gather.11.cloned.1.call-start = ((), (), s32[]{:S(2)}) async-start(), calls=%async_computation.11 | async-start | bytes 1327104 | tf_op jit(solution)/shard_map/all_gather | solution.py:142
  186.2 72.4 %all-gather.9.cloned.1.call-start = ((), (), s32[]{:S(2)}) async-start(), calls=%async_computation.10 | async-start | bytes 3932160 | tf_op jit(solution)/shard_map/all_gather | solution.py:172
  223.3 4.2 copy-start.11
  223.3 4.2 copy-start.41
  223.3 4.2 copy-start.57
  228.9 73.6 %all-gather.13.cloned.1.call-start = ((), (), s32[]{:S(2)}) async-start(), calls=%async_computation.12 | async-start | bytes 1327104 | tf_op jit(solution)/shard_map/all_gather | solution.py:143
  229.5 101.5 %all-gather.15.cloned.1.call-start = ((), (), s32[]{:S(2)}) async-start(), calls=%async_computation.14 | async-start | bytes 3932160 | tf_op jit(solution)/shard_map/all_gather | solution.py:181
  230.2 154.8 %reduce-scatter.15.cloned.1.call-start = ((), (), s32[]{:S(2)}) async-start(), calls=%async_computation.15 | async-start | bytes 3932160 | tf_op jit(solution)/shard_map/reduce_scatter | solution.py:191
  331.0 11.8 %copy-start.58 = (bf16[768,768]{1,0:T(8,128)(2,1)S(1)}, bf16[768,768]{1,0:T(8,128)(2,1)}, u32[]{:S(2)}) copy-start(bf16[768,768]{1,0:T(8,128)(2,1)} %all-gather.11.cloned.1.call-done) | copy-start | bytes 3538948
  346.9 78.5 %reduce-scatter.13.cloned.1.call-start = ((), (), s32[]{:S(2)}) async-start(), calls=%async_computation.13 | async-start | bytes 3932160 | tf_op jit(solution)/shard_map/reduce_scatter | solution.py:177
  353.5 105.9 %all-gather.17.cloned.1.call-start = ((), (), s32[]{:S(2)}) async-start(), calls=%async_computation.16 | async-start | bytes 3932160 | tf_op jit(solution)/shard_map/all_gather | solution.py:196
  425.4 4.3 copy-start.16
  430.9 227.9 %reduce-scatter.25.cloned.1.call-start = ((), (), s32[]{:S(2)}) async-start(), calls=%async_computation.21 | async-start | bytes 884736
  463.3 3.3 copy-start.2
  463.3 3.3 copy-start.14
  463.4 3.3 copy-start.18
  477.2 7.6 copy-start.4
  487.2 6.2 copy-start.5
  487.2 6.2 copy-start.15
  487.2 6.2 copy-start.19
  493.4 3.3 copy-start.2
  508.7 7.6 copy-start.4
  518.7 6.2 copy-start.5
  518.7 6.2 copy-start.15
  518.7 6.2 copy-start.19
  524.9 3.3 copy-start.2
  524.9 3.3 copy-start.14
  524.9 3.3 copy-start.18
  540.1 7.6 copy-start.4
  550.2 6.2 copy-start.5
  550.2 6.2 copy-start.15
  550.2 6.2 copy-start.19
  571.6 7.6 copy-start.4
  581.7 6.2 copy-start.5
  581.7 6.2 copy-start.15
  581.7 6.2 copy-start.19
  591.6 4.6 copy-start.6
  591.6 4.6 copy-start.22
  591.6 4.6 copy-start.56
  596.1 102.0 %reduce-scatter.17.cloned.1.call-start = ((), (), s32[]{:S(2)}) async-start(), calls=%async_computation.17 | async-start | bytes 3932160 | tf_op jit(solution)/shard_map/reduce_scatter | solution.py:225
  598.0 5.3 slice-start
  598.1 5.2 slice-start.1
  610.2 161.8 %reduce-scatter.21.cloned.1.call-start = ((), (), s32[]{:S(2)}) async-start(), calls=%async_computation.19 | async-start | bytes 2654208 | tf_op jit(solution)/shard_map/reduce_scatter | solution.py:233
  617.3 227.0 %reduce-scatter.23.cloned.1.call-start = ((), (), s32[]{:S(2)}) async-start(), calls=%async_computation.20 | async-start | bytes 2654208 | tf_op jit(solution)/shard_map/reduce_scatter | solution.py:234
  624.6 292.0 %reduce-scatter.19.cloned.1.call-start = ((), (), s32[]{:S(2)}) async-start(), calls=%async_computation.18 | async-start | bytes 2654208 | tf_op jit(solution)/shard_map/reduce_scatter | solution.py:231
  630.6 67.5 %copy-start.8 = (bf16[1,512,768]{2,1,0:T(8,128)(2,1)S(1)}, bf16[1,512,768]{2,1,0:T(8,128)(2,1)}, u32[]{:S(2)}) copy-start(bf16[1,512,768]{2,1,0:T(8,128)(2,1)} %param.17) | copy-start | bytes 2359300
  630.6 67.5 %copy-start.37 = (f32[512]{0:T(512)S(1)}, f32[512]{0:T(512)}, u32[]{:S(2)}) copy-start(f32[512]{0:T(512)} %copy-done.36) | copy-start | bytes 6148
  630.6 67.5 %copy-start.38 = (f32[768]{0:T(1024)S(1)}, f32[768]{0:T(1024)}, u32[]{:S(2)}) copy-start(f32[768]{0:T(1024)} %param.19) | copy-start | bytes 9220
  630.6 69.2 %copy-start.48 = (f32[512]{0:T(512)S(1)}, f32[512]{0:T(512)}, u32[]{:S(2)}) copy-start(f32[512]{0:T(512)} %copy-done.47) | copy-start | bytes 6148
  630.7 69.2 %copy-start.43 = (f32[512]{0:T(512)S(1)}, f32[512]{0:T(512)}, u32[]{:S(2)}) copy-start(f32[512]{0:T(512)} %copy-done.42) | copy-start | bytes 6148
  630.7 71.3 %copy-start.51 = (f32[768]{0:T(1024)S(1)}, f32[768]{0:T(1024)}, u32[]{:S(2)}) copy-start(f32[768]{0:T(1024)} %get-tuple-element.237) | copy-start | bytes 9220
  630.7 71.3 %copy-start.52 = (f32[768]{0:T(1024)S(1)}, f32[768]{0:T(1024)}, u32[]{:S(2)}) copy-start(f32[768]{0:T(1024)} %get-tuple-element.241) | copy-start | bytes 9220
  630.7 112.1 %copy-start.13 = (f32[1,512,768]{2,1,0:T(8,128)S(1)}, f32[1,512,768]{2,1,0:T(8,128)}, u32[]{:S(2)}) copy-start(f32[1,512,768]{2,1,0:T(8,128)} %copy-done.12) | copy-start | bytes 4718596
  630.7 112.1 %copy-start.17 = (bf16[1,512,768]{2,1,0:T(8,128)(2,1)S(1)}, bf16[1,512,768]{2,1,0:T(8,128)(2,1)}, u32[]{:S(2)}) copy-start(bf16[1,512,768]{2,1,0:T(8,128)(2,1)} %param.29) | copy-start | bytes 2359300
  630.7 112.1 %copy-start.46 = (f32[512]{0:T(512)S(1)}, f32[512]{0:T(512)}, u32[]{:S(2)}) copy-start(f32[512]{0:T(512)} %copy-done.45) | copy-start | bytes 6148
  (42 other events, 91.2 us)
Sparse Core Ops, SparseCore 0:
  13.5 31.2 all-gather.6
  185.7 37.5 reduce-scatter.10
  347.0 37.9 reduce-scatter.14
  387.4 37.9 reduce-scatter.12
Sparse Core Ops, SparseCore 1:
  188.5 41.1 all-gather.10
  231.7 26.8 all-gather.8
  260.9 41.5 all-gather.12
  304.1 26.8 all-gather.14
  430.9 28.3 all-gather.16
  596.2 62.5 reduce-scatter.24
  661.2 36.9 reduce-scatter.16
  702.5 69.4 reduce-scatter.20
  776.3 67.9 reduce-scatter.22
  848.8 67.8 reduce-scatter.18
where the time goes:
time: 935 us; the launch traced here: 924 us
  waiting for transfers between devices  455 us (49%)
  matrix products  216 us (23%)
  blocking collectives  110 us (12%)
  other arithmetic  89.8 us (10%)
  local copies, waits for them, and re-layouts  34.2 us (4%)
  between operations  16.6 us (2%)
    reduce_scatter x1, waiting for transfers between devices, per_device(): lax.psum_scatter(grad_qkv, 'dp', scatter_dimension=0, tiled=True)  72.4 us
    reduce_scatter x1, waiting for transfers between devices, per_device(): lax.psum_scatter(grad_down, 'dp', scatter_dimension=1, tiled=True)  72.3 us
    psum x1, blocking collectives, per_device(): lax.psum((grad_ln1_gain, grad_ln1_bias, grad_q_gain, grad_k_gain, grad_ln...  40.9 us
    all_gather x1, blocking collectives, per_device(): lax.all_gather(w_qkv, 'dp', axis=0, tiled=True)  38.6 us
    reduce_scatter x1, waiting for transfers between devices, per_device(): lax.psum_scatter(grad_normed_one.astype(jnp.bfloat16), 'tensor', scatter_...  37.7 us
    reduce_scatter x1, waiting for transfers between devices, per_device(): lax.psum_scatter(mlp_part.astype(jnp.bfloat16), 'tensor', scatter_dimensi...  37.3 us
    reduce_scatter x1, waiting for transfers between devices, per_device(): lax.psum_scatter(branch_part.astype(jnp.bfloat16), 'tensor', scatter_dime...  36.7 us
    reduce_scatter x1, waiting for transfers between devices, per_device(): lax.psum_scatter(grad_normed_two.astype(jnp.bfloat16), 'tensor', scatter_...  31.5 us
  transfers between devices with their start and end apart: 14, of which 12 were waited for; matrix products, arithmetic and copies ran while one was open for 8% of the time, Pallas kernels for 0%

commit v1 on v0

v1 whole, which is shorter than its diff:
```python
import functools

import jax
import jax.numpy as jnp
from jax import lax
from jax.experimental import pallas as pl
from jax.experimental.pallas import tpu as pltpu
from jax.sharding import PartitionSpec as P

HD=64; EPSILON=1e-6
LOG2E=1.4426950408889634
QSCALE=LOG2E/8.0
BIG=256.0
F32=jnp.float32; BF=jnp.bfloat16

def nn(a,b): return lax.dot_general(a,b,(((1,),(0,)),((),())),preferred_element_type=F32)

def norm_T(x):
    c = x - jnp.mean(x,axis=0,keepdims=True)
    inv = lax.rsqrt(jnp.mean(c*c,axis=0,keepdims=True)+EPSILON)
    return c*inv, inv

def split3(v):
    hi=v.astype(BF).astype(F32); r=v-hi
    mid=r.astype(BF).astype(F32); lo=r-mid
    return hi,mid,lo

def fwd_kernel(n_ref,l_ref, q_ref,k_ref,v_ref,fq_ref,fk_ref,qg_ref,kg_ref,o_ref,lse_ref,KT,QN,VN,*,HG,Q,K,BQ,BK,CH):
    ones_row = jnp.where(lax.broadcasted_iota(jnp.int32,(64,CH),0)==0,1.0,0.0).astype(F32)
    for h in range(HG):
        for c in range(K//CH):
            s=slice(c*CH,(c+1)*CH)
            kn,_=norm_T(k_ref[h,:,s])
            KT[h,:64,s]=(kn*kg_ref[...]).astype(BF)
            KT[h,64:,s]=fk_ref[:,s]
            VN[h,s,:]=jnp.concatenate([v_ref[h,:,s].astype(F32),ones_row],axis=0).T.astype(BF)
        for c in range(Q//CH):
            s=slice(c*CH,(c+1)*CH)
            qn,_=norm_T(q_ref[h,:,s])
            qa=jnp.concatenate([qn*(qg_ref[...]*QSCALE),fq_ref[:,s].astype(F32)],axis=0)
            QN[h,s,:]=qa.T.astype(BF)
    NK=K//BK
    for qb in range(Q//BQ):
        def body(i,accs):
            kb=pl.multiple_of(l_ref[qb*NK+i]*BK,BK)
            out=[]
            for h in range(HG):
                S=nn(QN[h,qb*BQ:(qb+1)*BQ,:],KT[h,:,pl.ds(kb,BK)])
                P=jnp.exp2(S).astype(BF)
                out.append(accs[h]+nn(P,VN[h,pl.ds(kb,BK),:]))
            return tuple(out)
        accs=lax.fori_loop(0,n_ref[qb],body,tuple(jnp.zeros((BQ,128),F32) for _ in range(HG)))
        for h in range(HG):
            t=accs[h].T
            tot=t[64:65]
            s=slice(qb*BQ,(qb+1)*BQ)
            o_ref[h,:,s]=(t[:64]/tot).astype(BF)
            lse_ref[h,:,s]=jnp.log2(tot)

def attn_fwd(n,l,q,kv,fq,fk,qg,kg,*,HG=3,BQ=256,BK=256,CH=512):
    R,_,Q=q.shape; K=kv.shape[-1]
    q=q.reshape(R,3,64,Q); kv=kv.reshape(R,2,3,64,K)
    G=3//HG
    kern=functools.partial(fwd_kernel,HG=HG,Q=Q,K=K,BQ=BQ,BK=BK,CH=CH)
    full=lambda shp: pl.BlockSpec(shp,lambda r,g,*_:(0,)*len(shp))
    o,lse=pl.pallas_call(kern,
      out_shape=(jax.ShapeDtypeStruct((R,3,64,Q),BF),jax.ShapeDtypeStruct((R,3,1,Q),F32)),
      grid_spec=pltpu.PrefetchScalarGridSpec(num_scalar_prefetch=2,grid=(R,G),
        in_specs=[pl.BlockSpec((None,HG,64,Q),lambda r,g,*_:(r,g,0,0)),
                  pl.BlockSpec((None,None,HG,64,K),lambda r,g,*_:(r,0,g,0,0)),
                  pl.BlockSpec((None,None,HG,64,K),lambda r,g,*_:(r,1,g,0,0)),
                  full((64,Q)),full((64,K)),full((64,1)),full((64,1))],
        out_specs=(pl.BlockSpec((None,HG,64,Q),lambda r,g,*_:(r,g,0,0)),pl.BlockSpec((None,HG,1,Q),lambda r,g,*_:(r,g,0,0))),
        scratch_shapes=[pltpu.VMEM((HG,128,K),BF),pltpu.VMEM((HG,Q,128),BF),pltpu.VMEM((HG,K,128),BF)]),
      compiler_params=pltpu.CompilerParams(vmem_limit_bytes=50*2**20),
      name="attn_fwd")(n,l,q,kv,kv,fq,fk,qg.reshape(64,1),kg.reshape(64,1))
    return o,lse

def bwd_kernel(n_ref,l_ref, q_ref,k_ref,v_ref,do_ref,o_ref,lse_ref,fq_ref,fk_ref,qg_ref,kg_ref,
               gq_ref,gkv_ref,gqg_ref,gkg_ref, KT,KN,VN,QT,QN,DOT,DON,DQT,DK,DV,*,HG,Q,K,BQ,BK,CH):
    first=(pl.program_id(0)==0)&(pl.program_id(1)==0)
    @pl.when(first)
    def _():
        gqg_ref[...]=jnp.zeros_like(gqg_ref); gkg_ref[...]=jnp.zeros_like(gkg_ref)
    row=lax.broadcasted_iota(jnp.int32,(64,CH),0)
    three=jnp.where(row<3,1.0,0.0).astype(F32)
    for h in range(HG):
        for c in range(K//CH):
            s=slice(c*CH,(c+1)*CH)
            kn,_=norm_T(k_ref[h,:,s])
            kt=jnp.concatenate([kn*kg_ref[...],fk_ref[:,s].astype(F32)],axis=0)
            KT[h,:,s]=kt[:64].astype(BF)
            KN[h,s,:]=kt.T.astype(BF)
            VN[h,s,:]=jnp.concatenate([v_ref[h,:,s].astype(F32),three],axis=0).T.astype(BF)
            DK[h,s,:]=jnp.zeros((CH,128),F32); DV[h,s,:]=jnp.zeros((CH,128),F32)
        for c in range(Q//CH):
            s=slice(c*CH,(c+1)*CH)
            qn,_=norm_T(q_ref[h,:,s])
            a,b,d=split3(-lse_ref[h,:,s])
            f=fq_ref[:,s].astype(F32)
            f=jnp.where(row==33,a,jnp.where(row==34,b,jnp.where(row==35,d,f)))
            qt=jnp.concatenate([qn*(qg_ref[...]*QSCALE),f],axis=0)
            QT[h,:,s]=qt.astype(BF)
            QN[h,s,:]=qt.T.astype(BF)
            do=do_ref[h,:,s].astype(F32)
            D=-jnp.sum(do*o_ref[h,:,s].astype(F32),axis=0,keepdims=True)
            a,b,d=split3(D)
            g=jnp.where(row==0,a,jnp.where(row==1,b,jnp.where(row==2,d,0.0)))
            dt=jnp.concatenate([do,g],axis=0)
            DOT[h,:,s]=dt.astype(BF)
            DON[h,s,:]=dt.T.astype(BF)
    NK=K//BK
    for qb in range(Q//BQ):
        qs=slice(qb*BQ,(qb+1)*BQ)
        def body(i,accs):
            kb=pl.multiple_of(l_ref[qb*NK+i]*BK,BK)
            ks=pl.ds(kb,BK)
            out=[]
            for h in range(HG):
                ST=nn(KN[h,ks,:],QT[h,:,qs])
                P=jnp.exp2(ST)
                DP=nn(VN[h,ks,:],DOT[h,:,qs])
                dS=(P*DP).astype(BF)
                DV[h,ks,:]+=nn(P.astype(BF),DON[h,qs,:])
                DK[h,ks,:]+=nn(dS,QN[h,qs,:])
                out.append(accs[h]+nn(KT[h,:,ks],dS))
            return tuple(out)
        accs=lax.fori_loop(0,n_ref[qb],body,tuple(jnp.zeros((64,BQ),F32) for _ in range(HG)))
        for h in range(HG): DQT[h,:,qs]=accs[h]
    def ln_back(dx,gain,raw):
        hat,inv=norm_T(raw)
        u=dx*gain
        g=inv*(u-jnp.mean(u,axis=0,keepdims=True)-hat*jnp.mean(u*hat,axis=0,keepdims=True))
        return g, jnp.sum(dx*hat,axis=1,keepdims=True)
    for h in range(HG):
        for c in range(K//CH):
            s=slice(c*CH,(c+1)*CH)
            g,gg=ln_back(DK[h,s,:].T[:64]*(1.0/LOG2E),kg_ref[...],k_ref[h,:,s])
            gkv_ref[0,h,:,s]=g.astype(BF)
            gkg_ref[...]+=gg
            gkv_ref[1,h,:,s]=DV[h,s,:].T[:64].astype(BF)
        for c in range(Q//CH):
            s=slice(c*CH,(c+1)*CH)
            g,gg=ln_back(DQT[h,:,s]*0.125,qg_ref[...],q_ref[h,:,s])
            gq_ref[h,:,s]=g.astype(BF)
            gqg_ref[...]+=gg

def attn_bwd(n,l,q,kv,do,o,lse,fq,fk,qg,kg,*,HG=3,BQ=256,BK=256,CH=512):
    R,_,Q=q.shape; K=kv.shape[-1]
    q=q.reshape(R,3,64,Q); kv=kv.reshape(R,2,3,64,K); do=do.reshape(R,3,64,Q)
    G=3//HG
    kern=functools.partial(bwd_kernel,HG=HG,Q=Q,K=K,BQ=BQ,BK=BK,CH=CH)
    full=lambda shp: pl.BlockSpec(shp,lambda r,g,*_:(0,)*len(shp))
    qsp=lambda: pl.BlockSpec((None,HG,64,Q),lambda r,g,*_:(r,g,0,0))
    return pl.pallas_call(kern,
      out_shape=(jax.ShapeDtypeStruct((R,3,64,Q),BF),jax.ShapeDtypeStruct((R,2,3,64,K),BF),jax.ShapeDtypeStruct((64,1),F32),jax.ShapeDtypeStruct((64,1),F32)),
      grid_spec=pltpu.PrefetchScalarGridSpec(num_scalar_prefetch=2,grid=(R,G),
        in_specs=[qsp(),
                  pl.BlockSpec((None,None,HG,64,K),lambda r,g,*_:(r,0,g,0,0)),
                  pl.BlockSpec((None,None,HG,64,K),lambda r,g,*_:(r,1,g,0,0)),
                  qsp(),qsp(),pl.BlockSpec((None,HG,1,Q),lambda r,g,*_:(r,g,0,0)),
                  full((64,Q)),full((64,K)),full((64,1)),full((64,1))],
        out_specs=(qsp(),pl.BlockSpec((None,2,HG,64,K),lambda r,g,*_:(r,0,g,0,0)),full((64,1)),full((64,1))),
        scratch_shapes=[pltpu.VMEM((HG,64,K),BF),pltpu.VMEM((HG,K,128),BF),pltpu.VMEM((HG,K,128),BF),
                        pltpu.VMEM((HG,128,Q),BF),pltpu.VMEM((HG,Q,128),BF),pltpu.VMEM((HG,128,Q),BF),pltpu.VMEM((HG,Q,128),BF),
                        pltpu.VMEM((HG,64,Q),F32),pltpu.VMEM((HG,K,128),F32),pltpu.VMEM((HG,K,128),F32)]),
      compiler_params=pltpu.CompilerParams(vmem_limit_bytes=56*2**20),
      name="attn_bwd")(n,l,q,kv,kv,do,o,lse,fq,fk,qg.reshape(64,1),kg.reshape(64,1))

def features(ids, Q, BQ=256, BK=256):
    K=ids.shape[0]
    r=jnp.arange(64,dtype=jnp.int32)[:,None]
    hot=(ids[None,:]+1)==r
    hot=hot&(r<32)
    fk=jnp.where(hot,1.0,jnp.where((r>=32)&(r<36),1.0,0.0)).astype(BF)
    fq=jnp.where(hot[:,:Q],BIG,jnp.where(r==32,-BIG,0.0)).astype(BF)
    kb=hot[:32].reshape(32,K//BK,BK).any(-1)
    qb=hot[:32,:Q].reshape(32,Q//BQ,BQ).any(-1)
    act=(qb[:,:,None]&kb[:,None,:]).any(0)
    n=act.sum(-1).astype(jnp.int32)
    NK=K//BK
    before=jnp.arange(NK)[:,None]>jnp.arange(NK)[None,:]
    rank=(act[:,None,:]&before[None]).sum(-1)
    lst=((rank[:,None,:]==jnp.arange(NK)[None,:,None])&act[:,None,:])
    lst=(lst*jnp.arange(NK)[None,None,:]).sum(-1).astype(jnp.int32)
    return fq,fk,n,lst.reshape(-1)


def xor_perm(size, mask):
    return [(i, i ^ mask) for i in range(size)]


def swap(values, axis, mask):
    return lax.ppermute(values, axis, xor_perm(lax.axis_size(axis), mask))


def place(held, got, bit, axis):
    low = jnp.where(bit == 0, held, got)
    high = jnp.where(bit == 0, got, held)
    return jnp.stack([low, high], axis=axis)


def gather_weights(shard):
    rows, cols = shard.shape
    size = lax.axis_size("dp")
    me = lax.axis_index("dp")
    held = shard[None]
    for level in reversed(range(1, size.bit_length() - 1)):
        got = swap(held, "dp", 1 << level)
        held = place(held, got, (me >> level) & 1, 1).reshape(-1, rows, cols)
    count = held.shape[0]
    half = rows // 2
    part_a, part_b = held[:, :half], held[:, half:]
    bit = me & 1
    part_a = jnp.stack([part_a, swap(part_a, "tensor", 2)], axis=0)
    part_b = place(part_b, swap(part_b, "dp", 1), bit, 1)
    part_a = place(part_a, swap(part_a, "dp", 1), bit, 2)
    part_b = jnp.stack([part_b, swap(part_b, "tensor", 2)], axis=0)
    both = jnp.concatenate([part_a, part_b], axis=3)
    return both.reshape(2, count * 2 * rows, cols)


def take_half(values, bit, axis):
    return lax.dynamic_index_in_dim(values, bit, axis, keepdims=False)


def scatter_grads(grad):
    size = lax.axis_size("dp")
    me = lax.axis_index("dp")
    cols = grad.shape[2]
    rows = grad.shape[1] // size
    half = rows // 2
    bit = me & 1
    grad = grad.reshape(2, size // 2, 2, rows, cols)
    part_a, part_b = grad[:, :, :, :half], grad[:, :, :, half:]
    got = swap(take_half(part_a, 1 - bit, 2).astype(BF), "dp", 1)
    part_a = take_half(part_a, bit, 2) + got.astype(F32)
    got = swap(part_b[1].astype(BF), "tensor", 2)
    part_b = part_b[0] + got.astype(F32)
    got = swap(part_a[1].astype(BF), "tensor", 2)
    part_a = part_a[0] + got.astype(F32)
    got = swap(take_half(part_b, 1 - bit, 1).astype(BF), "dp", 1)
    part_b = take_half(part_b, bit, 1) + got.astype(F32)
    held = jnp.concatenate([part_a, part_b], axis=1)
    for level in range(1, size.bit_length() - 1):
        bit = (me >> level) & 1
        held = held.reshape(-1, 2, rows, cols)
        got = swap(take_half(held, 1 - bit, 1).astype(BF), "dp", 1 << level)
        held = take_half(held, bit, 1) + got.astype(F32)
    return held.reshape(rows, cols)


def sum_all(values):
    values = values + swap(values, "tensor", 1)
    values = values + swap(values, "tensor", 2)
    for level in range(lax.axis_size("dp").bit_length() - 1):
        values = values + swap(values, "dp", 1 << level)
    return values


def hat_of(values):
    center = values - jnp.mean(values, axis=-1, keepdims=True)
    inv = lax.rsqrt(jnp.mean(center * center, axis=-1, keepdims=True) + EPSILON)
    return center * inv, inv


def hat_back(grad, gain, hat, inv):
    u = grad * gain
    return inv * (u - jnp.mean(u, axis=-1, keepdims=True) - hat * jnp.mean(u * hat, axis=-1, keepdims=True))


def gelu_pair(v):
    x = jnp.abs(v) * (0.5**0.5)
    t = 1.0 / (1.0 + 0.3275911 * x)
    e = jnp.exp(-x * x)
    poly = ((((1.061405429 * t - 1.453152027) * t + 1.421413741) * t - 0.284496736) * t + 0.254829592) * t
    tail = 0.5 * poly * e
    phi = jnp.where(v < 0, tail, 1.0 - tail)
    return v * phi, phi + v * e * 0.3989422804014327


def own_part(share):
    half = share.shape[0] // 2
    got = swap(share[half:].astype(BF), "tensor", 1)
    return share[:half] + got.astype(F32)


def with_core(own):
    return jnp.concatenate([own, swap(own, "tensor", 1)], axis=0)


def mm(spec, *arrays):
    return jnp.einsum(spec, *arrays, preferred_element_type=F32)


def per_device(tokens, picture_ids, ln1_gain, ln1_bias, w_qkv, q_gain, k_gain, w_out, ln2_gain, ln2_bias, w_up, w_down, cotangent):
    slots, width = tokens.shape[1:]
    local = w_qkv.shape[2]
    hidden_cols = w_up.shape[1]
    tok = tokens[0]
    cot = cotangent[0]
    tensor = lax.axis_index("tensor")
    tok_x = swap(tok, "tensor", 2)
    tok_c = swap(tok, "tensor", 1)
    w_one = gather_weights(jnp.concatenate([w_qkv[:, 1], w_qkv[:, 2], w_qkv[:, 0]], axis=1))
    w_two = gather_weights(jnp.concatenate([w_up, w_down.T, w_out.T], axis=1))
    tok_xc = swap(tok_x, "tensor", 1)
    cot_all = with_core(cot)
    ids = picture_ids[0].reshape(4, slots)
    ids = jnp.concatenate([lax.dynamic_index_in_dim(ids, tensor ^ i, 0, keepdims=False) for i in range(4)])
    q_slots = 2 * slots
    fq, fk, count, blocks = features(ids, q_slots, BQ, BK)

    hats = [hat_of(block.astype(F32)) for block in (tok, tok_c, tok_x, tok_xc)]
    normed = jnp.concatenate([(hat * ln1_gain + ln1_bias).astype(BF) for hat, _ in hats], axis=0)
    kv = mm("sd,rdc->rcs", normed, w_one[:, :, : 2 * local]).reshape(2, 2, local, 4 * slots)
    q = mm("sd,rdc->rcs", normed[:q_slots], w_one[:, :, 2 * local :])
    att, lse = attn_fwd(count, blocks, q, kv, fq, fk, q_gain, k_gain, HG=HGF, BQ=BQ, BK=BK)
    att_cols = att.reshape(2, local, q_slots)

    wu = w_two[:, :, :hidden_cols]
    wd = w_two[:, :, hidden_cols : 2 * hidden_cols]
    wo = w_two[:, :, 2 * hidden_cols :]
    middle = tok.astype(F32) + own_part(mm("rcs,rdc->sd", att_cols, wo))
    hat2, inv2 = hat_of(middle)
    normed2 = with_core((hat2 * ln2_gain + ln2_bias).astype(BF))
    hid, slope = gelu_pair(mm("sd,rdf->srf", normed2, wu))
    hid = hid.astype(BF)
    slope = slope.astype(BF)
    grad_up = (mm("sd,rdf->srf", cot_all, wd) * slope.astype(F32)).astype(BF)
    grad_normed2 = own_part(mm("srf,rdf->sd", grad_up, wu))
    grad_wu = mm("sd,srf->rdf", normed2, grad_up)
    grad_wd = mm("sd,srf->rdf", cot_all, hid)
    grad_gain2 = jnp.sum(grad_normed2 * hat2, axis=0)
    grad_bias2 = jnp.sum(grad_normed2, axis=0)
    grad_mid = cot.astype(F32) + hat_back(grad_normed2, ln2_gain, hat2, inv2)
    branch = with_core(grad_mid.astype(BF))
    grad_att = mm("sd,rdc->rcs", branch, wo).astype(BF)
    grad_wo = mm("sd,rcs->rdc", branch, att_cols)
    result = (middle + own_part(mm("srf,rdf->sd", hid, wd))).astype(BF)
    grad_two = scatter_grads(jnp.concatenate([grad_wu, grad_wd, grad_wo], axis=2))

    gq, gkv, grad_qg, grad_kg = attn_bwd(
        count, blocks, q, kv, grad_att, att, lse, fq, fk, q_gain, k_gain, HG=HGB, BQ=BQ, BK=BK
    )
    gq = gq.reshape(2, local, q_slots)
    gkv = gkv.reshape(2, 2 * local, 4 * slots)
    other = mm("rcs,rdc->sd", gkv[:, :, q_slots:], w_one[:, :, : 2 * local])
    here = mm("rcs,rdc->sd", jnp.concatenate([gkv[:, :, :q_slots], gq], axis=1), w_one)
    across = own_part(other)
    grad_normed = own_part(here)
    got = swap(across.astype(BF), "tensor", 2)
    grad_wkv = mm("sd,rcs->rdc", normed, gkv)
    grad_wq = mm("sd,rcs->rdc", normed[:q_slots], gq)
    grad_one = scatter_grads(jnp.concatenate([grad_wkv, grad_wq], axis=2))
    hat1, inv1 = hats[0]
    grad_gain1 = jnp.sum(grad_normed * hat1, axis=0) + jnp.sum(across * hats[2][0], axis=0)
    grad_bias1 = jnp.sum(grad_normed, axis=0) + jnp.sum(across, axis=0)
    heads = jnp.pad(jnp.concatenate([grad_qg[:, 0], grad_kg[:, 0]]), (0, width - 2 * HD))
    small = sum_all(jnp.stack([grad_gain1, grad_bias1, grad_gain2, grad_bias2, heads]))
    grad_normed = grad_normed + got.astype(F32)
    grad_tokens = (grad_mid + hat_back(grad_normed, ln1_gain, hat1, inv1)).astype(BF)

    grad_qkv = jnp.stack([grad_one[:, 2 * local :], grad_one[:, :local], grad_one[:, local : 2 * local]], axis=1)
    return (
        result[None],
        grad_tokens[None],
        small[0],
        small[1],
        grad_qkv,
        small[4, :HD],
        small[4, HD : 2 * HD],
        grad_two[:, 2 * hidden_cols :].T,
        small[2],
        small[3],
        grad_two[:, :hidden_cols],
        grad_two[:, hidden_cols : 2 * hidden_cols].T,
    )


BQ = 512
BK = 256
HGF = 3
HGB = 3


def solution(mesh):
    rows = P("dp", "tensor", None)
    wide = P("dp", "tensor")
    tall = P("tensor", "dp")
    qkv = P("dp", None, "tensor")
    in_specs = (rows, P("dp", None), P(), P(), qkv, P(), P(), tall, P(), P(), wide, tall, rows)
    out_specs = (rows, rows, P(), P(), qkv, P(), P(), tall, P(), P(), wide, tall)
    return jax.shard_map(per_device, mesh=mesh, in_specs=in_specs, out_specs=out_specs, check_vma=False)
```

time: 935 us -> 416 us (0.44)
  waiting for transfers between devices: 455 us -> 154 us
  matrix products: 216 us -> 51.1 us
  blocking collectives: 110 us -> 0 us
  Pallas kernels: 0 us -> 47 us
  starting transfers between devices: 1.19 us -> 47.7 us
  other arithmetic: 89.8 us -> 53.8 us
  local copies, waits for them, and re-layouts: 34.2 us -> 51.3 us
  between operations: 16.6 us -> 2.33 us
    reduce_scatter x7 -> x0, waiting for transfers between devices: 314 us -> none  [the longest x1 72.4 us: per_device(): lax.psum_scatter(grad_qkv, 'dp', scatter_dimension=0, tiled=True)]
    dot_general x39 -> x15, matrix products: 212 us -> 51.1 us  [mm(): return jnp.einsum(spec, *arrays, preferred_element_type=F32)]
    ppermute x0 -> x41, waiting for transfers between devices: none -> 154 us  [swap(): return lax.ppermute(values, axis, xor_perm(lax.axis_size(axis), mask))]
    all_gather x6 -> x0, waiting for transfers between devices: 110 us -> none  [the longest x1 28.5 us: per_device(): grad_input = lax.all_gather(cotangent, 'tensor', axis=1, tiled=True)]
    all_gather x2 -> x0, blocking collectives: 69.6 us -> none  [the longest x1 38.6 us: per_device(): lax.all_gather(w_qkv, 'dp', axis=0, tiled=True)]
    ppermute x0 -> x41, starting transfers between devices: none -> 47.7 us  [swap(): return lax.ppermute(values, axis, xor_perm(lax.axis_size(axis), mask))]
    pallas_call x0 -> x2, Pallas kernels: none -> 47 us  [the longest x1 30.1 us: attn_bwd(): pl.pallas_call(kern, out_shape=(jax.ShapeDtypeStruct((R, 3, 64, Q), BF),...]
    psum x1 -> x0, blocking collectives: 40.9 us -> none  [per_device(): lax.psum((grad_ln1_gain, grad_ln1_bias, grad_q_gain, grad_k_gain, grad_ln...]
  transfers between devices with their start and end apart: 14 -> 41, of which waited for: 12 -> 20; matrix products, arithmetic and copies ran while one was open for 8% -> 24% of each run, Pallas kernels for 0% -> 4%
where the time goes in v1:
time: 416 us; the launch traced here: 408 us
  waiting for transfers between devices  154 us (37%)
  other arithmetic  53.8 us (13%)
  local copies, waits for them, and re-layouts  51.3 us (12%)
  matrix products  51.1 us (12%)
  starting transfers between devices  47.7 us (11%)
  Pallas kernels  47 us (11%)
    ppermute x41, waiting for transfers between devices, swap(): return lax.ppermute(values, axis, xor_perm(lax.axis_size(axis), mask))  154 us
    dot_general x15, matrix products, mm(): return jnp.einsum(spec, *arrays, preferred_element_type=F32)  51.1 us
    ppermute x41, starting transfers between devices, swap(): return lax.ppermute(values, axis, xor_perm(lax.axis_size(axis), mask))  47.7 us
    pallas_call x1, Pallas kernels, attn_bwd(): pl.pallas_call(kern, out_shape=(jax.ShapeDtypeStruct((R, 3, 64, Q), BF),...  30.1 us
    pallas_call x1, Pallas kernels, attn_fwd(): pl.pallas_call(kern, out_shape=(jax.ShapeDtypeStruct((R, 3, 64, Q), BF),...  16.9 us
    concatenate x1, local copies, waits for them, and re-layouts, per_device(): jnp.concatenate([grad_wu, grad_wd, grad_wo], axis=2)  11.7 us
    concatenate x1, other arithmetic, per_device(): jnp.concatenate([grad_wu, grad_wd, grad_wo], axis=2)  8.78 us
  transfers between devices with their start and end apart: 41, of which 20 were waited for; matrix products, arithmetic and copies ran while one was open for 24% of the time, Pallas kernels for 4%

profile of v1, /device:TPU:0, one launch (start us, length us, event | category | flops | bytes accessed | tf_op | source)
XLA Modules:
  0.0 407.5 jit_solution(7031606337676573923)
XLA Ops:
  0.7 3.0 collective-permute-start.7
  5.3 2.6 collective-permute-start
  8.8 1.7 maximum_bitcast_fusion.16
  16.5 6.7 %collective-permute-start.1 = (bf16[2,96,576]{2,1,0:T(8,128)(2,1)S(1)}, bf16[2,96,576]{2,1,0:T(8,128)(2,1)S(1)}, u32[]{:S(2)}, u32[]{:S(2)}) collective-permute-start(bf16[2,96,576]{2,1,0:T(8,128)(2,1)S(1)} %maximum_bitcast_fusion.17), channel_id=1, source_target_pairs={{0,8},{4,12},{8,0},{12,4},{16,24},{20,28},{24,16},{28,20},{1,9},{5... | collective-permute-start | bytes 663560 | tf_op jit(solution)/shard_map/ppermute | solution.py:194
  23.2 11.6 %collective-permute-done.1 = bf16[2,96,576]{2,1,0:T(8,128)(2,1)S(1)} collective-permute-done((bf16[2,96,576]{2,1,0:T(8,128)(2,1)S(1)}, bf16[2,96,576]{2,1,0:T(8,128)(2,1)S(1)}, u32[]{:S(2)}, u32[]{:S(2)}) %collective-permute-start.1) | collective-permute-done | bytes 221216 | tf_op jit(solution)/shard_map/ppermute | solution.py:194
  35.0 1.6 collective-permute-start.4
  37.7 5.3 %collective-permute-done.4 = bf16[4,48,576]{2,1,0:T(8,128)(2,1)S(1)} collective-permute-done((bf16[4,48,576]{2,1,0:T(8,128)(2,1)S(1)}, bf16[4,48,576]{2,1,0:T(8,128)(2,1)S(1)}, u32[]{:S(2)}, u32[]{:S(2)}) %collective-permute-start.4) | collective-permute-done | bytes 221216 | tf_op jit(solution)/shard_map/ppermute | solution.py:194
  43.8 1.6 collective-permute-start.5
  45.4 6.6 %collective-permute-done.2 = bf16[4,48,576]{2,1,0:T(8,128)(2,1)S(1)} collective-permute-done((bf16[4,48,576]{2,1,0:T(8,128)(2,1)S(1)}, bf16[4,48,576]{2,1,0:T(8,128)(2,1)S(1)}, u32[]{:S(2)}, u32[]{:S(2)}) %collective-permute-start.2) | collective-permute-done | bytes 221216 | tf_op jit(solution)/shard_map/ppermute | solution.py:194
  52.1 1.6 collective-permute-start.3
  54.4 5.6 %collective-permute-done.10 = bf16[2,96,1728]{2,1,0:T(8,128)(2,1)S(1)} collective-permute-done((bf16[2,96,1728]{2,1,0:T(8,128)(2,1)S(1)}, bf16[2,96,1728]{2,1,0:T(8,128)(2,1)S(1)}, u32[]{:S(2)}, u32[]{:S(2)}) %collective-permute-start.10) | collective-permute-done | bytes 663584 | tf_op jit(solution)/shard_map/ppermute | solution.py:194
  60.3 1.6 collective-permute-start.13
  63.1 13.4 %collective-permute-done.13 = bf16[4,48,1728]{2,1,0:T(8,128)(2,1)S(1)} collective-permute-done((bf16[4,48,1728]{2,1,0:T(8,128)(2,1)S(1)}, bf16[4,48,1728]{2,1,0:T(8,128)(2,1)S(1)}, u32[]{:S(2)}, u32[]{:S(2)}) %collective-permute-start.13) | collective-permute-done | bytes 663584 | tf_op jit(solution)/shard_map/ppermute | solution.py:194
  78.1 13.9 %collective-permute-done.11 = bf16[4,48,1728]{2,1,0:T(8,128)(2,1)S(1)} collective-permute-done((bf16[4,48,1728]{2,1,0:T(8,128)(2,1)S(1)}, bf16[4,48,1728]{2,1,0:T(8,128)(2,1)S(1)}, u32[]{:S(2)}, u32[]{:S(2)}) %collective-permute-start.11) | collective-permute-done | bytes 663584 | tf_op jit(solution)/shard_map/ppermute | solution.py:194
  92.2 1.5 collective-permute-start.12
  93.7 1.6 fusion.37
  97.0 7.5 %fusion.64 = f32[2,384,2048]{2,1,0:T(8,128)} fusion(bf16[512,768]{1,0:T(8,128)(2,1)S(1)} %get-tuple-element.132, bf16[512,768]{1,0:T(8,128)(2,1)S(1)} %get-tuple-element.130, bf16[512,768]{1,0:T(8,128)(2,1)S(1)} %get-tuple-element.131, bf16[512,768]{1,0:T(8,128)(2,1)S(1)} %get-tuple-element.133, bf16[2,768,576]{2,1,0:T(8,128)(2,1)S(1)} %bitcast.270), kind=kOutput, calls=%fused_computation.125 | convolution fusion | flops 2428502016 | bytes 10616832 | tf_op jit(solution)/shard_map/sd,rdc->rcs/dot_general | solution.py:293
  104.6 16.9 %attn_fwd.1 = (bf16[2,3,64,1024]{3,2,1,0:T(8,128)(2,1)S(1)}, f32[2,3,1,1024]{3,2,1,0:T(1,128)S(1)}) custom-call(s32[2]{0:T(128)S(1)} %convert_reduce_fusion.5.n_ref, s32[16]{0:T(128)S(1)} %reshape.294.l_ref, f32[2,3,64,1024]{3,2,1,0:T(8,128)S(1)} %bitcast.237, f32[2,2,3,64,2048]{4,3,2,1,0:T(8,128)} %bitcast.241, f32[2,2,3,64,2048]{4,3,2,1,0:T(8,128)} %bitcast.242, ...), custom_call_target="tpu_custom_call" | custom-call | tf_op jit(solution)/shard_map/attn_fwd/pallas_call | solution.py:66
  122.1 2.3 collective-permute-done.14
  124.4 2.9 maximum_maximum_fusion
  129.0 2.3 collective-permute-done.15
  132.9 1.8 collective-permute-done.16
  134.6 2.8 fusion.57
  137.5 5.5 %multiply_convert_fusion.1 = bf16[1024,2,768]{2,0,1:T(8,128)(2,1)S(1)} fusion(f32[1024,2,768]{2,0,1:T(8,128)S(1)} %get-tuple-element.139, u8[1024,768]{1,0:T(8,128)(4,1)S(1)} %get-tuple-element.138), kind=kLoop, calls=%fused_computation.8 | loop fusion | flops 40894464 | bytes 10223616 | tf_op jit(solution)/shard_map/convert_element_type | solution.py:328
  143.0 8.5 %multiply_convert_fusion = bf16[1024,2,768]{2,0,1:T(8,128)(2,1)S(1)} fusion(f32[1024,2,768]{2,0,1:T(8,128)S(1)} %get-tuple-element.139, bf16[2,768,1728]{2,1,0:T(8,128)(2,1)S(1)} %bitcast.259, bf16[512,768]{1,0:T(8,128)(2,1)S(1)} %collective-permute-done.18, bf16[512,768]{1,0:T(8,128)(2,1)S(1)} %bitcast.280, u8[1024,768]{1,0:T(8,128)(4,1)S(1)} %get-tuple-element.138), kind=kOutput, calls=%fused_computation.6 | convolution fusion | flops 2467823616 | bytes 14155776 | tf_op jit(solution)/shard_map/sd,rdf->srf/dot_general | solution.py:293
  151.6 2.6 fusion.13
  155.4 2.6 fusion.16
  160.3 2.6 multiply_reduce_fusion
  163.0 3.7 fusion.103
  167.3 4.4 %convolution_bitcast_fusion = f32[2,768,768]{1,2,0:T(8,128)} fusion(bf16[1024,2,768]{2,0,1:T(8,128)(2,1)S(1)} %copy-done.22, bf16[512,768]{1,0:T(8,128)(2,1)S(1)} %copy-done.58, bf16[512,768]{1,0:T(8,128)(2,1)S(1)} %bitcast.281), kind=kOutput, calls=%fused_computation.25 | convolution fusion | flops 2419064832 | bytes 9437184 | tf_op jit(solution)/shard_map/sd,srf->rdf/dot_general | solution.py:293
  171.7 4.4 %convolution_bitcast_fusion.1 = f32[2,768,768]{1,2,0:T(8,128)} fusion(bf16[1024,2,768]{2,0,1:T(8,128)(2,1)S(1)} %copy-done.63, bf16[512,768]{1,0:T(8,128)(2,1)S(1)} %copy-done.56, bf16[512,768]{1,0:T(8,128)(2,1)S(1)} %copy-done.41), kind=kOutput, calls=%fused_computation.26 | convolution fusion | flops 2419064832 | bytes 9437184 | tf_op jit(solution)/shard_map/sd,srf->rdf/dot_general | solution.py:293
  176.1 3.4 convolution_convert_fusion
  179.6 30.1 %attn_bwd.1 = (bf16[2,3,64,1024]{3,2,1,0:T(8,128)(2,1)}, bf16[2,2,3,64,2048]{4,3,2,1,0:T(8,128)(2,1)}, f32[64,1]{1,0:T(8,128)}, f32[64,1]{1,0:T(8,128)}) custom-call(s32[2]{0:T(128)} %copy-done.9, s32[16]{0:T(128)} %copy-done.8, f32[2,3,64,1024]{3,2,1,0:T(8,128)} %bitcast.238, f32[2,2,3,64,2048]{4,3,2,1,0:T(8,128)} %bitcast.243, ...), custom_call_target="tpu_custom_call" | custom-call | tf_op jit(solution)/shard_map/attn_bwd/pallas_call | solution.py:155
  209.7 2.8 slice.233
  212.6 4.7 %convolution_bitcast_fusion.2 = f32[1024,768]{1,0:T(8,128)} fusion(bf16[2,384,2048]{2,1,0:T(8,128)(2,1)} %bitcast.277, bf16[2,768,576]{2,1,0:T(8,128)(2,1)S(1)} %bitcast.271), kind=kOutput, calls=%fused_computation.44 | convolution fusion | flops 1207959552 | bytes 5898240 | tf_op jit(solution)/shard_map/rcs,rdc->sd/dot_general | solution.py:293
  217.3 2.6 convolution_bitcast_fusion.4
  220.7 2.0 pad_maximum_fusion.1
  222.7 5.5 %copy.108 = f32[2,768,576]{2,1,0:T(8,128)} copy(f32[2,768,576]{1,2,0:T(8,128)} %pad_maximum_fusion.1) | data formatting | bytes 7077888 | tf_op jit(solution)/shard_map/concatenate | solution.py:355
  228.3 2.2 fusion.79
  230.5 3.0 slice.241
  233.5 2.4 fusion.19
  235.8 1.6 copy-done.26
  238.5 2.4 slice.370
  241.9 2.1 fusion.78
  243.9 12.2 %collective-permute-start.29 = (bf16[2,4,48,576]{3,2,1,0:T(8,128)(2,1)}, bf16[2,4,48,576]{3,2,1,0:T(8,128)(2,1)}, u32[]{:S(2)}, u32[]{:S(2)}) collective-permute-start(bf16[2,4,48,576]{3,2,1,0:T(8,128)(2,1)} %fusion.78), channel_id=1, source_target_pairs={{0,4},{4,0},{8,12},{12,8},{16,20},{20,16},{24,28},{28,24},{1,5},{5... | collective-permute-start | bytes 1327112 | tf_op jit(solution)/shard_map/ppermute | solution.py:194
  256.1 2.1 convolution_bitcast_fusion.5
  258.3 8.8 %pad_maximum_fusion = f32[2,768,1728]{1,2,0:T(8,128)} fusion(f32[2,768,192]{1,2,0:T(8,128)S(1)} %convolution_bitcast_fusion.5, f32[2,768,768]{1,2,0:T(8,128)} %convolution_bitcast_fusion, f32[2,768,768]{1,2,0:T(8,128)} %convolution_bitcast_fusion.1), kind=kLoop, calls=%fused_computation | loop fusion | flops 5308416 | bytes 21233664 | tf_op jit(solution)/shard_map/concatenate | solution.py:341
  267.1 11.7 %copy.111 = f32[2,768,1728]{2,1,0:T(8,128)} copy(f32[2,768,1728]{1,2,0:T(8,128)} %pad_maximum_fusion) | data formatting | bytes 21233664 | tf_op jit(solution)/shard_map/concatenate | solution.py:341
  278.8 2.9 slice.251
  281.7 2.1 fusion.62
  283.9 2.0 collective-permute-start.37
  288.6 5.9 %collective-permute-done.32 = bf16[4,48,576]{2,1,0:T(8,128)(2,1)S(1)} collective-permute-done((bf16[4,48,576]{2,1,0:T(8,128)(2,1)S(1)}, bf16[4,48,576]{2,1,0:T(8,128)(2,1)S(1)}, u32[]{:S(2)}, u32[]{:S(2)}) %collective-permute-start.32) | collective-permute-done | bytes 221216 | tf_op jit(solution)/shard_map/ppermute | solution.py:194
  294.6 26.6 %collective-permute-done.30 = bf16[4,48,576]{2,1,0:T(8,128)(2,1)S(1)} collective-permute-done((bf16[4,48,576]{2,1,0:T(8,128)(2,1)S(1)}, bf16[4,48,576]{2,1,0:T(8,128)(2,1)S(1)}, u32[]{:S(2)}, u32[]{:S(2)}) %collective-permute-start.30) | collective-permute-done | bytes 221216 | tf_op jit(solution)/shard_map/ppermute | solution.py:194
  321.9 6.4 %collective-permute-done.33 = bf16[2,96,576]{2,1,0:T(8,128)(2,1)S(1)} collective-permute-done((bf16[2,96,576]{2,1,0:T(8,128)(2,1)S(1)}, bf16[2,96,576]{2,1,0:T(8,128)(2,1)S(1)}, u32[]{:S(2)}, u32[]{:S(2)}) %collective-permute-start.33) | collective-permute-done | bytes 221216 | tf_op jit(solution)/shard_map/ppermute | solution.py:194
  328.4 1.6 fusion.82
  331.5 3.7 collective-permute-done.34
  335.3 2.1 fusion.1
  339.3 15.4 %collective-permute-done.35 = bf16[2,4,48,1728]{3,2,1,0:T(8,128)(2,1)S(1)} collective-permute-done((bf16[2,4,48,1728]{3,2,1,0:T(8,128)(2,1)S(1)}, bf16[2,4,48,1728]{3,2,1,0:T(8,128)(2,1)S(1)}, u32[]{:S(2)}, u32[]{:S(2)}) %collective-permute-start.35) | collective-permute-done | bytes 1327136 | tf_op jit(solution)/shard_map/ppermute | solution.py:194
  356.0 1.7 collective-permute-start.36
  358.6 2.1 fusion.81
  364.0 6.1 %collective-permute-done.25 = f32[5,768]{1,0:T(8,128)S(1)} collective-permute-done((f32[5,768]{1,0:T(8,128)S(1)}, f32[5,768]{1,0:T(8,128)S(1)}, u32[]{:S(2)}, u32[]{:S(2)}) %collective-permute-start.25) | collective-permute-done | bytes 15392 | tf_op jit(solution)/shard_map/ppermute | solution.py:194
  376.3 11.6 %collective-permute-done.27 = f32[5,768]{1,0:T(8,128)S(1)} collective-permute-done((f32[5,768]{1,0:T(8,128)S(1)}, f32[5,768]{1,0:T(8,128)S(1)}, u32[]{:S(2)}, u32[]{:S(2)}) %collective-permute-start.27) | collective-permute-done | bytes 15392 | tf_op jit(solution)/shard_map/ppermute | solution.py:194
  389.4 5.3 %collective-permute-done.28 = f32[5,768]{1,0:T(8,128)S(1)} collective-permute-done((f32[5,768]{1,0:T(8,128)S(1)}, f32[5,768]{1,0:T(8,128)S(1)}, u32[]{:S(2)}, u32[]{:S(2)}) %collective-permute-start.28) | collective-permute-done | bytes 15392 | tf_op jit(solution)/shard_map/ppermute | solution.py:194
  396.2 9.4 %collective-permute-done.40 = bf16[1,96,1728]{2,1,0:T(8,128)(2,1)S(1)} collective-permute-done((bf16[1,96,1728]{2,1,0:T(8,128)(2,1)S(1)}, bf16[1,96,1728]{2,1,0:T(8,128)(2,1)S(1)}, u32[]{:S(2)}, u32[]{:S(2)}) %collective-permute-start.40) | collective-permute-done | bytes 331808 | tf_op jit(solution)/shard_map/ppermute | solution.py:194
  (308 shorter events, 50.0 us)
Async XLA Ops:
  0.6 12.3 %copy-start.10 = (bf16[1,512,768]{2,1,0:T(8,128)(2,1)S(1)}, bf16[1,512,768]{2,1,0:T(8,128)(2,1)}, u32[]{:S(2)}) copy-start(bf16[1,512,768]{2,1,0:T(8,128)(2,1)} %param.13) | copy-start | bytes 2359300
  0.7 15.3 %copy-start.53 = (f32[64]{0:T(128)S(1)}, f32[64]{0:T(128)}, u32[]{:S(2)}) copy-start(f32[64]{0:T(128)} %param.18) | copy-start | bytes 772
  0.7 15.4 %copy-start.54 = (f32[64]{0:T(128)S(1)}, f32[64]{0:T(128)}, u32[]{:S(2)}) copy-start(f32[64]{0:T(128)} %param.19) | copy-start | bytes 772
  0.7 53.0 %collective-permute-start.7 = (bf16[512,768]{1,0:T(8,128)(2,1)}, bf16[512,768]{1,0:T(8,128)(2,1)S(1)}, u32[]{:S(2)}, u32[]{:S(2)}) collective-permute-start(bf16[512,768]{1,0:T(8,128)(2,1)} %bitcast.248), channel_id=1, source_target_pairs={{0,2},{1,3},{2,0},{3,1},{4,6},{5,7},{6,4},{7,5},{8,10},{9,11},{10,... | collective-permute-start | bytes 2359304 | tf_op jit(solution)/shard_map/ppermute | solution.py:194
  3.7 50.2 %collective-permute-start.6 = (bf16[512,768]{1,0:T(8,128)(2,1)}, bf16[512,768]{1,0:T(8,128)(2,1)S(1)}, u32[]{:S(2)}, u32[]{:S(2)}) collective-permute-start(bf16[512,768]{1,0:T(8,128)(2,1)} %bitcast.249), channel_id=1, source_target_pairs={{0,1},{1,0},{2,3},{3,2},{4,5},{5,4},{6,7},{7,6},{8,9},{9,8},{10,11... | collective-permute-start | bytes 2359304 | tf_op jit(solution)/shard_map/ppermute | solution.py:194
  5.3 11.0 %collective-permute-start = (bf16[1,96,576]{2,1,0:T(8,128)(2,1)}, bf16[1,96,576]{2,1,0:T(8,128)(2,1)S(1)}, u32[]{:S(2)}, u32[]{:S(2)}) collective-permute-start(bf16[1,96,576]{2,1,0:T(8,128)(2,1)} %maximum_bitcast_fusion.18), channel_id=1, source_target_pairs={{0,16},{4,20},{8,24},{12,28},{16,0},{20,4},{24,8},{28,12},{1,17},{... | collective-permute-start | bytes 331784 | tf_op jit(solution)/shard_map/ppermute | solution.py:194
  10.5 26.0 %collective-permute-start.9 = (bf16[1,96,1728]{2,1,0:T(8,128)(2,1)}, bf16[1,96,1728]{2,1,0:T(8,128)(2,1)}, u32[]{:S(2)}, u32[]{:S(2)}) collective-permute-start(bf16[1,96,1728]{2,1,0:T(8,128)(2,1)} %maximum_bitcast_fusion.16), channel_id=1, source_target_pairs={{0,16},{4,20},{8,24},{12,28},{16,0},{20,4},{24,8},{28,12},{1,17},{... | collective-permute-start | bytes 995336 | tf_op jit(solution)/shard_map/ppermute | solution.py:194
  15.3 89.3 %copy-start.8 = (s32[16]{0:T(128)}, s32[16]{0:T(128)S(1)}, u32[]{:S(2)}) copy-start(s32[16]{0:T(128)S(1)} %reshape.294.l_ref) | copy-start | bytes 196
  15.3 21.3 %copy-start.45 = (bf16[768,96]{0,1:T(8,128)(2,1)S(1)}, bf16[768,96]{0,1:T(8,128)(2,1)}, u32[]{:S(2)}) copy-start(bf16[768,96]{0,1:T(8,128)(2,1)} %param.24) | copy-start | bytes 442372
  15.3 21.3 %copy-start.46 = (bf16[96,768]{1,0:T(8,128)(2,1)S(1)}, bf16[96,768]{1,0:T(8,128)(2,1)}, u32[]{:S(2)}) copy-start(bf16[96,768]{1,0:T(8,128)(2,1)} %param.23) | copy-start | bytes 442372
  15.8 88.8 %copy-start.4 = (bf16[64,1024]{1,0:T(8,128)(2,1)}, bf16[64,1024]{1,0:T(8,128)(2,1)S(1)}, u32[]{:S(2)}) copy-start(bf16[64,1024]{1,0:T(8,128)(2,1)S(1)} %select_convert_fusion.1.fq_ref) | copy-start | bytes 393220
  16.0 88.6 %copy-start.3 = (bf16[64,2048]{1,0:T(8,128)(2,1)}, bf16[64,2048]{1,0:T(8,128)(2,1)S(1)}, u32[]{:S(2)}) copy-start(bf16[64,2048]{1,0:T(8,128)(2,1)S(1)} %select_convert_fusion.fk_ref) | copy-start | bytes 786436
  16.1 88.5 %copy-start.5 = (f32[64,1]{1,0:T(8,128)}, f32[64,1]{1,0:T(8,128)S(1)}, u32[]{:S(2)}) copy-start(f32[64,1]{1,0:T(8,128)S(1)} %copy.96.qg_ref) | copy-start | bytes 772
  16.2 88.4 %copy-start.6 = (f32[64,1]{1,0:T(8,128)}, f32[64,1]{1,0:T(8,128)S(1)}, u32[]{:S(2)}) copy-start(f32[64,1]{1,0:T(8,128)S(1)} %copy.97.kg_ref) | copy-start | bytes 772
  16.3 88.3 %copy-start.9 = (s32[2]{0:T(128)}, s32[2]{0:T(128)S(1)}, u32[]{:S(2)}) copy-start(s32[2]{0:T(128)S(1)} %convert_reduce_fusion.5.n_ref) | copy-start | bytes 28
  16.5 18.3 %collective-permute-start.1 = (bf16[2,96,576]{2,1,0:T(8,128)(2,1)S(1)}, bf16[2,96,576]{2,1,0:T(8,128)(2,1)S(1)}, u32[]{:S(2)}, u32[]{:S(2)}) collective-permute-start(bf16[2,96,576]{2,1,0:T(8,128)(2,1)S(1)} %maximum_bitcast_fusion.17), channel_id=1, source_target_pairs={{0,8},{4,12},{8,0},{12,4},{16,24},{20,28},{24,16},{28,20},{1,9},{5... | collective-permute-start | bytes 663560 | tf_op jit(solution)/shard_map/ppermute | solution.py:194
  35.0 8.0 %collective-permute-start.4 = (bf16[4,48,576]{2,1,0:T(8,128)(2,1)S(1)}, bf16[4,48,576]{2,1,0:T(8,128)(2,1)S(1)}, u32[]{:S(2)}, u32[]{:S(2)}) collective-permute-start(bf16[4,48,576]{2,1,0:T(8,128)(2,1)S(1)} %slice.218), channel_id=1, source_target_pairs={{0,4},{4,0},{8,12},{12,8},{16,20},{20,16},{24,28},{28,24},{1,5},{5... | collective-permute-start | bytes 663560 | tf_op jit(solution)/shard_map/ppermute | solution.py:194
  43.0 9.0 %collective-permute-start.2 = (bf16[4,48,576]{2,1,0:T(8,128)(2,1)S(1)}, bf16[4,48,576]{2,1,0:T(8,128)(2,1)S(1)}, u32[]{:S(2)}, u32[]{:S(2)}) collective-permute-start(bf16[4,48,576]{2,1,0:T(8,128)(2,1)S(1)} %get-tuple-element.115), channel_id=1, source_target_pairs={{0,2},{1,3},{2,0},{3,1},{4,6},{5,7},{6,4},{7,5},{8,10},{9,11},{10,... | collective-permute-start | bytes 663560 | tf_op jit(solution)/shard_map/ppermute | solution.py:194
  43.6 16.3 %collective-permute-start.10 = (bf16[2,96,1728]{2,1,0:T(8,128)(2,1)S(1)}, bf16[2,96,1728]{2,1,0:T(8,128)(2,1)S(1)}, u32[]{:S(2)}, u32[]{:S(2)}) collective-permute-start(bf16[2,96,1728]{2,1,0:T(8,128)(2,1)S(1)} %maximum_bitcast_fusion.15), channel_id=1, source_target_pairs={{0,8},{4,12},{8,0},{12,4},{16,24},{20,28},{24,16},{28,20},{1,9},{5... | collective-permute-start | bytes 1990664 | tf_op jit(solution)/shard_map/ppermute | solution.py:194
  43.8 18.8 %collective-permute-start.5 = (bf16[4,2,48,576]{3,2,0,1:T(8,128)(2,1)S(1)}, bf16[4,2,48,576]{3,2,0,1:T(8,128)(2,1)S(1)}, u32[]{:S(2)}, u32[]{:S(2)}) collective-permute-start(bf16[4,2,48,576]{3,2,0,1:T(8,128)(2,1)S(1)} %get-tuple-element.117), channel_id=1, source_target_pairs={{0,2},{1,3},{2,0},{3,1},{4,6},{5,7},{6,4},{7,5},{8,10},{9,11},{10,... | collective-permute-start | bytes 1327112 | tf_op jit(solution)/shard_map/ppermute | solution.py:194
  52.1 10.4 %collective-permute-start.3 = (bf16[2,4,48,576]{3,2,1,0:T(8,128)(2,1)S(1)}, bf16[2,4,48,576]{3,2,1,0:T(8,128)(2,1)S(1)}, u32[]{:S(2)}, u32[]{:S(2)}) collective-permute-start(bf16[2,4,48,576]{3,2,1,0:T(8,128)(2,1)S(1)} %pad_maximum_fusion.8), channel_id=1, source_target_pairs={{0,4},{4,0},{8,12},{12,8},{16,20},{20,16},{24,28},{28,24},{1,5},{5... | collective-permute-start | bytes 1327112 | tf_op jit(solution)/shard_map/ppermute | solution.py:194
  53.6 40.0 %copy-start.11 = (bf16[512,768]{1,0:T(8,128)(2,1)}, bf16[512,768]{1,0:T(8,128)(2,1)S(1)}, u32[]{:S(2)}) copy-start(bf16[512,768]{1,0:T(8,128)(2,1)S(1)} %collective-permute-done.7) | copy-start | bytes 2359300
  53.6 23.9 %collective-permute-start.8 = (bf16[512,768]{1,0:T(8,128)(2,1)S(1)}, bf16[512,768]{1,0:T(8,128)(2,1)S(1)}, u32[]{:S(2)}, u32[]{:S(2)}) collective-permute-start(bf16[512,768]{1,0:T(8,128)(2,1)S(1)} %collective-permute-done.7), channel_id=1, source_target_pairs={{0,1},{1,0},{2,3},{3,2},{4,5},{5,4},{6,7},{7,6},{8,9},{9,8},{10,11... | collective-permute-start | bytes 2359304 | tf_op jit(solution)/shard_map/ppermute | solution.py:194
  60.3 16.2 %collective-permute-start.13 = (bf16[4,48,1728]{2,1,0:T(8,128)(2,1)S(1)}, bf16[4,48,1728]{2,1,0:T(8,128)(2,1)S(1)}, u32[]{:S(2)}, u32[]{:S(2)}) collective-permute-start(bf16[4,48,1728]{2,1,0:T(8,128)(2,1)S(1)} %slice.223), channel_id=1, source_target_pairs={{0,4},{4,0},{8,12},{12,8},{16,20},{20,16},{24,28},{28,24},{1,5},{5... | collective-permute-start | bytes 1990664 | tf_op jit(solution)/shard_map/ppermute | solution.py:194
  63.1 33.9 %copy-start.23 = (bf16[2,4,2,96,576]{4,3,2,1,0:T(8,128)(2,1)}, bf16[2,4,2,96,576]{4,3,2,1,0:T(8,128)(2,1)S(1)}, u32[]{:S(2)}) copy-start(bf16[2,4,2,96,576]{4,3,2,1,0:T(8,128)(2,1)S(1)} %copy.93) | copy-start | bytes 5308420
  76.7 17.0 %copy-start.50 = (f32[768]{0:T(1024)S(1)}, f32[768]{0:T(1024)}, u32[]{:S(2)}) copy-start(f32[768]{0:T(1024)} %param.15) | copy-start | bytes 9220
  76.7 17.0 %copy-start.51 = (f32[768]{0:T(1024)S(1)}, f32[768]{0:T(1024)}, u32[]{:S(2)}) copy-start(f32[768]{0:T(1024)} %param.16) | copy-start | bytes 9220
  76.7 15.3 %collective-permute-start.11 = (bf16[4,48,1728]{2,1,0:T(8,128)(2,1)S(1)}, bf16[4,48,1728]{2,1,0:T(8,128)(2,1)S(1)}, u32[]{:S(2)}, u32[]{:S(2)}) collective-permute-start(bf16[4,48,1728]{2,1,0:T(8,128)(2,1)S(1)} %get-tuple-element.101), channel_id=1, source_target_pairs={{0,2},{1,3},{2,0},{3,1},{4,6},{5,7},{6,4},{7,5},{8,10},{9,11},{10,... | collective-permute-start | bytes 1990664 | tf_op jit(solution)/shard_map/ppermute | solution.py:194
  92.2 29.4 %collective-permute-start.12 = (bf16[2,4,48,1728]{3,2,1,0:T(8,128)(2,1)S(1)}, bf16[2,4,48,1728]{3,2,1,0:T(8,128)(2,1)S(1)}, u32[]{:S(2)}, u32[]{:S(2)}) collective-permute-start(bf16[2,4,48,1728]{3,2,1,0:T(8,128)(2,1)S(1)} %pad_maximum_fusion.4), channel_id=1, source_target_pairs={{0,4},{4,0},{8,12},{12,8},{16,20},{20,16},{24,28},{28,24},{1,5},{5... | collective-permute-start | bytes 3981320 | tf_op jit(solution)/shard_map/ppermute | solution.py:194
  95.5 28.9 %collective-permute-start.14 = (bf16[4,2,48,1728]{3,2,0,1:T(8,128)(2,1)S(1)}, bf16[4,2,48,1728]{3,2,0,1:T(8,128)(2,1)}, u32[]{:S(2)}, u32[]{:S(2)}) collective-permute-start(bf16[4,2,48,1728]{3,2,0,1:T(8,128)(2,1)S(1)} %get-tuple-element.103), channel_id=1, source_target_pairs={{0,2},{1,3},{2,0},{3,1},{4,6},{5,7},{6,4},{7,5},{8,10},{9,11},{10,... | collective-permute-start | bytes 3981320 | tf_op jit(solution)/shard_map/ppermute | solution.py:194
  127.7 27.7 %copy-start.16 = (bf16[2,4,2,96,1728]{4,3,2,1,0:T(8,128)(2,1)}, bf16[2,4,2,96,1728]{4,3,2,1,0:T(8,128)(2,1)S(1)}, u32[]{:S(2)}) copy-start(bf16[2,4,2,96,1728]{4,3,2,1,0:T(8,128)(2,1)S(1)} %copy.101) | copy-start | bytes 15925252
  128.9 2.4 collective-permute-start.15
  132.3 2.4 collective-permute-start.16
  132.7 10.3 %collective-permute-start.18 = (bf16[512,768]{1,0:T(8,128)(2,1)S(1)}, bf16[512,768]{1,0:T(8,128)(2,1)S(1)}, u32[]{:S(2)}, u32[]{:S(2)}) collective-permute-start(bf16[512,768]{1,0:T(8,128)(2,1)S(1)} %bitcast.279), channel_id=1, source_target_pairs={{0,1},{1,0},{2,3},{3,2},{4,5},{5,4},{6,7},{7,6},{8,9},{9,8},{10,11... | collective-permute-start | bytes 2359304 | tf_op jit(solution)/shard_map/ppermute | solution.py:194
  143.0 12.4 %copy-start.21 = (bf16[1024,2,768]{2,0,1:T(8,128)(2,1)}, bf16[1024,2,768]{2,0,1:T(8,128)(2,1)S(1)}, u32[]{:S(2)}) copy-start(bf16[1024,2,768]{2,0,1:T(8,128)(2,1)S(1)} %multiply_convert_fusion.1) | copy-start | bytes 9437188
  143.0 8.6 %copy-start.57 = (bf16[512,768]{1,0:T(8,128)(2,1)}, bf16[512,768]{1,0:T(8,128)(2,1)S(1)}, u32[]{:S(2)}) copy-start(bf16[512,768]{1,0:T(8,128)(2,1)S(1)} %collective-permute-done.18) | copy-start | bytes 2359300
  155.3 5.1 %collective-permute-start.19 = (bf16[512,768]{1,0:T(8,128)(2,1)}, bf16[512,768]{1,0:T(8,128)(2,1)}, u32[]{:S(2)}, u32[]{:S(2)}) collective-permute-start(bf16[512,768]{1,0:T(8,128)(2,1)} %slice.372), channel_id=1, source_target_pairs={{0,1},{1,0},{2,3},{3,2},{4,5},{5,4},{6,7},{7,6},{8,9},{9,8},{10,11... | collective-permute-start | bytes 2359304 | tf_op jit(solution)/shard_map/ppermute | solution.py:194
  159.9 3.0 collective-permute-start.17
  166.7 9.4 %copy-start.44 = (bf16[512,768]{1,0:T(8,128)(2,1)}, bf16[512,768]{1,0:T(8,128)(2,1)S(1)}, u32[]{:S(2)}) copy-start(bf16[512,768]{1,0:T(8,128)(2,1)S(1)} %get-tuple-element.87) | copy-start | bytes 2359300
  166.7 9.4 %collective-permute-start.20 = (bf16[512,768]{1,0:T(8,128)(2,1)S(1)}, bf16[512,768]{1,0:T(8,128)(2,1)S(1)}, u32[]{:S(2)}, u32[]{:S(2)}) collective-permute-start(bf16[512,768]{1,0:T(8,128)(2,1)S(1)} %get-tuple-element.87), channel_id=1, source_target_pairs={{0,1},{1,0},{2,3},{3,2},{4,5},{5,4},{6,7},{7,6},{8,9},{9,8},{10,11... | collective-permute-start | bytes 2359304 | tf_op jit(solution)/shard_map/ppermute | solution.py:194
  237.4 18.7 %copy-start.2 = (bf16[2,3,64,1024]{3,2,1,0:T(8,128)(2,1)S(1)}, bf16[2,3,64,1024]{3,2,1,0:T(8,128)(2,1)}, u32[]{:S(2)}) copy-start(bf16[2,3,64,1024]{3,2,1,0:T(8,128)(2,1)} %copy-done.1) | copy-start | bytes 2359300
  238.4 119.3 %collective-permute-start.21 = (bf16[512,768]{1,0:T(8,128)(2,1)}, bf16[512,768]{1,0:T(8,128)(2,1)S(1)}, u32[]{:S(2)}, u32[]{:S(2)}) collective-permute-start(bf16[512,768]{1,0:T(8,128)(2,1)} %slice.371), channel_id=1, source_target_pairs={{0,1},{1,0},{2,3},{3,2},{4,5},{5,4},{6,7},{7,6},{8,9},{9,8},{10,11... | collective-permute-start | bytes 2359304 | tf_op jit(solution)/shard_map/ppermute | solution.py:194
  240.9 87.5 %collective-permute-start.22 = (bf16[512,768]{1,0:T(8,128)(2,1)}, bf16[512,768]{1,0:T(8,128)(2,1)}, u32[]{:S(2)}, u32[]{:S(2)}) collective-permute-start(bf16[512,768]{1,0:T(8,128)(2,1)} %slice.370), channel_id=1, source_target_pairs={{0,1},{1,0},{2,3},{3,2},{4,5},{5,4},{6,7},{7,6},{8,9},{9,8},{10,11... | collective-permute-start | bytes 2359304 | tf_op jit(solution)/shard_map/ppermute | solution.py:194
  241.5 44.4 %collective-permute-start.31 = (bf16[4,2,48,576]{3,2,1,0:T(8,128)(2,1)}, bf16[4,2,48,576]{3,2,1,0:T(8,128)(2,1)S(1)}, u32[]{:S(2)}, u32[]{:S(2)}) collective-permute-start(bf16[4,2,48,576]{3,2,1,0:T(8,128)(2,1)} %fusion.79), channel_id=1, source_target_pairs={{0,2},{1,3},{2,0},{3,1},{4,6},{5,7},{6,4},{7,5},{8,10},{9,11},{10,... | collective-permute-start | bytes 1327112 | tf_op jit(solution)/shard_map/ppermute | solution.py:194
  243.9 43.4 %collective-permute-start.29 = (bf16[2,4,48,576]{3,2,1,0:T(8,128)(2,1)}, bf16[2,4,48,576]{3,2,1,0:T(8,128)(2,1)}, u32[]{:S(2)}, u32[]{:S(2)}) collective-permute-start(bf16[2,4,48,576]{3,2,1,0:T(8,128)(2,1)} %fusion.78), channel_id=1, source_target_pairs={{0,4},{4,0},{8,12},{12,8},{16,20},{20,16},{24,28},{28,24},{1,5},{5... | collective-permute-start | bytes 1327112 | tf_op jit(solution)/shard_map/ppermute | solution.py:194
  283.9 51.4 %collective-permute-start.37 = (bf16[4,2,48,1728]{3,2,1,0:T(8,128)(2,1)S(1)}, bf16[4,2,48,1728]{3,2,1,0:T(8,128)(2,1)S(1)}, u32[]{:S(2)}, u32[]{:S(2)}) collective-permute-start(bf16[4,2,48,1728]{3,2,1,0:T(8,128)(2,1)S(1)} %fusion.62), channel_id=1, source_target_pairs={{0,2},{1,3},{2,0},{3,1},{4,6},{5,7},{6,4},{7,5},{8,10},{9,11},{10,... | collective-permute-start | bytes 3981320 | tf_op jit(solution)/shard_map/ppermute | solution.py:194
  287.3 7.2 %collective-permute-start.32 = (bf16[4,48,576]{2,1,0:T(8,128)(2,1)S(1)}, bf16[4,48,576]{2,1,0:T(8,128)(2,1)S(1)}, u32[]{:S(2)}, u32[]{:S(2)}) collective-permute-start(bf16[4,48,576]{2,1,0:T(8,128)(2,1)S(1)} %fusion.84), channel_id=1, source_target_pairs={{0,4},{4,0},{8,12},{12,8},{16,20},{20,16},{24,28},{28,24},{1,5},{5... | collective-permute-start | bytes 663560 | tf_op jit(solution)/shard_map/ppermute | solution.py:194
  288.6 32.6 %collective-permute-start.30 = (bf16[4,48,576]{2,1,0:T(8,128)(2,1)S(1)}, bf16[4,48,576]{2,1,0:T(8,128)(2,1)S(1)}, u32[]{:S(2)}, u32[]{:S(2)}) collective-permute-start(bf16[4,48,576]{2,1,0:T(8,128)(2,1)S(1)} %fusion.86), channel_id=1, source_target_pairs={{0,2},{1,3},{2,0},{3,1},{4,6},{5,7},{6,4},{7,5},{8,10},{9,11},{10,... | collective-permute-start | bytes 663560 | tf_op jit(solution)/shard_map/ppermute | solution.py:194
  321.3 6.9 %collective-permute-start.33 = (bf16[2,96,576]{2,1,0:T(8,128)(2,1)S(1)}, bf16[2,96,576]{2,1,0:T(8,128)(2,1)S(1)}, u32[]{:S(2)}, u32[]{:S(2)}) collective-permute-start(bf16[2,96,576]{2,1,0:T(8,128)(2,1)S(1)} %fusion.85), channel_id=1, source_target_pairs={{0,8},{4,12},{8,0},{12,4},{16,24},{20,28},{24,16},{28,20},{1,9},{5... | collective-permute-start | bytes 663560 | tf_op jit(solution)/shard_map/ppermute | solution.py:194
  321.5 33.2 %collective-permute-start.35 = (bf16[2,4,48,1728]{3,2,1,0:T(8,128)(2,1)S(1)}, bf16[2,4,48,1728]{3,2,1,0:T(8,128)(2,1)S(1)}, u32[]{:S(2)}, u32[]{:S(2)}) collective-permute-start(bf16[2,4,48,1728]{3,2,1,0:T(8,128)(2,1)S(1)} %fusion.61), channel_id=1, source_target_pairs={{0,4},{4,0},{8,12},{12,8},{16,20},{20,16},{24,28},{28,24},{1,5},{5... | collective-permute-start | bytes 3981320 | tf_op jit(solution)/shard_map/ppermute | solution.py:194
  328.3 6.9 %collective-permute-start.34 = (bf16[1,96,576]{2,1,0:T(8,128)(2,1)S(1)}, bf16[1,96,576]{2,1,0:T(8,128)(2,1)S(1)}, u32[]{:S(2)}, u32[]{:S(2)}) collective-permute-start(bf16[1,96,576]{2,1,0:T(8,128)(2,1)S(1)} %dynamic-slice_convert_fusion.7), channel_id=1, source_target_pairs={{0,16},{4,20},{8,24},{12,28},{16,0},{20,4},{24,8},{28,12},{1,17},{... | collective-permute-start | bytes 331784 | tf_op jit(solution)/shard_map/ppermute | solution.py:194
  330.1 28.5 %collective-permute-start.23 = (bf16[512,768]{1,0:T(8,128)(2,1)S(1)}, bf16[512,768]{1,0:T(8,128)(2,1)S(1)}, u32[]{:S(2)}, u32[]{:S(2)}) collective-permute-start(bf16[512,768]{1,0:T(8,128)(2,1)S(1)} %get-tuple-element.94), channel_id=1, source_target_pairs={{0,2},{1,3},{2,0},{3,1},{4,6},{5,7},{6,4},{7,5},{8,10},{9,11},{10,... | collective-permute-start | bytes 2359304 | tf_op jit(solution)/shard_map/ppermute | solution.py:194
  337.4 17.7 %copy-start.13 = (f32[4,2,48,1728]{3,2,1,0:T(8,128)}, f32[4,2,48,1728]{3,2,1,0:T(8,128)S(1)}, u32[]{:S(2)}) copy-start(f32[4,2,48,1728]{3,2,1,0:T(8,128)S(1)} %fusion.1) | copy-start | bytes 7962628
  338.4 32.7 %collective-permute-start.38 = (bf16[4,48,1728]{2,1,0:T(8,128)(2,1)}, bf16[4,48,1728]{2,1,0:T(8,128)(2,1)S(1)}, u32[]{:S(2)}, u32[]{:S(2)}) collective-permute-start(bf16[4,48,1728]{2,1,0:T(8,128)(2,1)} %fusion.74), channel_id=1, source_target_pairs={{0,4},{4,0},{8,12},{12,8},{16,20},{20,16},{24,28},{28,24},{1,5},{5... | collective-permute-start | bytes 1990664 | tf_op jit(solution)/shard_map/ppermute | solution.py:194
  356.0 16.5 %collective-permute-start.36 = (bf16[4,48,1728]{2,1,0:T(8,128)(2,1)}, bf16[4,48,1728]{2,1,0:T(8,128)(2,1)}, u32[]{:S(2)}, u32[]{:S(2)}) collective-permute-start(bf16[4,48,1728]{2,1,0:T(8,128)(2,1)} %fusion.76), channel_id=1, source_target_pairs={{0,2},{1,3},{2,0},{3,1},{4,6},{5,7},{6,4},{7,5},{8,10},{9,11},{10,... | collective-permute-start | bytes 1990664 | tf_op jit(solution)/shard_map/ppermute | solution.py:194
  360.8 11.8 %copy-start.15 = (f32[2,4,48,1728]{3,2,1,0:T(8,128)S(1)}, f32[2,4,48,1728]{3,2,1,0:T(8,128)}, u32[]{:S(2)}) copy-start(f32[2,4,48,1728]{3,2,1,0:T(8,128)} %copy-done.14) | copy-start | bytes 7962628
  360.8 1.3 collective-permute-start.24
  362.1 8.1 %collective-permute-start.25 = (f32[5,768]{1,0:T(8,128)S(1)}, f32[5,768]{1,0:T(8,128)S(1)}, u32[]{:S(2)}, u32[]{:S(2)}) collective-permute-start(f32[5,768]{1,0:T(8,128)S(1)} %add.304), channel_id=1, source_target_pairs={{0,2},{1,3},{2,0},{3,1},{4,6},{5,7},{6,4},{7,5},{8,10},{9,11},{10,... | collective-permute-start | bytes 46088 | tf_op jit(solution)/shard_map/ppermute | solution.py:194
  370.1 5.5 %collective-permute-start.26 = (f32[5,768]{1,0:T(8,128)S(1)}, f32[5,768]{1,0:T(8,128)S(1)}, u32[]{:S(2)}, u32[]{:S(2)}) collective-permute-start(f32[5,768]{1,0:T(8,128)S(1)} %add.305), channel_id=1, source_target_pairs={{0,4},{4,0},{8,12},{12,8},{16,20},{20,16},{24,28},{28,24},{1,5},{5... | collective-permute-start | bytes 46088 | tf_op jit(solution)/shard_map/ppermute | solution.py:194
  373.8 14.1 %copy-start.17 = (f32[512,768]{1,0:T(8,128)S(1)}, f32[512,768]{1,0:T(8,128)}, u32[]{:S(2)}) copy-start(f32[512,768]{1,0:T(8,128)} %get-tuple-element.88) | copy-start | bytes 4718596
  374.1 20.6 %collective-permute-start.39 = (bf16[2,96,1728]{2,1,0:T(8,128)(2,1)S(1)}, bf16[2,96,1728]{2,1,0:T(8,128)(2,1)S(1)}, u32[]{:S(2)}, u32[]{:S(2)}) collective-permute-start(bf16[2,96,1728]{2,1,0:T(8,128)(2,1)S(1)} %fusion.75), channel_id=1, source_target_pairs={{0,8},{4,12},{8,0},{12,4},{16,24},{20,28},{24,16},{28,20},{1,9},{5... | collective-permute-start | bytes 1990664 | tf_op jit(solution)/shard_map/ppermute | solution.py:194
  375.6 12.3 %collective-permute-start.27 = (f32[5,768]{1,0:T(8,128)S(1)}, f32[5,768]{1,0:T(8,128)S(1)}, u32[]{:S(2)}, u32[]{:S(2)}) collective-permute-start(f32[5,768]{1,0:T(8,128)S(1)} %add.306), channel_id=1, source_target_pairs={{0,8},{4,12},{8,0},{12,4},{16,24},{20,28},{24,16},{28,20},{1,9},{5... | collective-permute-start | bytes 46088 | tf_op jit(solution)/shard_map/ppermute | solution.py:194
  387.9 6.8 %collective-permute-start.28 = (f32[5,768]{1,0:T(8,128)S(1)}, f32[5,768]{1,0:T(8,128)S(1)}, u32[]{:S(2)}, u32[]{:S(2)}) collective-permute-start(f32[5,768]{1,0:T(8,128)S(1)} %add.307), channel_id=1, source_target_pairs={{0,16},{4,20},{8,24},{12,28},{16,0},{20,4},{24,8},{28,12},{1,17},{... | collective-permute-start | bytes 46088 | tf_op jit(solution)/shard_map/ppermute | solution.py:194
  394.9 10.7 %collective-permute-start.40 = (bf16[1,96,1728]{2,1,0:T(8,128)(2,1)S(1)}, bf16[1,96,1728]{2,1,0:T(8,128)(2,1)S(1)}, u32[]{:S(2)}, u32[]{:S(2)}) collective-permute-start(bf16[1,96,1728]{2,1,0:T(8,128)(2,1)S(1)} %dynamic-slice_convert_fusion.4), channel_id=1, source_target_pairs={{0,16},{4,20},{8,24},{12,28},{16,0},{20,4},{24,8},{28,12},{1,17},{... | collective-permute-start | bytes 995336 | tf_op jit(solution)/shard_map/ppermute | solution.py:194
  (41 other events, 158.1 us)

commit v2 on v1

v2 whole, which is shorter than its diff:
```python
import functools

import jax
import jax.numpy as jnp
from jax import lax
from jax.experimental import pallas as pl
from jax.experimental.pallas import tpu as pltpu
from jax.sharding import PartitionSpec as P

HD=64; EPSILON=1e-6
LOG2E=1.4426950408889634
QSCALE=LOG2E/8.0
BIG=256.0
F32=jnp.float32; BF=jnp.bfloat16

def nn(a,b): return lax.dot_general(a,b,(((1,),(0,)),((),())),preferred_element_type=F32)

def norm_T(x):
    c = x - jnp.mean(x,axis=0,keepdims=True)
    inv = lax.rsqrt(jnp.mean(c*c,axis=0,keepdims=True)+EPSILON)
    return c*inv, inv

def split3(v):
    hi=v.astype(BF).astype(F32); r=v-hi
    mid=r.astype(BF).astype(F32); lo=r-mid
    return hi,mid,lo

def fwd_kernel(n_ref,l_ref, q_ref,k_ref,v_ref,fq_ref,fk_ref,qg_ref,kg_ref,o_ref,lse_ref,KT,QN,VN,*,HG,Q,K,BQ,BK,CH):
    ones_row = jnp.where(lax.broadcasted_iota(jnp.int32,(64,CH),0)==0,1.0,0.0).astype(F32)
    for h in range(HG):
        for c in range(K//CH):
            s=slice(c*CH,(c+1)*CH)
            kn,_=norm_T(k_ref[h,:,s])
            KT[h,:64,s]=(kn*kg_ref[...]).astype(BF)
            KT[h,64:,s]=fk_ref[:,s]
            VN[h,s,:]=jnp.concatenate([v_ref[h,:,s].astype(F32),ones_row],axis=0).T.astype(BF)
        for c in range(Q//CH):
            s=slice(c*CH,(c+1)*CH)
            qn,_=norm_T(q_ref[h,:,s])
            qa=jnp.concatenate([qn*(qg_ref[...]*QSCALE),fq_ref[:,s].astype(F32)],axis=0)
            QN[h,s,:]=qa.T.astype(BF)
    NK=K//BK
    for qb in range(Q//BQ):
        def body(i,accs):
            kb=pl.multiple_of(l_ref[qb*NK+i]*BK,BK)
            out=[]
            for h in range(HG):
                S=nn(QN[h,qb*BQ:(qb+1)*BQ,:],KT[h,:,pl.ds(kb,BK)])
                P=jnp.exp2(S).astype(BF)
                out.append(accs[h]+nn(P,VN[h,pl.ds(kb,BK),:]))
            return tuple(out)
        accs=lax.fori_loop(0,n_ref[qb],body,tuple(jnp.zeros((BQ,128),F32) for _ in range(HG)))
        for h in range(HG):
            t=accs[h].T
            tot=t[64:65]
            s=slice(qb*BQ,(qb+1)*BQ)
            o_ref[h,:,s]=(t[:64]/tot).astype(BF)
            lse_ref[h,:,s]=jnp.log2(tot)

def attn_fwd(n,l,q,kv,fq,fk,qg,kg,*,HG=3,BQ=256,BK=256,CH=512,deps=()):
    Q=q.shape[-1]; K=kv.shape[-1]
    q=q.reshape(3,64,Q); kv=kv.reshape(2,3,64,K)
    kern=functools.partial(fwd_kernel,HG=HG,Q=Q,K=K,BQ=BQ,BK=BK,CH=CH)
    full=lambda shp: pl.BlockSpec(shp,lambda g,*_:(0,)*len(shp))
    return pl.pallas_call(drop_deps(kern,9,len(deps)),
      out_shape=(jax.ShapeDtypeStruct((3,64,Q),BF),jax.ShapeDtypeStruct((3,1,Q),F32)),
      grid_spec=pltpu.PrefetchScalarGridSpec(num_scalar_prefetch=2,grid=(3//HG,),
        in_specs=[pl.BlockSpec((HG,64,Q),lambda g,*_:(g,0,0)),
                  pl.BlockSpec((None,HG,64,K),lambda g,*_:(0,g,0,0)),
                  pl.BlockSpec((None,HG,64,K),lambda g,*_:(1,g,0,0)),
                  full((64,Q)),full((64,K)),full((64,1)),full((64,1))]+[pl.BlockSpec(memory_space=pl.ANY)]*len(deps),
        out_specs=(pl.BlockSpec((HG,64,Q),lambda g,*_:(g,0,0)),pl.BlockSpec((HG,1,Q),lambda g,*_:(g,0,0))),
        scratch_shapes=[pltpu.VMEM((HG,128,K),BF),pltpu.VMEM((HG,Q,128),BF),pltpu.VMEM((HG,K,128),BF)]),
      compiler_params=pltpu.CompilerParams(vmem_limit_bytes=48*2**20),
      cost_estimate=cost(1.2e10),name="attn_fwd")(n,l,q,kv,kv,fq,fk,qg.reshape(64,1),kg.reshape(64,1),*deps)

def bwd_kernel(n_ref,l_ref, q_ref,k_ref,v_ref,do_ref,o_ref,lse_ref,fq_ref,fk_ref,qg_ref,kg_ref,
               gq_ref,gkv_ref,gqg_ref,gkg_ref, KT,KN,VN,QT,QN,DOT,DON,DQT,DK,DV,*,HG,Q,K,BQ,BK,CH):
    first=pl.program_id(0)==0
    @pl.when(first)
    def _():
        gqg_ref[...]=jnp.zeros_like(gqg_ref); gkg_ref[...]=jnp.zeros_like(gkg_ref)
    row=lax.broadcasted_iota(jnp.int32,(64,CH),0)
    three=jnp.where(row<3,1.0,0.0).astype(F32)
    for h in range(HG):
        for c in range(K//CH):
            s=slice(c*CH,(c+1)*CH)
            kn,_=norm_T(k_ref[h,:,s])
            kt=jnp.concatenate([kn*kg_ref[...],fk_ref[:,s].astype(F32)],axis=0)
            KT[h,:,s]=kt[:64].astype(BF)
            KN[h,s,:]=kt.T.astype(BF)
            VN[h,s,:]=jnp.concatenate([v_ref[h,:,s].astype(F32),three],axis=0).T.astype(BF)
            DK[h,s,:]=jnp.zeros((CH,128),F32); DV[h,s,:]=jnp.zeros((CH,128),F32)
        for c in range(Q//CH):
            s=slice(c*CH,(c+1)*CH)
            qn,_=norm_T(q_ref[h,:,s])
            a,b,d=split3(-lse_ref[h,:,s])
            f=fq_ref[:,s].astype(F32)
            f=jnp.where(row==33,a,jnp.where(row==34,b,jnp.where(row==35,d,f)))
            qt=jnp.concatenate([qn*(qg_ref[...]*QSCALE),f],axis=0)
            QT[h,:,s]=qt.astype(BF)
            QN[h,s,:]=qt.T.astype(BF)
            do=do_ref[h,:,s].astype(F32)
            D=-jnp.sum(do*o_ref[h,:,s].astype(F32),axis=0,keepdims=True)
            a,b,d=split3(D)
            g=jnp.where(row==0,a,jnp.where(row==1,b,jnp.where(row==2,d,0.0)))
            dt=jnp.concatenate([do,g],axis=0)
            DOT[h,:,s]=dt.astype(BF)
            DON[h,s,:]=dt.T.astype(BF)
    NK=K//BK
    for qb in range(Q//BQ):
        qs=slice(qb*BQ,(qb+1)*BQ)
        def body(i,accs):
            kb=pl.multiple_of(l_ref[qb*NK+i]*BK,BK)
            ks=pl.ds(kb,BK)
            out=[]
            for h in range(HG):
                ST=nn(KN[h,ks,:],QT[h,:,qs])
                P=jnp.exp2(ST)
                DP=nn(VN[h,ks,:],DOT[h,:,qs])
                dS=(P*DP).astype(BF)
                DV[h,ks,:]+=nn(P.astype(BF),DON[h,qs,:])
                DK[h,ks,:]+=nn(dS,QN[h,qs,:])
                out.append(accs[h]+nn(KT[h,:,ks],dS))
            return tuple(out)
        accs=lax.fori_loop(0,n_ref[qb],body,tuple(jnp.zeros((64,BQ),F32) for _ in range(HG)))
        for h in range(HG): DQT[h,:,qs]=accs[h]
    def ln_back(dx,gain,raw):
        hat,inv=norm_T(raw)
        u=dx*gain
        g=inv*(u-jnp.mean(u,axis=0,keepdims=True)-hat*jnp.mean(u*hat,axis=0,keepdims=True))
        return g, jnp.sum(dx*hat,axis=1,keepdims=True)
    for h in range(HG):
        for c in range(K//CH):
            s=slice(c*CH,(c+1)*CH)
            g,gg=ln_back(DK[h,s,:].T[:64]*(1.0/LOG2E),kg_ref[...],k_ref[h,:,s])
            gkv_ref[0,h,:,s]=g.astype(BF)
            gkg_ref[...]+=gg
            gkv_ref[1,h,:,s]=DV[h,s,:].T[:64].astype(BF)
        for c in range(Q//CH):
            s=slice(c*CH,(c+1)*CH)
            g,gg=ln_back(DQT[h,:,s]*0.125,qg_ref[...],q_ref[h,:,s])
            gq_ref[h,:,s]=g.astype(BF)
            gqg_ref[...]+=gg

def attn_bwd(n,l,q,kv,do,o,lse,fq,fk,qg,kg,*,HG=3,BQ=256,BK=256,CH=512,deps=()):
    Q=q.shape[-1]; K=kv.shape[-1]
    q=q.reshape(3,64,Q); kv=kv.reshape(2,3,64,K); do=do.reshape(3,64,Q)
    kern=functools.partial(bwd_kernel,HG=HG,Q=Q,K=K,BQ=BQ,BK=BK,CH=CH)
    full=lambda shp: pl.BlockSpec(shp,lambda g,*_:(0,)*len(shp))
    qsp=lambda: pl.BlockSpec((HG,64,Q),lambda g,*_:(g,0,0))
    return pl.pallas_call(drop_deps(kern,12,len(deps)),
      out_shape=(jax.ShapeDtypeStruct((3,64,Q),BF),jax.ShapeDtypeStruct((2,3,64,K),BF),jax.ShapeDtypeStruct((64,1),F32),jax.ShapeDtypeStruct((64,1),F32)),
      grid_spec=pltpu.PrefetchScalarGridSpec(num_scalar_prefetch=2,grid=(3//HG,),
        in_specs=[qsp(),
                  pl.BlockSpec((None,HG,64,K),lambda g,*_:(0,g,0,0)),
                  pl.BlockSpec((None,HG,64,K),lambda g,*_:(1,g,0,0)),
                  qsp(),qsp(),pl.BlockSpec((HG,1,Q),lambda g,*_:(g,0,0)),
                  full((64,Q)),full((64,K)),full((64,1)),full((64,1))]+[pl.BlockSpec(memory_space=pl.ANY)]*len(deps),
        out_specs=(qsp(),pl.BlockSpec((2,HG,64,K),lambda g,*_:(0,g,0,0)),full((64,1)),full((64,1))),
        scratch_shapes=[pltpu.VMEM((HG,64,K),BF),pltpu.VMEM((HG,K,128),BF),pltpu.VMEM((HG,K,128),BF),
                        pltpu.VMEM((HG,128,Q),BF),pltpu.VMEM((HG,Q,128),BF),pltpu.VMEM((HG,128,Q),BF),pltpu.VMEM((HG,Q,128),BF),
                        pltpu.VMEM((HG,64,Q),F32),pltpu.VMEM((HG,K,128),F32),pltpu.VMEM((HG,K,128),F32)]),
      compiler_params=pltpu.CompilerParams(vmem_limit_bytes=48*2**20),
      cost_estimate=cost(2e10),name="attn_bwd")(n,l,q,kv,kv,do,o,lse,fq,fk,qg.reshape(64,1),kg.reshape(64,1),*deps)

def features(ids, Q, BQ=256, BK=256):
    K=ids.shape[0]
    r=jnp.arange(64,dtype=jnp.int32)[:,None]
    hot=(ids[None,:]+1)==r
    hot=hot&(r<32)
    fk=jnp.where(hot,1.0,jnp.where((r>=32)&(r<36),1.0,0.0)).astype(BF)
    fq=jnp.where(hot[:,:Q],BIG,jnp.where(r==32,-BIG,0.0)).astype(BF)
    kb=hot[:32].reshape(32,K//BK,BK).any(-1)
    qb=hot[:32,:Q].reshape(32,Q//BQ,BQ).any(-1)
    act=(qb[:,:,None]&kb[:,None,:]).any(0)
    n=act.sum(-1).astype(jnp.int32)
    NK=K//BK
    before=jnp.arange(NK)[:,None]>jnp.arange(NK)[None,:]
    rank=(act[:,None,:]&before[None]).sum(-1)
    lst=((rank[:,None,:]==jnp.arange(NK)[None,:,None])&act[:,None,:])
    lst=(lst*jnp.arange(NK)[None,None,:]).sum(-1).astype(jnp.int32)
    return fq,fk,n,lst.reshape(-1)


def drop_deps(kern, inputs, extra):
    if not extra:
        return kern
    return lambda *refs: kern(*refs[:inputs], *refs[inputs + extra :])


def cost(flops):
    return pl.CostEstimate(flops=int(flops * 1e-6), bytes_accessed=1024, transcendentals=0)


ANY = pl.BlockSpec(memory_space=pl.ANY)


def whole(shape):
    return pl.BlockSpec(tuple(shape), lambda *_: (0,) * len(shape))


def glue(kern, inputs, outs, bit, deps, name):
    kern = drop_deps(kern, len(inputs) + 1, len(deps))
    return pl.pallas_call(
        kern,
        out_shape=tuple(jax.ShapeDtypeStruct(s, t) for s, t in outs),
        grid_spec=pltpu.PrefetchScalarGridSpec(
            num_scalar_prefetch=1,
            grid=(1,),
            in_specs=[whole(i.shape) for i in inputs] + [ANY] * len(deps),
            out_specs=tuple(whole(s) for s, _ in outs),
        ),
        compiler_params=pltpu.CompilerParams(vmem_limit_bytes=48 * 2**20),
        cost_estimate=cost(1),
        name=name,
    )(bit.reshape(1), *inputs, *deps)


def pair_dp(held, got, bit, cuts=None, deps=()):
    m, rows, cols = held.shape
    cuts = [0, rows] if cuts is None else [0, *cuts, rows]

    def kern(bit_ref, held_ref, got_ref, *outs):
        bit = bit_ref[0]
        for i in range(m):
            for lo, hi, out in zip(cuts, cuts[1:], outs):
                out[i, bit] = held_ref[i, lo:hi]
                out[i, 1 - bit] = got_ref[i, lo:hi]

    outs = [((m, 2, hi - lo, cols), held.dtype) for lo, hi in zip(cuts, cuts[1:])]
    res = glue(kern, (held, got), outs, bit, deps, "pair_dp")
    return [r.reshape(2 * m, r.shape[2], cols) for r in res]


def pair_both(part_a, got_a, part_b, got_b, bit, deps=()):
    m, rows_a, cols = part_a.shape
    rows_b = part_b.shape[1]

    def kern(bit_ref, a, ga, b, gb, out_a, out_b):
        bit = bit_ref[0]
        out_a[0] = a[...]
        out_a[1] = ga[...]
        for i in range(m):
            out_b[i, bit] = b[i]
            out_b[i, 1 - bit] = gb[i]

    outs = [((2, m, rows_a, cols), BF), ((m, 2, rows_b, cols), BF)]
    return glue(kern, (part_a, got_a, part_b, got_b), outs, bit, deps, "pair_both")


def pair_last(part_a, got_a, part_b, got_b, bit, deps=()):
    _, m, rows_a, cols = part_a.shape
    rows_b = part_b.shape[2]

    def kern(bit_ref, a, ga, b, gb, out):
        bit = bit_ref[0]
        for i in range(m):
            for t in range(2):
                out[t, i, bit, :rows_a] = a[t, i]
                out[t, i, 1 - bit, :rows_a] = ga[t, i]
            for y in range(2):
                out[0, i, y, rows_a:] = b[i, y]
                out[1, i, y, rows_a:] = gb[i, y]

    outs = [((2, m, 2, rows_a + rows_b, cols), BF)]
    (res,) = glue(kern, (part_a, got_a, part_b, got_b), outs, bit, deps, "pair_last")
    return res.reshape(2, 2 * m * (rows_a + rows_b), cols)


def fold_dp(kept, got, bit, deps=()):
    n, rows, cols = kept.shape

    def kern(bit_ref, kept_ref, got_ref, keep, send):
        bit = bit_ref[0]
        for i in range(n // 2):
            keep[i] = kept_ref[2 * i + bit].astype(F32) + got_ref[2 * i + bit].astype(F32)
            send[i] = (kept_ref[2 * i + 1 - bit].astype(F32) + got_ref[2 * i + 1 - bit].astype(F32)).astype(BF)

    outs = [((n // 2, rows, cols), F32), ((n // 2, rows, cols), BF)]
    return glue(kern, (kept, got), outs, bit, deps, "fold_dp")


def fold_x(kept, got, bit, deps=()):
    shape = kept.shape[1:]

    def kern(bit_ref, kept_ref, got_ref, keep, send):
        keep[...] = kept_ref[0].astype(F32) + got_ref[0].astype(F32)
        send[...] = (kept_ref[1].astype(F32) + got_ref[1].astype(F32)).astype(BF)

    return glue(kern, (kept, got), [(shape, F32), (shape, BF)], bit, deps, "fold_x")


def split_store(value, bit, keep, send, blocks):
    rows = value.shape[0] // blocks
    for b in range(2):

        @pl.when(bit == b)
        def _(b=b):
            for j in range(blocks):
                part = value[j * rows : (j + 1) * rows].astype(BF)
                if j % 2 == b:
                    keep[j // 2] = part
                else:
                    send[j // 2] = part


def nt(a, b):
    return lax.dot_general(a, b, (((1,), (1,)), ((), ())), preferred_element_type=F32)


def gelu_pair(v):
    x = jnp.abs(v) * (0.5**0.5)
    t = 1.0 / (1.0 + 0.3275911 * x)
    e = jnp.exp2(v * v * (-0.5 * LOG2E))
    poly = ((((1.061405429 * t - 1.453152027) * t + 1.421413741) * t - 0.284496736) * t + 0.254829592) * t
    tail = 0.5 * poly * e
    phi = jnp.where(v < 0, tail, 1.0 - tail)
    return v * phi, phi + v * e * 0.3989422804014327


def mlp_fwd_kernel(bit_ref, n2_ref, cot_ref, wu_ref, wd_ref, slope_ref, keep_ref, part_ref, own_ref, send_ref, cott, acc, *, rows, chunk):
    step = pl.program_id(0) * pl.num_programs(1) + pl.program_id(1)
    last = pl.num_programs(0) * pl.num_programs(1) - 1

    @pl.when(step == 0)
    def _():
        for i in range(rows // chunk):
            s = slice(i * chunk, (i + 1) * chunk)
            cott[:, s] = cot_ref[s, :].T
        acc[...] = jnp.zeros_like(acc)

    total = jnp.zeros(wd_ref.shape, F32)
    for i in range(rows // chunk):
        s = slice(i * chunk, (i + 1) * chunk)
        hid, slope = gelu_pair(nn(n2_ref[s, :], wu_ref[...]))
        slope_ref[s, :] = slope.astype(BF)
        hid = hid.astype(BF)
        acc[s, :] += nt(hid, wd_ref[...])
        total += nn(cott[:, s], hid)
    split_store(total, bit_ref[0], keep_ref, part_ref, 2 * keep_ref.shape[0])

    @pl.when(step == last)
    def _():
        own_ref[...] = acc[: rows // 2]
        send_ref[...] = acc[rows // 2 :].astype(BF)


def mlp_bwd_kernel(bit_ref, n2_ref, cot_ref, wu_ref, wd_ref, slope_ref, keep_ref, part_ref, own_ref, send_ref, n2t, acc, *, rows, chunk):
    step = pl.program_id(0) * pl.num_programs(1) + pl.program_id(1)
    last = pl.num_programs(0) * pl.num_programs(1) - 1

    @pl.when(step == 0)
    def _():
        for i in range(rows // chunk):
            s = slice(i * chunk, (i + 1) * chunk)
            n2t[:, s] = n2_ref[s, :].T
        acc[...] = jnp.zeros_like(acc)

    total = jnp.zeros(wu_ref.shape, F32)
    for i in range(rows // chunk):
        s = slice(i * chunk, (i + 1) * chunk)
        grad = (nn(cot_ref[s, :], wd_ref[...]) * slope_ref[s, :].astype(F32)).astype(BF)
        acc[s, :] += nt(grad, wu_ref[...])
        total += nn(n2t[:, s], grad)
    split_store(total, bit_ref[0], keep_ref, part_ref, 2 * keep_ref.shape[0])

    @pl.when(step == last)
    def _():
        own_ref[...] = acc[: rows // 2]
        send_ref[...] = acc[rows // 2 :].astype(BF)


def mlp_fwd(n2, cot, wu, wd, bit, blocks, deps=()):
    return mlp_call(mlp_fwd_kernel, True, (n2, cot, wu, wd), bit, blocks, deps)


def mlp_bwd(n2, cot, wu, wd, slope, bit, blocks, deps=()):
    return mlp_call(mlp_bwd_kernel, False, (n2, cot, wu, wd, slope), bit, blocks, deps)


def mlp_call(kernel, forward, arrays, bit, blocks, deps):
    rows, width = arrays[0].shape
    cols = arrays[3].shape[2]
    blk = 256
    full = pl.BlockSpec((rows, width), lambda r, c, _: (0, 0))
    half = pl.BlockSpec((rows // 2, width), lambda r, c, _: (0, 0))
    weight = pl.BlockSpec((None, width, blk), lambda r, c, _: (r, 0, c))
    slope = pl.BlockSpec((None, rows, blk), lambda r, c, _: (r, 0, c))
    part = pl.BlockSpec((None, blocks // 2, width // blocks, blk), lambda r, c, _: (r, 0, 0, c))
    part_shape = jax.ShapeDtypeStruct((2, blocks // 2, width // blocks, cols), BF)
    out_specs = (part, part, half, half)
    out_shape = (part_shape, part_shape, jax.ShapeDtypeStruct((rows // 2, width), F32), jax.ShapeDtypeStruct((rows // 2, width), BF))
    if forward:
        out_specs = (slope, *out_specs)
        out_shape = (jax.ShapeDtypeStruct((2, rows, cols), BF), *out_shape)
    kern = functools.partial(kernel, rows=rows, chunk=256)
    return pl.pallas_call(
        drop_deps(kern, len(arrays) + 1, len(deps)),
        out_shape=out_shape,
        grid_spec=pltpu.PrefetchScalarGridSpec(
            num_scalar_prefetch=1,
            grid=(2, cols // blk),
            in_specs=[full, full, weight, weight, slope][: len(arrays)] + [ANY] * len(deps),
            out_specs=out_specs,
            scratch_shapes=[pltpu.VMEM((width, rows), BF), pltpu.VMEM((rows, width), F32)],
        ),
        compiler_params=pltpu.CompilerParams(vmem_limit_bytes=48 * 2**20),
        cost_estimate=cost(1.2e10),
        name="mlp_fwd" if forward else "mlp_bwd",
    )(bit.reshape(1), *arrays, *deps)


def proj_grad_kernel(bit_ref, gkv_ref, gq_ref, x_ref, w_ref, *rest, kv_cols, q_cols, atts):
    rest = list(rest)
    prev_ref = None if atts else rest.pop(0)
    att_refs = [rest.pop(0) for _ in range(atts)]
    branch_ref = rest.pop(0) if atts else None
    keep_ref, part_ref, gx_ref, accw = rest
    step = pl.program_id(0)
    own = pl.num_programs(0) // 2
    gkv = gkv_ref[...]
    x = x_ref[...]

    @pl.when(step == 0)
    def _():
        accw[...] = jnp.zeros_like(accw)

    accw[:kv_cols] += nn(gkv, x)
    base = nt(gkv.T, w_ref[:, :kv_cols])
    if prev_ref is not None:
        base += prev_ref[...].astype(F32)

    @pl.when(step >= own)
    def _():
        gx_ref[...] = base.astype(BF)

    @pl.when(step < own)
    def _():
        gq = gq_ref[...]
        accw[kv_cols : kv_cols + q_cols] += nn(gq, x)
        gx_ref[...] = (base + nt(gq.T, w_ref[:, kv_cols : kv_cols + q_cols])).astype(BF)
        for i, att in enumerate(att_refs):
            lo = kv_cols + (i + 1) * q_cols
            accw[lo : lo + q_cols] += nn(att[...], branch_ref[...])

    @pl.when(step == pl.num_programs(0) - 1)
    def _():
        split_store(accw[...].T, bit_ref[0], keep_ref, part_ref, 2 * keep_ref.shape[0])


def proj_grad(gkv, gq, x, w, bit, blocks, prev=None, atts=(), branch=None, deps=()):
    kv_cols, slots = gkv.shape
    q_cols, q_slots = gq.shape
    width = w.shape[0]
    cols = kv_cols + q_cols * (1 + len(atts))
    blk = slots // 4
    last = q_slots // blk - 1
    kern = functools.partial(proj_grad_kernel, kv_cols=kv_cols, q_cols=q_cols, atts=len(atts))
    thin = pl.BlockSpec((q_cols, blk), lambda s, _: (0, jnp.minimum(s, last)))
    arrays = [gkv, gq, x, w]
    specs = [
        pl.BlockSpec((kv_cols, blk), lambda s, _: (0, s)),
        thin,
        pl.BlockSpec((blk, width), lambda s, _: (s, 0)),
        pl.BlockSpec(w.shape, lambda s, _: (0, 0)),
    ]
    if prev is not None:
        arrays.append(prev)
        specs.append(pl.BlockSpec((None, blk, width), lambda s, _: (s, 0, 0)))
    else:
        arrays += [*atts, branch]
        specs += [thin] * len(atts) + [pl.BlockSpec((blk, width), lambda s, _: (jnp.minimum(s, last), 0))]
    part = (blocks // 2, width // blocks, cols)
    return pl.pallas_call(
        drop_deps(kern, len(arrays) + 1, len(deps)),
        out_shape=(jax.ShapeDtypeStruct(part, BF), jax.ShapeDtypeStruct(part, BF), jax.ShapeDtypeStruct((4, blk, width), BF)),
        grid_spec=pltpu.PrefetchScalarGridSpec(
            num_scalar_prefetch=1,
            grid=(4,),
            in_specs=specs + [ANY] * len(deps),
            out_specs=(whole(part), whole(part), pl.BlockSpec((None, blk, width), lambda s, _: (s, 0, 0))),
            scratch_shapes=[pltpu.VMEM((cols, width), F32)],
        ),
        compiler_params=pltpu.CompilerParams(vmem_limit_bytes=48 * 2**20),
        cost_estimate=cost(5e9),
        name="proj_grad",
    )(bit.reshape(1), *arrays, *deps)


def xor_perm(size, mask):
    return [(i, i ^ mask) for i in range(size)]


def swap(values, axis, mask):
    return lax.ppermute(values, axis, xor_perm(lax.axis_size(axis), mask))


def dp_levels():
    return list(reversed(range(lax.axis_size("dp").bit_length() - 1)))


def after(values, other):
    return values + (other[(0,) * other.ndim] * 0).astype(values.dtype)


def sum_all(values):
    values = values + swap(values, "tensor", 1)
    values = values + swap(values, "tensor", 2)
    for level in reversed(dp_levels()):
        values = values + swap(values, "dp", 1 << level)
    return values


def hat_of(values):
    center = values - jnp.mean(values, axis=-1, keepdims=True)
    inv = lax.rsqrt(jnp.mean(center * center, axis=-1, keepdims=True) + EPSILON)
    return center * inv, inv


def hat_back(grad, gain, hat, inv):
    u = grad * gain
    return inv * (u - jnp.mean(u, axis=-1, keepdims=True) - hat * jnp.mean(u * hat, axis=-1, keepdims=True))


def core_sum(own, send):
    return own.astype(F32) + swap(send, "tensor", 1).astype(F32)


def with_core(own):
    return jnp.concatenate([own, swap(own, "tensor", 1)], axis=0)


def mm(spec, *arrays):
    return jnp.einsum(spec, *arrays, preferred_element_type=F32)


def per_device(tokens, picture_ids, ln1_gain, ln1_bias, w_qkv, q_gain, k_gain, w_out, ln2_gain, ln2_bias, w_up, w_down, cotangent):
    slots, width = tokens.shape[1:]
    local = w_qkv.shape[2]
    fcols = w_up.shape[1]
    dp = lax.axis_size("dp")
    rows = width // dp
    tok = tokens[0]
    cot = cotangent[0]
    tensor = lax.axis_index("tensor")
    me = lax.axis_index("dp")
    levels = dp_levels()
    far, near = levels[:-1], levels[-1]
    bits = {level: (me >> level) & 1 for level in levels}
    n_dp = width // rows
    q_slots = 2 * slots

    def dp_swap(values, level):
        return swap(values, "dp", 1 << level)

    def grow(held, level, deps=(), cuts=None):
        return pair_dp(held, dp_swap(held, level), bits[level], cuts, deps)

    out_t = w_out.T
    part_0 = jnp.concatenate([w_qkv[:, 1], w_qkv[:, 2], w_qkv[:, 0]], axis=1)
    got = swap(jnp.concatenate([part_0, out_t], axis=1), "tensor", 2)
    tok_x = swap(after(tok, got), "tensor", 2)
    tok_c = swap(tok, "tensor", 1)
    part_1 = jnp.concatenate([got, out_t], axis=1)[None]
    part_0 = part_0[None]
    up = w_up[None]
    down = w_down.T[None]
    for i, level in enumerate(far):
        (part_0,) = grow(part_0, level, (part_1,))
        (part_1,) = grow(part_1, level, (part_0,))
        if i == 0:
            up = after(up, part_1)
    half = rows // 3 // 16 * 16 if rows >= 48 else rows // 2
    one = len(far) == 1
    up = grow(up, far[0], (part_1,), (half,) if one else None)
    down = after(down, up[0])
    for level in far[1:-1]:
        up = grow(up[0], level)
    (w_0,) = grow(part_0, near, tuple(up))
    w_0 = w_0.reshape(width, 3 * local)

    tok_xc = swap(tok_x, "tensor", 1)
    cot_all = with_core(cot)
    ids = picture_ids[0].reshape(4, slots)
    ids = jnp.concatenate([lax.dynamic_index_in_dim(ids, tensor ^ i, 0, keepdims=False) for i in range(4)])
    fq, fk, count, blocks = features(ids, q_slots, BQ, BK)
    hats = [hat_of(block.astype(F32)) for block in (tok, tok_c, tok_x, tok_xc)]
    normed = jnp.concatenate([(hat * ln1_gain + ln1_bias).astype(BF) for hat, _ in hats], axis=0)

    def forward(weights, deps):
        kv = mm("sd,dc->cs", normed, weights[:, : 2 * local]).reshape(2, local, 4 * slots)
        q = mm("sd,dc->cs", normed[:q_slots], weights[:, 2 * local : 3 * local])
        att, lse = attn_fwd(count, blocks, q, kv, fq, fk, q_gain, k_gain, HG=HGF, BQ=BQ, BK=BK, deps=deps)
        return q, kv, att, lse

    head_0 = forward(w_0, tuple(up))
    att_0 = head_0[2]
    if not one:
        up = grow(up[0], far[-1], (att_0,), (half,))
    up_a, up_b = up
    got_a = swap(up_a, "tensor", 2)
    got_b = dp_swap(up_b, near)
    down = grow(down, far[0], (up_a,), (half,) if one else None)
    for level in far[1:-1]:
        down = grow(down[0], level)
    (w_1,) = grow(part_1, near, tuple(down))
    w_1 = w_1.reshape(width, 5 * local)
    head_1 = forward(w_1, tuple(down))
    att_1 = head_1[2]

    up_a, up_b = pair_both(up_a, got_a, up_b, got_b, bits[near], (att_1,))
    got_a = dp_swap(up_a, near)
    got_b = swap(up_b, "tensor", 2)
    if not one:
        down = grow(down[0], far[-1], (up_b,), (half,))
    down_a, down_b = down
    dgot_a = swap(down_a, "tensor", 2)
    dgot_b = dp_swap(down_b, near)

    wo = jnp.stack([w_1[:, 4 * local :], w_1[:, 3 * local : 4 * local]])
    heads = (head_0, head_1)
    att_cols = jnp.stack([h[2].reshape(local, q_slots) for h in heads])
    share = mm("rcs,rdc->sd", att_cols, wo)
    middle = tok.astype(F32) + core_sum(share[:slots], share[slots:].astype(BF))
    hat2, inv2 = hat_of(middle)
    normed2 = with_core((hat2 * ln2_gain + ln2_bias).astype(BF))
    down_a, down_b = pair_both(down_a, dgot_a, down_b, dgot_b, bits[near], (normed2,))
    dgot_a = dp_swap(down_a, near)
    dgot_b = swap(down_b, "tensor", 2)
    wu = pair_last(up_a, got_a, up_b, got_b, bits[near])
    wd = pair_last(down_a, dgot_a, down_b, dgot_b, bits[near], (wu,))

    slope, d_keep, d_send, mlp_own, mlp_send = mlp_fwd(normed2, cot_all, wu, wd, bits[near], n_dp)
    d_got = dp_swap(d_send, near)
    u_keep, u_send, gn2_own, gn2_send = mlp_bwd(normed2, cot_all, wu, wd, slope, bits[near], n_dp, (d_send,))
    u_got = dp_swap(u_send, near)
    grad_normed2 = core_sum(gn2_own, gn2_send)
    grad_mid = cot.astype(F32) + hat_back(grad_normed2, ln2_gain, hat2, inv2)
    branch = with_core(grad_mid.astype(BF))
    grad_att = mm("sd,rdc->rcs", branch, wo).astype(BF)
    d_keep, d_send = fold_x(d_keep, d_got, bits[near], (branch,))
    d_got = swap(d_send, "tensor", 2)

    def back(g, deps):
        q, kv, att, lse = heads[g]
        gq, gkv, qg, kg = attn_bwd(
            count, blocks, q, kv, grad_att[g], att, lse, fq, fk, q_gain, k_gain, HG=HGB, BQ=BQ, BK=BK, deps=deps
        )
        return gq.reshape(local, q_slots), gkv.reshape(2 * local, 4 * slots), qg, kg

    rest = levels[::-1][1:]
    gq, gkv, qg_1, kg_1 = back(1, (u_send, d_send))
    u_keep, u_send = fold_x(u_keep, u_got, bits[near], (gq,))
    u_got = swap(u_send, "tensor", 2)
    d_keep, d_send = fold_dp(d_keep, d_got, bits[rest[0]], (gq,))
    d_got = dp_swap(d_send, rest[0])
    a_keep, a_send, gx = proj_grad(
        gkv, gq, normed, w_1, bits[near], n_dp, atts=(att_cols[1], att_cols[0]), branch=branch, deps=(u_send, d_send)
    )
    a_got = dp_swap(a_send, near)
    d_keep, d_send = fold_dp(d_keep, d_got, bits[rest[1]], (gx,))
    d_got = dp_swap(d_send, rest[1])
    gq, gkv, qg_0, kg_0 = back(0, (a_send, d_send))
    u_keep, u_send = fold_dp(u_keep, u_got, bits[rest[0]], (gq,))
    u_got = dp_swap(u_send, rest[0])
    a_keep, a_send = fold_dp(a_keep, a_got, bits[rest[0]], (gq,))
    a_got = dp_swap(a_send, rest[0])
    z_keep, z_send, gx = proj_grad(gkv, gq, normed, w_0, bits[near], n_dp, prev=gx, deps=(u_send, a_send))
    z_got = dp_swap(z_send, near)
    across = core_sum(gx[2], gx[3])
    got = swap(across.astype(BF), "tensor", 2)
    grad_normed = core_sum(gx[0], gx[1])
    u_keep, u_send = fold_dp(u_keep, u_got, bits[rest[1]], (gx,))
    u_got = dp_swap(u_send, rest[1])
    a_keep, a_send = fold_dp(a_keep, a_got, bits[rest[1]], (gx,))
    a_got = dp_swap(a_send, rest[1])

    def finish(keep, got, levels):
        for level in levels:
            keep, send = fold_dp(keep, got, bits[level])
            got = dp_swap(send, level)
        return (keep + got.astype(F32)).reshape(rows, -1)

    grad_zero = finish(z_keep, z_got, rest)
    grad_a = finish(a_keep, a_got, rest[2:])
    grad_u = finish(u_keep, u_got, rest[2:])
    grad_d = finish(d_keep, d_got, rest[2:])
    mine = jnp.concatenate([grad_zero, grad_a[:, 4 * local :]], axis=1)
    grad_one = mine + swap(grad_a[:, : 4 * local].astype(BF), "tensor", 2).astype(F32)

    grad_gain2 = jnp.sum(grad_normed2 * hat2, axis=0)
    grad_bias2 = jnp.sum(grad_normed2, axis=0)
    result = (middle + core_sum(mlp_own, mlp_send)).astype(BF)
    hat1, inv1 = hats[0]
    grad_gain1 = jnp.sum(grad_normed * hat1, axis=0) + jnp.sum(across * hats[2][0], axis=0)
    grad_bias1 = jnp.sum(grad_normed, axis=0) + jnp.sum(across, axis=0)
    gains = jnp.concatenate([(qg_0 + qg_1)[:, 0], (kg_0 + kg_1)[:, 0]])
    small = sum_all(jnp.stack([grad_gain1, grad_bias1, grad_gain2, grad_bias2, jnp.pad(gains, (0, width - 2 * HD))]))
    grad_normed = grad_normed + got.astype(F32)
    grad_tokens = (grad_mid + hat_back(grad_normed, ln1_gain, hat1, inv1)).astype(BF)

    grad_qkv = jnp.stack([grad_one[:, 2 * local : 3 * local], grad_one[:, :local], grad_one[:, local : 2 * local]], axis=1)
    return (
        result[None],
        grad_tokens[None],
        small[0],
        small[1],
        grad_qkv,
        small[4, :HD],
        small[4, HD : 2 * HD],
        grad_one[:, 3 * local :].T,
        small[2],
        small[3],
        grad_u,
        grad_d.T,
    )


BQ = 512
BK = 256
HGF = 3
HGB = 3


def solution(mesh):
    rows = P("dp", "tensor", None)
    wide = P("dp", "tensor")
    tall = P("tensor", "dp")
    qkv = P("dp", None, "tensor")
    in_specs = (rows, P("dp", None), P(), P(), qkv, P(), P(), tall, P(), P(), wide, tall, rows)
    out_specs = (rows, rows, P(), P(), qkv, P(), P(), tall, P(), P(), wide, tall)
    return jax.shard_map(per_device, mesh=mesh, in_specs=in_specs, out_specs=out_specs, check_vma=False)
```

time: 416 us -> 367 us (0.88)
  Pallas kernels: 47 us -> 119 us
  matrix products: 51.1 us -> 6.5 us
  local copies, waits for them, and re-layouts: 51.3 us -> 18.4 us
  other arithmetic: 53.8 us -> 32.4 us
  waiting for transfers between devices: 154 us -> 137 us
  starting transfers between devices: 47.7 us -> 42.3 us
    pallas_call x2 -> x32, Pallas kernels: 47 us -> 119 us  [the longest x2 38.7 us: attn_bwd(): pl.pallas_call(drop_deps(kern, 12, len(deps)), out_shape=(jax.ShapeDtypeS...]
    dot_general x15 -> x6, matrix products: 51.1 us -> 6.5 us  [mm(): return jnp.einsum(spec, *arrays, preferred_element_type=F32)]
    concatenate x4 -> x0, local copies, waits for them, and re-layouts: 17.9 us -> none  [the longest x1 11.7 us: per_device(): jnp.concatenate([grad_wu, grad_wd, grad_wo], axis=2)]
    ppermute x41 -> x51, waiting for transfers between devices: 154 us -> 137 us  [swap(): return lax.ppermute(values, axis, xor_perm(lax.axis_size(axis), mask))]
    slice x10 -> x7, local copies, waits for them, and re-layouts: 14.3 us -> 1.7 us  [the longest x3 1.54 us: after(): return values + (other[(0,) * other.ndim] * 0).astype(values.dtype)]
    concatenate x7 -> x6, other arithmetic: 14.3 us -> 3.55 us  [the longest x1 1.87 us: per_device(): jnp.concatenate([(hat * ln1_gain + ln1_bias).astype(BF) for hat, _ in hat...]
    convert_element_type x12 -> x0, local copies, waits for them, and re-layouts: 8.67 us -> none  [the longest x2 4.25 us: scatter_grads(): got = swap(part_b[1].astype(BF), 'tensor', 2)]
    add x10 -> x6, other arithmetic: 7.87 us -> 1.27 us  [the longest x3 0.96 us: after(): return values + (other[(0,) * other.ndim] * 0).astype(values.dtype)]
  transfers between devices with their start and end apart: 41 -> 51, of which waited for: 20 -> 27; matrix products, arithmetic and copies ran while one was open for 24% -> 10% of each run, Pallas kernels for 4% -> 14%
where the time goes in v2:
time: 367 us; the launch traced here: 360 us
  waiting for transfers between devices  137 us (37%)
  Pallas kernels  119 us (32%)
  starting transfers between devices  42.3 us (12%)
  other arithmetic  32.4 us (9%)
  local copies, waits for them, and re-layouts  18.4 us (5%)
  matrix products  6.5 us (2%)
  between operations  4.26 us (1%)
    ppermute x51, waiting for transfers between devices, swap(): return lax.ppermute(values, axis, xor_perm(lax.axis_size(axis), mask))  137 us
    ppermute x51, starting transfers between devices, swap(): return lax.ppermute(values, axis, xor_perm(lax.axis_size(axis), mask))  42.3 us
    pallas_call x2, Pallas kernels, attn_bwd(): pl.pallas_call(drop_deps(kern, 12, len(deps)), out_shape=(jax.ShapeDtypeS...  38.7 us
    pallas_call x2, Pallas kernels, mlp_call(): pl.pallas_call(drop_deps(kern, len(arrays) + 1, len(deps)), out_shape=out...  37.4 us
    pallas_call x2, Pallas kernels, attn_fwd(): pl.pallas_call(drop_deps(kern, 9, len(deps)), out_shape=(jax.ShapeDtypeSt...  21.5 us
    pallas_call x2, Pallas kernels, proj_grad(): pl.pallas_call(drop_deps(kern, len(arrays) + 1, len(deps)), out_shape=(ja...  18.6 us
    unnamed x90, local copies, waits for them, and re-layouts  11.4 us
  transfers between devices with their start and end apart: 51, of which 27 were waited for; matrix products, arithmetic and copies ran while one was open for 10% of the time, Pallas kernels for 14%

profile of v2, /device:TPU:0, one launch (start us, length us, event | category | flops | bytes accessed | tf_op | source)
XLA Modules:
  0.0 359.7 jit_solution(3110910268396012559)
XLA Ops:
  1.7 4.1 %collective-permute-start = (bf16[1,96,576]{2,1,0:T(8,128)(2,1)S(1)}, bf16[1,96,576]{2,1,0:T(8,128)(2,1)S(1)}, u32[]{:S(2)}, u32[]{:S(2)}) collective-permute-start(bf16[1,96,576]{2,1,0:T(8,128)(2,1)S(1)} %maximum_bitcast_fusion.1.refs_1_), channel_id=1, source_target_pairs={{0,16},{4,20},{8,24},{12,28},{16,0},{20,4},{24,8},{28,12},{1,17},{... | collective-permute-start | bytes 331784 | tf_op jit(solution)/shard_map/ppermute | solution.py:496
  6.8 1.6 collective-permute-start.1
  13.2 1.6 collective-permute-start.2
  16.0 9.1 %collective-permute-done.3.refs_2_ = bf16[1,96,960]{2,1,0:T(8,128)(2,1)S(1)} collective-permute-done((bf16[1,96,960]{2,1,0:T(8,128)(2,1)S(1)}, bf16[1,96,960]{2,1,0:T(8,128)(2,1)S(1)}, u32[]{:S(2)}, u32[]{:S(2)}) %collective-permute-start.3) | collective-permute-done | bytes 184352 | tf_op jit(solution)/shard_map/ppermute | solution.py:496
  26.3 1.8 collective-permute-start.5
  30.0 1.6 collective-permute-start.4
  31.6 7.8 %collective-permute-done.6.refs_2_ = bf16[2,96,960]{2,1,0:T(8,128)(2,1)S(1)} collective-permute-done((bf16[2,96,960]{2,1,0:T(8,128)(2,1)S(1)}, bf16[2,96,960]{2,1,0:T(8,128)(2,1)S(1)}, u32[]{:S(2)}, u32[]{:S(2)}) %collective-permute-start.6) | collective-permute-done | bytes 368672 | tf_op jit(solution)/shard_map/ppermute | solution.py:496
  40.3 1.5 collective-permute-start.10
  42.6 1.9 collective-permute-start.11
  44.5 1.3 convert_reduce_fusion.3
  45.8 1.5 fusion.31
  48.4 1.3 convert_reduce_fusion.2
  49.7 1.5 fusion.30
  51.8 2.5 fusion.15
  54.4 1.5 fusion.52
  57.5 11.0 %attn_fwd.2 = (bf16[3,64,1024]{2,1,0:T(8,128)(2,1)S(1)}, f32[3,1,1024]{2,1,0:T(1,128)S(1)}) custom-call(s32[2]{0:T(128)S(1)} %convert_reduce_fusion.5.refs_0_, s32[16]{0:T(128)S(1)} %reshape.336.refs_1_, f32[3,64,1024]{2,1,0:T(8,128)S(1)} %bitcast.180, f32[2,3,64,2048]{3,2,1,0:T(8,128)S(1)} %bitcast.129, f32[2,3,64,2048]{3,2,1,0:T(8,128)S(1)} %bitcast.130, ...), custom_call_target="tpu_custom_call" | custom-call | flops 12000 | bytes 1024 | tf_op jit(solution)/shard_map/attn_fwd/pallas_call | solution.py:65
  69.4 1.4 fusion.50
  71.2 10.5 %attn_fwd.3 = (bf16[3,64,1024]{2,1,0:T(8,128)(2,1)S(1)}, f32[3,1,1024]{2,1,0:T(1,128)S(1)}) custom-call(s32[2]{0:T(128)S(1)} %convert_reduce_fusion.5.refs_0_, s32[16]{0:T(128)S(1)} %reshape.336.refs_1_, f32[3,64,1024]{2,1,0:T(8,128)S(1)} %bitcast.178, f32[2,3,64,2048]{3,2,1,0:T(8,128)S(1)} %bitcast.133, f32[2,3,64,2048]{3,2,1,0:T(8,128)S(1)} %bitcast.134, ...), custom_call_target="tpu_custom_call" | custom-call | flops 12000 | bytes 1024 | tf_op jit(solution)/shard_map/attn_fwd/pallas_call | solution.py:65
  83.5 1.9 collective-permute-done.13
  87.2 2.9 collective-permute-start.17
  90.2 6.7 %collective-permute-done.16.refs_2_ = bf16[4,32,768]{2,1,0:T(8,128)(2,1)S(1)} collective-permute-done((bf16[4,32,768]{2,1,0:T(8,128)(2,1)S(1)}, bf16[4,32,768]{2,1,0:T(8,128)(2,1)S(1)}, u32[]{:S(2)}, u32[]{:S(2)}) %collective-permute-start.16) | collective-permute-done | bytes 196640 | tf_op jit(solution)/shard_map/ppermute | solution.py:496
  96.9 2.7 collective-permute-done.17.refs_4_
  99.8 1.8 collective-permute-start.22
  101.6 2.0 collective-permute-start.19
  103.7 5.7 %collective-permute-done.21.refs_2_ = bf16[4,32,768]{2,1,0:T(8,128)(2,1)S(1)} collective-permute-done((bf16[4,32,768]{2,1,0:T(8,128)(2,1)S(1)}, bf16[4,32,768]{2,1,0:T(8,128)(2,1)S(1)}, u32[]{:S(2)}, u32[]{:S(2)}) %collective-permute-start.21) | collective-permute-done | bytes 196640 | tf_op jit(solution)/shard_map/ppermute | solution.py:496
  110.6 1.5 collective-permute-start.18
  112.7 1.3 pad_maximum_fusion.3.cot_ref.refs_2_
  114.0 8.7 %collective-permute-done.18.ga = bf16[2,4,32,768]{3,2,1,0:T(8,128)(2,1)S(1)} collective-permute-done((bf16[2,4,32,768]{3,2,1,0:T(8,128)(2,1)S(1)}, bf16[2,4,32,768]{3,2,1,0:T(8,128)(2,1)S(1)}, u32[]{:S(2)}, u32[]{:S(2)}) %collective-permute-start.18) | collective-permute-done | bytes 393248 | tf_op jit(solution)/shard_map/ppermute | solution.py:496
  122.7 3.5 collective-permute-done.19.gb
  126.4 1.4 copy-done.3
  128.9 12.2 %collective-permute-done.24.refs_4_ = bf16[4,2,64,768]{3,2,1,0:T(8,128)(2,1)S(1)} collective-permute-done((bf16[4,2,64,768]{3,2,1,0:T(8,128)(2,1)S(1)}, bf16[4,2,64,768]{3,2,1,0:T(8,128)(2,1)S(1)}, u32[]{:S(2)}, u32[]{:S(2)}) %collective-permute-start.24) | collective-permute-done | bytes 786464 | tf_op jit(solution)/shard_map/ppermute | solution.py:496
  141.3 1.4 copy-done.5
  142.7 20.7 %mlp_fwd.1 = (bf16[2,1024,768]{2,1,0:T(8,128)(2,1)}, bf16[2,4,96,768]{3,2,1,0:T(8,128)(2,1)S(1)}, bf16[2,4,96,768]{3,2,1,0:T(8,128)(2,1)S(1)}, f32[512,768]{1,0:T(8,128)S(1)}, bf16[512,768]{1,0:T(8,128)(2,1)S(1)}) custom-call(s32[1]{0:T(128)} %bitcast.5.refs_0_.bit_ref, bf16[1024,768]{1,0:T(8,128)(2,1)} %copy-done.4, ...), custom_call_target="tpu_custom_call" | custom-call | flops 12000 | bytes 1024 | tf_op jit(solution)/shard_map/mlp_fwd/pallas_call | solution.py:398
  163.4 16.7 %mlp_bwd.1 = (bf16[2,4,96,768]{3,2,1,0:T(8,128)(2,1)S(1)}, bf16[2,4,96,768]{3,2,1,0:T(8,128)(2,1)}, f32[512,768]{1,0:T(8,128)S(1)}, bf16[512,768]{1,0:T(8,128)(2,1)S(1)}) custom-call(s32[1]{0:T(128)} %bitcast.5.refs_0_.bit_ref, bf16[1024,768]{1,0:T(8,128)(2,1)} %copy-done.4, bf16[1024,768]{1,0:T(8,128)(2,1)} %pad_maximum_fusion.3.cot_ref.refs_2_, ...), custom_call_target="tpu_custom_call" | custom-call | flops 12000 | bytes 1024 | tf_op jit(solution)/shard_map/mlp_bwd/pallas_call | solution.py:398
  183.5 2.2 fusion.64
  186.4 1.5 collective-permute-done.27
  188.1 21.3 %collective-permute-done.28.refs_2_ = bf16[2,4,96,768]{3,2,1,0:T(8,128)(2,1)S(1)} collective-permute-done((bf16[2,4,96,768]{3,2,1,0:T(8,128)(2,1)S(1)}, bf16[2,4,96,768]{3,2,1,0:T(8,128)(2,1)S(1)}, u32[]{:S(2)}, u32[]{:S(2)}) %collective-permute-start.28) | collective-permute-done | bytes 1179680 | tf_op jit(solution)/shard_map/ppermute | solution.py:496
  211.5 1.9 pad_maximum_fusion.refs_3_
  215.3 19.3 %attn_bwd.2 = (bf16[3,64,1024]{2,1,0:T(8,128)(2,1)S(1)}, bf16[2,3,64,2048]{3,2,1,0:T(8,128)(2,1)S(1)}, f32[64,1]{1,0:T(8,128)S(1)}, f32[64,1]{1,0:T(8,128)S(1)}) custom-call(s32[2]{0:T(128)S(1)} %convert_reduce_fusion.5.refs_0_, s32[16]{0:T(128)S(1)} %copy-done.16, f32[3,64,1024]{2,1,0:T(8,128)S(1)} %bitcast.179, f32[2,3,64,2048]{3,2,1,0:T(8,128)} %bitcast.135, ...), custom_call_target="tpu_custom_call" | custom-call | flops 20000 | bytes 1024 | tf_op jit(solution)/shard_map/attn_bwd/pallas_call | solution.py:152
  236.0 9.9 %proj_grad.2 = (bf16[4,96,960]{2,1,0:T(8,128)(2,1)S(1)}, bf16[4,96,960]{2,1,0:T(8,128)(2,1)S(1)}, bf16[4,512,768]{2,1,0:T(8,128)(2,1)}) custom-call(s32[1]{0:T(128)} %bitcast.5.refs_0_.bit_ref, bf16[384,2048]{1,0:T(8,128)(2,1)S(1)} %bitcast.187, bf16[192,1024]{1,0:T(8,128)(2,1)S(1)} %bitcast.171, bf16[2048,768]{1,0:T(8,128)(2,1)} %pad_maximum_fusion.refs_3_, ...), custom_call_target="tpu_custom_call" | custom-call | flops 5000 | bytes 1024 | tf_op jit(solution)/shard_map/proj_grad/pallas_call | solution.py:475
  246.0 1.6 collective-permute-start.33
  247.6 6.8 %collective-permute-done.31.refs_2_ = bf16[2,96,768]{2,1,0:T(8,128)(2,1)S(1)} collective-permute-done((bf16[2,96,768]{2,1,0:T(8,128)(2,1)S(1)}, bf16[2,96,768]{2,1,0:T(8,128)(2,1)S(1)}, u32[]{:S(2)}, u32[]{:S(2)}) %collective-permute-start.31) | collective-permute-done | bytes 294944 | tf_op jit(solution)/shard_map/ppermute | solution.py:496
  254.4 1.9 copy-done.7
  256.4 19.4 %attn_bwd.3 = (bf16[3,64,1024]{2,1,0:T(8,128)(2,1)S(1)}, bf16[2,3,64,2048]{3,2,1,0:T(8,128)(2,1)S(1)}, f32[64,1]{1,0:T(8,128)S(1)}, f32[64,1]{1,0:T(8,128)S(1)}) custom-call(s32[2]{0:T(128)S(1)} %convert_reduce_fusion.5.refs_0_, s32[16]{0:T(128)S(1)} %copy-done.16, f32[3,64,1024]{2,1,0:T(8,128)S(1)} %bitcast.181, f32[2,3,64,2048]{3,2,1,0:T(8,128)} %bitcast.131, ...), custom_call_target="tpu_custom_call" | custom-call | flops 20000 | bytes 1024 | tf_op jit(solution)/shard_map/attn_bwd/pallas_call | solution.py:152
  276.1 8.7 %proj_grad.3 = (bf16[4,96,576]{2,1,0:T(8,128)(2,1)S(1)}, bf16[4,96,576]{2,1,0:T(8,128)(2,1)S(1)}, bf16[4,512,768]{2,1,0:T(8,128)(2,1)}) custom-call(s32[1]{0:T(128)} %bitcast.5.refs_0_.bit_ref, bf16[384,2048]{1,0:T(8,128)(2,1)S(1)} %bitcast.186, bf16[192,1024]{1,0:T(8,128)(2,1)S(1)} %bitcast.168, bf16[2048,768]{1,0:T(8,128)(2,1)} %pad_maximum_fusion.refs_3_, ...), custom_call_target="tpu_custom_call" | custom-call | flops 5000 | bytes 1024 | tf_op jit(solution)/shard_map/proj_grad/pallas_call | solution.py:475
  284.8 1.6 slice_bitcast_fusion.1
  286.8 2.1 collective-permute-start.45
  288.9 1.4 collective-permute-start.42
  290.5 4.1 %collective-permute-done.50 = bf16[1,96,768]{2,1,0:T(8,128)(2,1)S(1)} collective-permute-done((bf16[1,96,768]{2,1,0:T(8,128)(2,1)S(1)}, bf16[1,96,768]{2,1,0:T(8,128)(2,1)S(1)}, u32[]{:S(2)}, u32[]{:S(2)}) %collective-permute-start.50) | collective-permute-done | bytes 147488 | tf_op jit(solution)/shard_map/ppermute | solution.py:496
  295.3 4.3 %collective-permute-done.48.refs_2_ = bf16[2,96,768]{2,1,0:T(8,128)(2,1)S(1)} collective-permute-done((bf16[2,96,768]{2,1,0:T(8,128)(2,1)S(1)}, bf16[2,96,768]{2,1,0:T(8,128)(2,1)S(1)}, u32[]{:S(2)}, u32[]{:S(2)}) %collective-permute-start.48) | collective-permute-done | bytes 294944 | tf_op jit(solution)/shard_map/ppermute | solution.py:496
  299.9 10.9 %collective-permute-done.45.refs_2_ = bf16[2,96,960]{2,1,0:T(8,128)(2,1)S(1)} collective-permute-done((bf16[2,96,960]{2,1,0:T(8,128)(2,1)S(1)}, bf16[2,96,960]{2,1,0:T(8,128)(2,1)S(1)}, u32[]{:S(2)}, u32[]{:S(2)}) %collective-permute-start.45) | collective-permute-done | bytes 368672 | tf_op jit(solution)/shard_map/ppermute | solution.py:496
  311.4 1.3 collective-permute-start.36
  313.4 9.5 %collective-permute-done.43.got_ref = bf16[2,96,576]{2,1,0:T(8,128)(2,1)S(1)} collective-permute-done((bf16[2,96,576]{2,1,0:T(8,128)(2,1)S(1)}, bf16[2,96,576]{2,1,0:T(8,128)(2,1)S(1)}, u32[]{:S(2)}, u32[]{:S(2)}) %collective-permute-start.43) | collective-permute-done | bytes 221216 | tf_op jit(solution)/shard_map/ppermute | solution.py:496
  324.3 5.3 %collective-permute-done.44 = bf16[1,96,576]{2,1,0:T(8,128)(2,1)S(1)} collective-permute-done((bf16[1,96,576]{2,1,0:T(8,128)(2,1)S(1)}, bf16[1,96,576]{2,1,0:T(8,128)(2,1)S(1)}, u32[]{:S(2)}, u32[]{:S(2)}) %collective-permute-start.44) | collective-permute-done | bytes 110624 | tf_op jit(solution)/shard_map/ppermute | solution.py:496
  329.7 4.0 %collective-permute-done.47 = bf16[96,768]{1,0:T(8,128)(2,1)S(1)} collective-permute-done((bf16[96,768]{1,0:T(8,128)(2,1)S(1)}, bf16[96,768]{1,0:T(8,128)(2,1)S(1)}, u32[]{:S(2)}, u32[]{:S(2)}) %collective-permute-start.47) | collective-permute-done | bytes 147488 | tf_op jit(solution)/shard_map/ppermute | solution.py:496
  333.8 3.5 fusion.41
  338.2 1.3 collective-permute-done.37
  342.6 1.5 collective-permute-done.38
  344.1 1.4 collective-permute-start.39
  346.2 1.7 collective-permute-done.39
  347.9 1.7 collective-permute-start.40
  349.6 2.1 collective-permute-done.40
  351.7 2.6 collective-permute-start.41
  354.3 3.7 %fusion.46 = bf16[1,512,768]{2,1,0:T(8,128)(2,1)} fusion(f32[512,768]{1,0:T(8,128)} %get-tuple-element.189, f32[512]{0:T(512)S(1)} %broadcast_multiply_fusion, f32[512]{0:T(512)S(1)} %broadcast_multiply_fusion.1, f32[512]{0:T(512)S(1)} %add_rsqrt_fusion.4, f32[512]{0:T(512)S(1)} %broadcast_multiply_fusion.8, f32[768]{0:T(1024)S(1)} %copy-done.37, ...), kind=kLoop, calls=%fused_computation.73 | loop fusion | flops 5898240 | bytes 5516288 | tf_op jit(solution)/shard_map/broadcast_in_dim | solution.py:706
  (266 shorter events, 41.9 us)
Async XLA Ops:
  1.7 11.4 %collective-permute-start = (bf16[1,96,576]{2,1,0:T(8,128)(2,1)S(1)}, bf16[1,96,576]{2,1,0:T(8,128)(2,1)S(1)}, u32[]{:S(2)}, u32[]{:S(2)}) collective-permute-start(bf16[1,96,576]{2,1,0:T(8,128)(2,1)S(1)} %maximum_bitcast_fusion.1.refs_1_), channel_id=1, source_target_pairs={{0,16},{4,20},{8,24},{12,28},{16,0},{20,4},{24,8},{28,12},{1,17},{... | collective-permute-start | bytes 331784 | tf_op jit(solution)/shard_map/ppermute | solution.py:496
  6.8 5.6 %collective-permute-start.1 = (bf16[96,768]{1,0:T(8,128)(2,1)S(1)}, bf16[96,768]{1,0:T(8,128)(2,1)S(1)}, u32[]{:S(2)}, u32[]{:S(2)}) collective-permute-start(bf16[96,768]{1,0:T(8,128)(2,1)S(1)} %pad_maximum_fusion.11), channel_id=1, source_target_pairs={{0,2},{1,3},{2,0},{3,1},{4,6},{5,7},{6,4},{7,5},{8,10},{9,11},{10,... | collective-permute-start | bytes 442376 | tf_op jit(solution)/shard_map/ppermute | solution.py:496
  8.4 34.2 %collective-permute-start.7 = (bf16[512,768]{1,0:T(8,128)(2,1)}, bf16[512,768]{1,0:T(8,128)(2,1)}, u32[]{:S(2)}, u32[]{:S(2)}) collective-permute-start(bf16[512,768]{1,0:T(8,128)(2,1)} %bitcast.198), channel_id=1, source_target_pairs={{0,1},{1,0},{2,3},{3,2},{4,5},{5,4},{6,7},{7,6},{8,9},{9,8},{10,11... | collective-permute-start | bytes 2359304 | tf_op jit(solution)/shard_map/ppermute | solution.py:496
  10.4 15.9 %copy-start.34 = (bf16[96,768]{1,0:T(8,128)(2,1)S(1)}, bf16[96,768]{1,0:T(8,128)(2,1)}, u32[]{:S(2)}) copy-start(bf16[96,768]{1,0:T(8,128)(2,1)} %param.23) | copy-start | bytes 442372
  12.4 12.6 %collective-permute-start.3 = (bf16[1,96,960]{2,1,0:T(8,128)(2,1)S(1)}, bf16[1,96,960]{2,1,0:T(8,128)(2,1)S(1)}, u32[]{:S(2)}, u32[]{:S(2)}) collective-permute-start(bf16[1,96,960]{2,1,0:T(8,128)(2,1)S(1)} %maximum_bitcast_fusion.refs_3_.refs_1_), channel_id=1, source_target_pairs={{0,16},{4,20},{8,24},{12,28},{16,0},{20,4},{24,8},{28,12},{1,17},{... | collective-permute-start | bytes 552968 | tf_op jit(solution)/shard_map/ppermute | solution.py:496
  13.2 16.5 %copy-start.41 = (f32[64]{0:T(128)S(1)}, f32[64]{0:T(128)}, u32[]{:S(2)}) copy-start(f32[64]{0:T(128)} %param.18) | copy-start | bytes 772
  13.2 16.6 %copy-start.42 = (f32[64]{0:T(128)S(1)}, f32[64]{0:T(128)}, u32[]{:S(2)}) copy-start(f32[64]{0:T(128)} %param.19) | copy-start | bytes 772
  13.2 16.8 %collective-permute-start.2 = (bf16[2,96,576]{2,1,0:T(8,128)(2,1)S(1)}, bf16[2,96,576]{2,1,0:T(8,128)(2,1)S(1)}, u32[]{:S(2)}, u32[]{:S(2)}) collective-permute-start(bf16[2,96,576]{2,1,0:T(8,128)(2,1)S(1)} %bitcast.182), channel_id=1, source_target_pairs={{0,8},{4,12},{8,0},{12,4},{16,24},{20,28},{24,16},{28,20},{1,9},{5... | collective-permute-start | bytes 663560 | tf_op jit(solution)/shard_map/ppermute | solution.py:496
  25.6 13.8 %collective-permute-start.6 = (bf16[2,96,960]{2,1,0:T(8,128)(2,1)S(1)}, bf16[2,96,960]{2,1,0:T(8,128)(2,1)S(1)}, u32[]{:S(2)}, u32[]{:S(2)}) collective-permute-start(bf16[2,96,960]{2,1,0:T(8,128)(2,1)S(1)} %bitcast.175), channel_id=1, source_target_pairs={{0,8},{4,12},{8,0},{12,4},{16,24},{20,28},{24,16},{28,20},{1,9},{5... | collective-permute-start | bytes 1105928 | tf_op jit(solution)/shard_map/ppermute | solution.py:496
  26.3 13.2 %collective-permute-start.5 = (bf16[1,96,768]{2,1,0:T(8,128)(2,1)S(1)}, bf16[1,96,768]{2,1,0:T(8,128)(2,1)S(1)}, u32[]{:S(2)}, u32[]{:S(2)}) collective-permute-start(bf16[1,96,768]{2,1,0:T(8,128)(2,1)S(1)} %add_bitcast_fusion.5.refs_1_), channel_id=1, source_target_pairs={{0,16},{4,20},{8,24},{12,28},{16,0},{20,4},{24,8},{28,12},{1,17},{... | collective-permute-start | bytes 442376 | tf_op jit(solution)/shard_map/ppermute | solution.py:496
  29.0 19.2 %collective-permute-start.8 = (bf16[512,768]{1,0:T(8,128)(2,1)}, bf16[512,768]{1,0:T(8,128)(2,1)}, u32[]{:S(2)}, u32[]{:S(2)}) collective-permute-start(bf16[512,768]{1,0:T(8,128)(2,1)} %broadcast_add_fusion), channel_id=1, source_target_pairs={{0,2},{1,3},{2,0},{3,1},{4,6},{5,7},{6,4},{7,5},{8,10},{9,11},{10,... | collective-permute-start | bytes 2359304 | tf_op jit(solution)/shard_map/ppermute | solution.py:496
  29.8 41.4 %copy-start.11 = (f32[64,1]{1,0:T(8,128)}, f32[64,1]{1,0:T(8,128)S(1)}, u32[]{:S(2)}) copy-start(f32[64,1]{1,0:T(8,128)S(1)} %copy.64.refs_7_.refs_10_) | copy-start | bytes 772
  29.9 41.3 %copy-start.13 = (f32[64,1]{1,0:T(8,128)}, f32[64,1]{1,0:T(8,128)S(1)}, u32[]{:S(2)}) copy-start(f32[64,1]{1,0:T(8,128)S(1)} %copy.65.refs_8_.refs_11_) | copy-start | bytes 772
  29.9 41.2 %copy-start.15 = (s32[16]{0:T(128)}, s32[16]{0:T(128)S(1)}, u32[]{:S(2)}) copy-start(s32[16]{0:T(128)S(1)} %reshape.336.refs_1_) | copy-start | bytes 196
  30.0 12.5 %copy-start.35 = (bf16[768,96]{0,1:T(8,128)(2,1)S(1)}, bf16[768,96]{0,1:T(8,128)(2,1)}, u32[]{:S(2)}) copy-start(bf16[768,96]{0,1:T(8,128)(2,1)} %param.24) | copy-start | bytes 442372
  30.0 18.3 %collective-permute-start.4 = (bf16[4,96,576]{2,1,0:T(8,128)(2,1)S(1)}, bf16[4,96,576]{2,1,0:T(8,128)(2,1)S(1)}, u32[]{:S(2)}, u32[]{:S(2)}) collective-permute-start(bf16[4,96,576]{2,1,0:T(8,128)(2,1)S(1)} %bitcast.158), channel_id=1, source_target_pairs={{0,4},{4,0},{8,12},{12,8},{16,20},{20,16},{24,28},{28,24},{1,5},{5... | collective-permute-start | bytes 1327112 | tf_op jit(solution)/shard_map/ppermute | solution.py:496
  40.1 28.4 %collective-permute-start.12 = (bf16[2,96,768]{2,1,0:T(8,128)(2,1)S(1)}, bf16[2,96,768]{2,1,0:T(8,128)(2,1)S(1)}, u32[]{:S(2)}, u32[]{:S(2)}) collective-permute-start(bf16[2,96,768]{2,1,0:T(8,128)(2,1)S(1)} %bitcast.150), channel_id=1, source_target_pairs={{0,8},{4,12},{8,0},{12,4},{16,24},{20,28},{24,16},{28,20},{1,9},{5... | collective-permute-start | bytes 884744 | tf_op jit(solution)/shard_map/ppermute | solution.py:496
  40.3 28.2 %collective-permute-start.10 = (bf16[4,96,960]{2,1,0:T(8,128)(2,1)S(1)}, bf16[4,96,960]{2,1,0:T(8,128)(2,1)S(1)}, u32[]{:S(2)}, u32[]{:S(2)}) collective-permute-start(bf16[4,96,960]{2,1,0:T(8,128)(2,1)S(1)} %bitcast.147), channel_id=1, source_target_pairs={{0,4},{4,0},{8,12},{12,8},{16,20},{20,16},{24,28},{28,24},{1,5},{5... | collective-permute-start | bytes 2211848 | tf_op jit(solution)/shard_map/ppermute | solution.py:496
  42.6 26.0 %collective-permute-start.11 = (bf16[1,96,768]{2,1,0:T(8,128)(2,1)S(1)}, bf16[1,96,768]{2,1,0:T(8,128)(2,1)S(1)}, u32[]{:S(2)}, u32[]{:S(2)}) collective-permute-start(bf16[1,96,768]{2,1,0:T(8,128)(2,1)S(1)} %add_bitcast_fusion.4.refs_1_), channel_id=1, source_target_pairs={{0,16},{4,20},{8,24},{12,28},{16,0},{20,4},{24,8},{28,12},{1,17},{... | collective-permute-start | bytes 442376 | tf_op jit(solution)/shard_map/ppermute | solution.py:496
  48.3 3.0 collective-permute-start.9
  54.3 15.1 %copy-start.19 = (bf16[512,768]{1,0:T(8,128)(2,1)}, bf16[512,768]{1,0:T(8,128)(2,1)S(1)}, u32[]{:S(2)}) copy-start(bf16[512,768]{1,0:T(8,128)(2,1)S(1)} %get-tuple-element.209) | copy-start | bytes 2359300
  54.3 15.1 %copy-start.21 = (bf16[512,768]{1,0:T(8,128)(2,1)}, bf16[512,768]{1,0:T(8,128)(2,1)S(1)}, u32[]{:S(2)}) copy-start(bf16[512,768]{1,0:T(8,128)(2,1)S(1)} %get-tuple-element.210) | copy-start | bytes 2359300
  54.4 15.1 %copy-start.23 = (bf16[512,768]{1,0:T(8,128)(2,1)}, bf16[512,768]{1,0:T(8,128)(2,1)S(1)}, u32[]{:S(2)}) copy-start(bf16[512,768]{1,0:T(8,128)(2,1)S(1)} %get-tuple-element.211) | copy-start | bytes 2359300
  82.9 2.5 collective-permute-start.13
  86.8 14.8 %copy-start.27 = (bf16[1,512,768]{2,1,0:T(8,128)(2,1)S(1)}, bf16[1,512,768]{2,1,0:T(8,128)(2,1)}, u32[]{:S(2)}) copy-start(bf16[1,512,768]{2,1,0:T(8,128)(2,1)} %param.25) | copy-start | bytes 2359300
  86.8 16.8 %collective-permute-start.14 = (bf16[512,768]{1,0:T(8,128)(2,1)S(1)}, bf16[512,768]{1,0:T(8,128)(2,1)S(1)}, u32[]{:S(2)}, u32[]{:S(2)}) collective-permute-start(bf16[512,768]{1,0:T(8,128)(2,1)S(1)} %add_convert_fusion.1), channel_id=1, source_target_pairs={{0,1},{1,0},{2,3},{3,2},{4,5},{5,4},{6,7},{7,6},{8,9},{9,8},{10,11... | collective-permute-start | bytes 2359304 | tf_op jit(solution)/shard_map/ppermute | solution.py:496
  87.2 12.4 %collective-permute-start.17 = (bf16[4,64,768]{2,1,0:T(8,128)(2,1)S(1)}, bf16[4,64,768]{2,1,0:T(8,128)(2,1)S(1)}, u32[]{:S(2)}, u32[]{:S(2)}) collective-permute-start(bf16[4,64,768]{2,1,0:T(8,128)(2,1)S(1)} %bitcast.192), channel_id=1, source_target_pairs={{0,4},{4,0},{8,12},{12,8},{16,20},{20,16},{24,28},{28,24},{1,5},{5... | collective-permute-start | bytes 1179656 | tf_op jit(solution)/shard_map/ppermute | solution.py:496
  90.2 9.5 %collective-permute-start.20 = (bf16[2,96,768]{2,1,0:T(8,128)(2,1)S(1)}, bf16[2,96,768]{2,1,0:T(8,128)(2,1)S(1)}, u32[]{:S(2)}, u32[]{:S(2)}) collective-permute-start(bf16[2,96,768]{2,1,0:T(8,128)(2,1)S(1)} %bitcast.156), channel_id=1, source_target_pairs={{0,8},{4,12},{8,0},{12,4},{16,24},{20,28},{24,16},{28,20},{1,9},{5... | collective-permute-start | bytes 884744 | tf_op jit(solution)/shard_map/ppermute | solution.py:496
  90.2 6.7 %collective-permute-start.16 = (bf16[4,32,768]{2,1,0:T(8,128)(2,1)S(1)}, bf16[4,32,768]{2,1,0:T(8,128)(2,1)S(1)}, u32[]{:S(2)}, u32[]{:S(2)}) collective-permute-start(bf16[4,32,768]{2,1,0:T(8,128)(2,1)S(1)} %bitcast.190), channel_id=1, source_target_pairs={{0,2},{1,3},{2,0},{3,1},{4,6},{5,7},{6,4},{7,5},{8,10},{9,11},{10,... | collective-permute-start | bytes 589832 | tf_op jit(solution)/shard_map/ppermute | solution.py:496
  99.8 10.7 %collective-permute-start.22 = (bf16[4,64,768]{2,1,0:T(8,128)(2,1)S(1)}, bf16[4,64,768]{2,1,0:T(8,128)(2,1)S(1)}, u32[]{:S(2)}, u32[]{:S(2)}) collective-permute-start(bf16[4,64,768]{2,1,0:T(8,128)(2,1)S(1)} %bitcast.194), channel_id=1, source_target_pairs={{0,4},{4,0},{8,12},{12,8},{16,20},{20,16},{24,28},{28,24},{1,5},{5... | collective-permute-start | bytes 1179656 | tf_op jit(solution)/shard_map/ppermute | solution.py:496
  101.6 7.8 %collective-permute-start.21 = (bf16[4,32,768]{2,1,0:T(8,128)(2,1)S(1)}, bf16[4,32,768]{2,1,0:T(8,128)(2,1)S(1)}, u32[]{:S(2)}, u32[]{:S(2)}) collective-permute-start(bf16[4,32,768]{2,1,0:T(8,128)(2,1)S(1)} %bitcast.196), channel_id=1, source_target_pairs={{0,2},{1,3},{2,0},{3,1},{4,6},{5,7},{6,4},{7,5},{8,10},{9,11},{10,... | collective-permute-start | bytes 589832 | tf_op jit(solution)/shard_map/ppermute | solution.py:496
  101.6 11.2 %collective-permute-start.15 = (bf16[512,768]{1,0:T(8,128)(2,1)S(1)}, bf16[512,768]{1,0:T(8,128)(2,1)S(1)}, u32[]{:S(2)}, u32[]{:S(2)}) collective-permute-start(bf16[512,768]{1,0:T(8,128)(2,1)S(1)} %bitcast.199), channel_id=1, source_target_pairs={{0,1},{1,0},{2,3},{3,2},{4,5},{5,4},{6,7},{7,6},{8,9},{9,8},{10,11... | collective-permute-start | bytes 2359304 | tf_op jit(solution)/shard_map/ppermute | solution.py:496
  101.6 24.7 %collective-permute-start.19 = (bf16[4,2,64,768]{3,2,1,0:T(8,128)(2,1)S(1)}, bf16[4,2,64,768]{3,2,1,0:T(8,128)(2,1)S(1)}, u32[]{:S(2)}, u32[]{:S(2)}) collective-permute-start(bf16[4,2,64,768]{3,2,1,0:T(8,128)(2,1)S(1)} %get-tuple-element.72.b.refs_3_), channel_id=1, source_target_pairs={{0,2},{1,3},{2,0},{3,1},{4,6},{5,7},{6,4},{7,5},{8,10},{9,11},{10,... | collective-permute-start | bytes 2359304 | tf_op jit(solution)/shard_map/ppermute | solution.py:496
  110.5 30.6 %collective-permute-start.24 = (bf16[4,2,64,768]{3,2,1,0:T(8,128)(2,1)S(1)}, bf16[4,2,64,768]{3,2,1,0:T(8,128)(2,1)S(1)}, u32[]{:S(2)}, u32[]{:S(2)}) collective-permute-start(bf16[4,2,64,768]{3,2,1,0:T(8,128)(2,1)S(1)} %get-tuple-element.76.refs_3_), channel_id=1, source_target_pairs={{0,2},{1,3},{2,0},{3,1},{4,6},{5,7},{6,4},{7,5},{8,10},{9,11},{10,... | collective-permute-start | bytes 2359304 | tf_op jit(solution)/shard_map/ppermute | solution.py:496
  110.6 12.1 %collective-permute-start.18 = (bf16[2,4,32,768]{3,2,1,0:T(8,128)(2,1)S(1)}, bf16[2,4,32,768]{3,2,1,0:T(8,128)(2,1)S(1)}, u32[]{:S(2)}, u32[]{:S(2)}) collective-permute-start(bf16[2,4,32,768]{3,2,1,0:T(8,128)(2,1)S(1)} %get-tuple-element.71.a), channel_id=1, source_target_pairs={{0,4},{4,0},{8,12},{12,8},{16,20},{20,16},{24,28},{28,24},{1,5},{5... | collective-permute-start | bytes 1179656 | tf_op jit(solution)/shard_map/ppermute | solution.py:496
  112.1 16.7 %collective-permute-start.23 = (bf16[2,4,32,768]{3,2,1,0:T(8,128)(2,1)S(1)}, bf16[2,4,32,768]{3,2,1,0:T(8,128)(2,1)S(1)}, u32[]{:S(2)}, u32[]{:S(2)}) collective-permute-start(bf16[2,4,32,768]{3,2,1,0:T(8,128)(2,1)S(1)} %get-tuple-element.75.refs_1_), channel_id=1, source_target_pairs={{0,4},{4,0},{8,12},{12,8},{16,20},{20,16},{24,28},{28,24},{1,5},{5... | collective-permute-start | bytes 1179656 | tf_op jit(solution)/shard_map/ppermute | solution.py:496
  180.1 2.3 collective-permute-start.26
  180.1 3.4 collective-permute-start.25
  180.6 28.8 %collective-permute-start.28 = (bf16[2,4,96,768]{3,2,1,0:T(8,128)(2,1)S(1)}, bf16[2,4,96,768]{3,2,1,0:T(8,128)(2,1)S(1)}, u32[]{:S(2)}, u32[]{:S(2)}) collective-permute-start(bf16[2,4,96,768]{3,2,1,0:T(8,128)(2,1)S(1)} %get-tuple-element.80.refs_6_), channel_id=1, source_target_pairs={{0,4},{4,0},{8,12},{12,8},{16,20},{20,16},{24,28},{28,24},{1,5},{5... | collective-permute-start | bytes 3538952 | tf_op jit(solution)/shard_map/ppermute | solution.py:496
  185.7 2.3 collective-permute-start.27
  185.8 48.8 %collective-permute-start.29 = (bf16[2,4,96,768]{3,2,1,0:T(8,128)(2,1)}, bf16[2,4,96,768]{3,2,1,0:T(8,128)(2,1)S(1)}, u32[]{:S(2)}, u32[]{:S(2)}) collective-permute-start(bf16[2,4,96,768]{3,2,1,0:T(8,128)(2,1)} %get-tuple-element.85.refs_12_), channel_id=1, source_target_pairs={{0,4},{4,0},{8,12},{12,8},{16,20},{20,16},{24,28},{28,24},{1,5},{5... | collective-permute-start | bytes 3538952 | tf_op jit(solution)/shard_map/ppermute | solution.py:496
  188.1 21.6 %copy-start.6 = (bf16[1024,768]{1,0:T(8,128)(2,1)}, bf16[1024,768]{1,0:T(8,128)(2,1)S(1)}, u32[]{:S(2)}) copy-start(bf16[1024,768]{1,0:T(8,128)(2,1)S(1)} %pad_maximum_fusion.4.refs_3_.refs_7_) | copy-start | bytes 4718596
  209.7 25.2 %collective-permute-start.30 = (bf16[4,96,768]{2,1,0:T(8,128)(2,1)S(1)}, bf16[4,96,768]{2,1,0:T(8,128)(2,1)S(1)}, u32[]{:S(2)}, u32[]{:S(2)}) collective-permute-start(bf16[4,96,768]{2,1,0:T(8,128)(2,1)S(1)} %get-tuple-element.87.refs_13_), channel_id=1, source_target_pairs={{0,2},{1,3},{2,0},{3,1},{4,6},{5,7},{6,4},{7,5},{8,10},{9,11},{10,... | collective-permute-start | bytes 1769480 | tf_op jit(solution)/shard_map/ppermute | solution.py:496
  246.0 30.0 %collective-permute-start.33 = (bf16[4,96,960]{2,1,0:T(8,128)(2,1)S(1)}, bf16[4,96,960]{2,1,0:T(8,128)(2,1)S(1)}, u32[]{:S(2)}, u32[]{:S(2)}) collective-permute-start(bf16[4,96,960]{2,1,0:T(8,128)(2,1)S(1)} %get-tuple-element.94.refs_12_), channel_id=1, source_target_pairs={{0,4},{4,0},{8,12},{12,8},{16,20},{20,16},{24,28},{28,24},{1,5},{5... | collective-permute-start | bytes 2211848 | tf_op jit(solution)/shard_map/ppermute | solution.py:496
  247.6 28.2 %collective-permute-start.32 = (bf16[4,96,768]{2,1,0:T(8,128)(2,1)S(1)}, bf16[4,96,768]{2,1,0:T(8,128)(2,1)S(1)}, u32[]{:S(2)}, u32[]{:S(2)}) collective-permute-start(bf16[4,96,768]{2,1,0:T(8,128)(2,1)S(1)} %get-tuple-element.91.refs_8_), channel_id=1, source_target_pairs={{0,2},{1,3},{2,0},{3,1},{4,6},{5,7},{6,4},{7,5},{8,10},{9,11},{10,... | collective-permute-start | bytes 1769480 | tf_op jit(solution)/shard_map/ppermute | solution.py:496
  247.6 6.8 %collective-permute-start.31 = (bf16[2,96,768]{2,1,0:T(8,128)(2,1)S(1)}, bf16[2,96,768]{2,1,0:T(8,128)(2,1)S(1)}, u32[]{:S(2)}, u32[]{:S(2)}) collective-permute-start(bf16[2,96,768]{2,1,0:T(8,128)(2,1)S(1)} %get-tuple-element.93.refs_9_), channel_id=1, source_target_pairs={{0,8},{4,12},{8,0},{12,4},{16,24},{20,28},{24,16},{28,20},{1,9},{5... | collective-permute-start | bytes 884744 | tf_op jit(solution)/shard_map/ppermute | solution.py:496
  284.8 14.9 %copy-start.2 = (bf16[4,512,768]{2,1,0:T(8,128)(2,1)S(1)}, bf16[4,512,768]{2,1,0:T(8,128)(2,1)}, u32[]{:S(2)}) copy-start(bf16[4,512,768]{2,1,0:T(8,128)(2,1)} %get-tuple-element.104.refs_3_) | copy-start | bytes 9437188
  286.4 24.7 %collective-permute-start.35 = (bf16[512,768]{1,0:T(8,128)(2,1)S(1)}, bf16[512,768]{1,0:T(8,128)(2,1)S(1)}, u32[]{:S(2)}, u32[]{:S(2)}) collective-permute-start(bf16[512,768]{1,0:T(8,128)(2,1)S(1)} %get-tuple-element.193), channel_id=1, source_target_pairs={{0,1},{1,0},{2,3},{3,2},{4,5},{5,4},{6,7},{7,6},{8,9},{9,8},{10,11... | collective-permute-start | bytes 2359304 | tf_op jit(solution)/shard_map/ppermute | solution.py:496
  286.5 8.0 %collective-permute-start.50 = (bf16[1,96,768]{2,1,0:T(8,128)(2,1)S(1)}, bf16[1,96,768]{2,1,0:T(8,128)(2,1)S(1)}, u32[]{:S(2)}, u32[]{:S(2)}) collective-permute-start(bf16[1,96,768]{2,1,0:T(8,128)(2,1)S(1)} %get-tuple-element.97.refs_13_), channel_id=1, source_target_pairs={{0,16},{4,20},{8,24},{12,28},{16,0},{20,4},{24,8},{28,12},{1,17},{... | collective-permute-start | bytes 442376 | tf_op jit(solution)/shard_map/ppermute | solution.py:496
  286.6 13.0 %collective-permute-start.48 = (bf16[2,96,768]{2,1,0:T(8,128)(2,1)S(1)}, bf16[2,96,768]{2,1,0:T(8,128)(2,1)S(1)}, u32[]{:S(2)}, u32[]{:S(2)}) collective-permute-start(bf16[2,96,768]{2,1,0:T(8,128)(2,1)S(1)} %get-tuple-element.101.refs_6_), channel_id=1, source_target_pairs={{0,8},{4,12},{8,0},{12,4},{16,24},{20,28},{24,16},{28,20},{1,9},{5... | collective-permute-start | bytes 884744 | tf_op jit(solution)/shard_map/ppermute | solution.py:496
  286.8 24.0 %collective-permute-start.45 = (bf16[2,96,960]{2,1,0:T(8,128)(2,1)S(1)}, bf16[2,96,960]{2,1,0:T(8,128)(2,1)S(1)}, u32[]{:S(2)}, u32[]{:S(2)}) collective-permute-start(bf16[2,96,960]{2,1,0:T(8,128)(2,1)S(1)} %get-tuple-element.103.refs_7_), channel_id=1, source_target_pairs={{0,8},{4,12},{8,0},{12,4},{16,24},{20,28},{24,16},{28,20},{1,9},{5... | collective-permute-start | bytes 1105928 | tf_op jit(solution)/shard_map/ppermute | solution.py:496
  288.9 22.1 %collective-permute-start.42 = (bf16[4,96,576]{2,1,0:T(8,128)(2,1)S(1)}, bf16[4,96,576]{2,1,0:T(8,128)(2,1)S(1)}, u32[]{:S(2)}, u32[]{:S(2)}) collective-permute-start(bf16[4,96,576]{2,1,0:T(8,128)(2,1)S(1)} %get-tuple-element.110), channel_id=1, source_target_pairs={{0,4},{4,0},{8,12},{12,8},{16,20},{20,16},{24,28},{28,24},{1,5},{5... | collective-permute-start | bytes 1327112 | tf_op jit(solution)/shard_map/ppermute | solution.py:496
  299.7 12.9 %collective-permute-start.49 = (bf16[1,96,768]{2,1,0:T(8,128)(2,1)S(1)}, bf16[1,96,768]{2,1,0:T(8,128)(2,1)S(1)}, u32[]{:S(2)}, u32[]{:S(2)}) collective-permute-start(bf16[1,96,768]{2,1,0:T(8,128)(2,1)S(1)} %get-tuple-element.120), channel_id=1, source_target_pairs={{0,16},{4,20},{8,24},{12,28},{16,0},{20,4},{24,8},{28,12},{1,17},{... | collective-permute-start | bytes 442376 | tf_op jit(solution)/shard_map/ppermute | solution.py:496
  299.8 34.0 %collective-permute-start.34 = (bf16[512,768]{1,0:T(8,128)(2,1)S(1)}, bf16[512,768]{1,0:T(8,128)(2,1)S(1)}, u32[]{:S(2)}, u32[]{:S(2)}) collective-permute-start(bf16[512,768]{1,0:T(8,128)(2,1)S(1)} %get-tuple-element.192), channel_id=1, source_target_pairs={{0,1},{1,0},{2,3},{3,2},{4,5},{5,4},{6,7},{7,6},{8,9},{9,8},{10,11... | collective-permute-start | bytes 2359304 | tf_op jit(solution)/shard_map/ppermute | solution.py:496
  310.8 12.4 %collective-permute-start.46 = (bf16[1,96,960]{2,1,0:T(8,128)(2,1)S(1)}, bf16[1,96,960]{2,1,0:T(8,128)(2,1)S(1)}, u32[]{:S(2)}, u32[]{:S(2)}) collective-permute-start(bf16[1,96,960]{2,1,0:T(8,128)(2,1)S(1)} %get-tuple-element.117), channel_id=1, source_target_pairs={{0,16},{4,20},{8,24},{12,28},{16,0},{20,4},{24,8},{28,12},{1,17},{... | collective-permute-start | bytes 552968 | tf_op jit(solution)/shard_map/ppermute | solution.py:496
  311.1 11.8 %collective-permute-start.43 = (bf16[2,96,576]{2,1,0:T(8,128)(2,1)S(1)}, bf16[2,96,576]{2,1,0:T(8,128)(2,1)S(1)}, u32[]{:S(2)}, u32[]{:S(2)}) collective-permute-start(bf16[2,96,576]{2,1,0:T(8,128)(2,1)S(1)} %get-tuple-element.112), channel_id=1, source_target_pairs={{0,8},{4,12},{8,0},{12,4},{16,24},{20,28},{24,16},{28,20},{1,9},{5... | collective-permute-start | bytes 663560 | tf_op jit(solution)/shard_map/ppermute | solution.py:496
  311.4 22.4 %collective-permute-start.36 = (bf16[512,768]{1,0:T(8,128)(2,1)S(1)}, bf16[512,768]{1,0:T(8,128)(2,1)S(1)}, u32[]{:S(2)}, u32[]{:S(2)}) collective-permute-start(bf16[512,768]{1,0:T(8,128)(2,1)S(1)} %fusion.42), channel_id=1, source_target_pairs={{0,2},{1,3},{2,0},{3,1},{4,6},{5,7},{6,4},{7,5},{8,10},{9,11},{10,... | collective-permute-start | bytes 2359304 | tf_op jit(solution)/shard_map/ppermute | solution.py:496
  322.9 6.7 %collective-permute-start.44 = (bf16[1,96,576]{2,1,0:T(8,128)(2,1)S(1)}, bf16[1,96,576]{2,1,0:T(8,128)(2,1)S(1)}, u32[]{:S(2)}, u32[]{:S(2)}) collective-permute-start(bf16[1,96,576]{2,1,0:T(8,128)(2,1)S(1)} %get-tuple-element.114), channel_id=1, source_target_pairs={{0,16},{4,20},{8,24},{12,28},{16,0},{20,4},{24,8},{28,12},{1,17},{... | collective-permute-start | bytes 331784 | tf_op jit(solution)/shard_map/ppermute | solution.py:496
  323.3 10.4 %collective-permute-start.47 = (bf16[96,768]{1,0:T(8,128)(2,1)S(1)}, bf16[96,768]{1,0:T(8,128)(2,1)S(1)}, u32[]{:S(2)}, u32[]{:S(2)}) collective-permute-start(bf16[96,768]{1,0:T(8,128)(2,1)S(1)} %slice.217), channel_id=1, source_target_pairs={{0,2},{1,3},{2,0},{3,1},{4,6},{5,7},{6,4},{7,5},{8,10},{9,11},{10,... | collective-permute-start | bytes 442376 | tf_op jit(solution)/shard_map/ppermute | solution.py:496
  338.1 1.4 collective-permute-start.37
  340.2 3.8 %collective-permute-start.38 = (f32[5,768]{1,0:T(8,128)S(1)}, f32[5,768]{1,0:T(8,128)S(1)}, u32[]{:S(2)}, u32[]{:S(2)}) collective-permute-start(f32[5,768]{1,0:T(8,128)S(1)} %add.259), channel_id=1, source_target_pairs={{0,2},{1,3},{2,0},{3,1},{4,6},{5,7},{6,4},{7,5},{8,10},{9,11},{10,... | collective-permute-start | bytes 46088 | tf_op jit(solution)/shard_map/ppermute | solution.py:496
  344.1 3.8 %collective-permute-start.39 = (f32[5,768]{1,0:T(8,128)S(1)}, f32[5,768]{1,0:T(8,128)S(1)}, u32[]{:S(2)}, u32[]{:S(2)}) collective-permute-start(f32[5,768]{1,0:T(8,128)S(1)} %add.260), channel_id=1, source_target_pairs={{0,4},{4,0},{8,12},{12,8},{16,20},{20,16},{24,28},{28,24},{1,5},{5... | collective-permute-start | bytes 46088 | tf_op jit(solution)/shard_map/ppermute | solution.py:496
  347.9 3.8 %collective-permute-start.40 = (f32[5,768]{1,0:T(8,128)S(1)}, f32[5,768]{1,0:T(8,128)S(1)}, u32[]{:S(2)}, u32[]{:S(2)}) collective-permute-start(f32[5,768]{1,0:T(8,128)S(1)} %add.261), channel_id=1, source_target_pairs={{0,8},{4,12},{8,0},{12,4},{16,24},{20,28},{24,16},{28,20},{1,9},{5... | collective-permute-start | bytes 46088 | tf_op jit(solution)/shard_map/ppermute | solution.py:496
  351.7 6.3 %collective-permute-start.41 = (f32[5,768]{1,0:T(8,128)S(1)}, f32[5,768]{1,0:T(8,128)S(1)}, u32[]{:S(2)}, u32[]{:S(2)}) collective-permute-start(f32[5,768]{1,0:T(8,128)S(1)} %add.262), channel_id=1, source_target_pairs={{0,16},{4,20},{8,24},{12,28},{16,0},{20,4},{24,8},{28,12},{1,17},{... | collective-permute-start | bytes 46088 | tf_op jit(solution)/shard_map/ppermute | solution.py:496
  (30 other events, 119.2 us)
